TPU v7x, 32 devices: a whole 2x2x4 slice. The times are simulated.
32 devices in a mesh: rep: 4 (over z), fsdp: 8 (over y, x, core).
Axes of the slice: x: 2, y: 2, z: 4, core: 2. Of those that a mesh axis runs over, the one named last changes fastest.
Arguments:
- latents: float32 [2, 32, 256, 16], P(None, ('rep', 'fsdp')), may hold values from -6 to 6
- noise: float32 [2, 32, 256, 16], P(None, ('rep', 'fsdp')), may hold values from -6 to 6
- timesteps: int32 [2, 32], P(None, ('rep', 'fsdp')), may hold values from 0 to 999
- labels: int32 [2, 32], P(None, ('rep', 'fsdp')), may hold values from 0 to 1000
- patch_state: float32 [2, 16, 384], P(None, None, 'fsdp'), may hold values from -1 to 1, as said below
- time1_w: float32 [256, 384], P('fsdp'), may hold values from -0.375 to 0.375
- time1_f: float32 [640], replicated, may hold values from 0.001 to 1
- time2_w: float32 [384, 384], P('fsdp'), may hold values from -0.3125 to 0.3125
- time2_f: float32 [768], replicated, may hold values from 0.001 to 1
- table_w: float32 [1001, 384], P(None, 'fsdp'), may hold values from -4 to 4
- table_f: float32 [1385], replicated, may hold values from 0.001 to 1
- mod_w: float32 [384, 3072], P('fsdp'), may hold values from -0.3125 to 0.3125
- mod_f: float32 [3456], replicated, may hold values from 0.001 to 1
- qkv_w: float32 [384, 1152], P('fsdp'), may hold values from -0.3125 to 0.3125
- qkv_f: float32 [1536], replicated, may hold values from 0.001 to 1
- proj_w: float32 [384, 384], P('fsdp'), may hold values from -1.25 to 1.25
- proj_f: float32 [768], replicated, may hold values from 0.001 to 1
- fc1_w: float32 [384, 1536], P('fsdp'), may hold values from -0.3125 to 0.3125
- fc1_f: float32 [1920], replicated, may hold values from 0.001 to 1
- fc2_w: float32 [1536, 384], P('fsdp'), may hold values from -0.15625 to 0.15625
- fc2_f: float32 [1920], replicated, may hold values from 0.001 to 1
- out_state: float32 [2, 384, 32], P(None, 'fsdp'), may hold values from -1 to 1, as said below
Outputs:
- new_patch: float32 [2, 16, 384], P(None, None, 'fsdp')
- new_time1: float32 [256, 384], P('fsdp')
- new_time1_f: float32 [640], replicated
- new_time2: float32 [384, 384], P('fsdp')
- new_time2_f: float32 [768], replicated
- new_table: float32 [1001, 384], P(None, 'fsdp')
- new_table_f: float32 [1385], replicated
- new_mod: float32 [384, 3072], P('fsdp')
- new_mod_f: float32 [3456], replicated
- new_qkv: float32 [384, 1152], P('fsdp')
- new_qkv_f: float32 [1536], replicated
- new_proj: float32 [384, 384], P('fsdp')
- new_proj_f: float32 [768], replicated
- new_fc1: float32 [384, 1536], P('fsdp')
- new_fc1_f: float32 [1920], replicated
- new_fc2: float32 [1536, 384], P('fsdp')
- new_fc2_f: float32 [1920], replicated
- new_out: float32 [2, 384, 32], P(None, 'fsdp')
- loss: float32 [], replicated
- update_rms: float32 [10], replicated
Inputs may be any that keep to these rules, and one draw needn't show every extreme that they name: `patch_state`: the first slice holds weights, the second positive second moments. `out_state`: the first slice holds weights, the second positive second moments.
All inputs are finite; a program needn't handle non-finite values.
Results may differ from a plain program's by a relative error of at most 0.0085.
The roundings to bfloat16 on the way count: a program that leaves them out, or rounds other values in their place, can miss the bound.
Values may be sent and summed in bfloat16 or wider, within the bound.
No kernel may reach another device: no remote copies, remote signals or barrier semaphores. Data moves between devices by JAX's collectives and lax.ppermute only.
A program may use at most 128 MiB of HBM per device.

v0:
```python
import math

import jax
import jax.numpy as jnp
from jax import lax
from jax.sharding import PartitionSpec as P

D = 384
HEADS = 6
HEAD_DIM = 64
TFREQ = 256
GRID = 16
PIN = 16
POUT = 32
CLASSES = 1001
STEPS = 1000
MICRO = 2
TOK_IMG = 256


decay_rate = 0.5
clip_level = 1.0
step_rate = 0.5
grad_floor = 1e-30
norm_floor = 1e-06


def diffusion_tables():
    position = jnp.arange(STEPS, dtype=jnp.float32)
    betas = 0.0001 + (0.02 - 0.0001) * position / (STEPS - 1)
    log_bar = jnp.cumsum(jnp.log1p(-betas))
    log_prev = jnp.concatenate([jnp.zeros((1,), jnp.float32), log_bar[:-1]])
    posterior = betas * -jnp.expm1(log_prev) / -jnp.expm1(log_bar)
    posterior = jnp.where(position == 0.0, posterior[1], posterior)
    return (betas, log_bar, jnp.log(posterior))


def step_constants(tsteps):
    betas, log_bar, log_post = diffusion_tables()
    picks = tsteps[:, None] == jnp.arange(STEPS, dtype=jnp.int32)[None, :]

    def choose(table):
        return jnp.sum(jnp.where(picks, table[None, :], 0.0), axis=1)

    beta_now = choose(betas)
    bar_log = choose(log_bar)
    post_log = choose(log_post)
    remain = -jnp.expm1(bar_log)
    coef_sq = beta_now * beta_now / ((1.0 - beta_now) * remain)
    return (jnp.exp(0.5 * bar_log), jnp.sqrt(remain), jnp.log(beta_now), post_log, coef_sq)


def time_features(tsteps):
    halfway = TFREQ // 2
    frequency = jnp.exp(-math.log(10000.0) * jnp.arange(halfway, dtype=jnp.float32) / halfway)
    angles = tsteps.astype(jnp.float32)[:, None] * frequency[None, :]
    return jnp.concatenate([jnp.cos(angles), jnp.sin(angles)], axis=1)


def grid_positions():
    quarter = D // 4
    omegas = jnp.exp(-math.log(10000.0) * jnp.arange(quarter, dtype=jnp.float32) / quarter)
    tokens = jnp.arange(TOK_IMG, dtype=jnp.int32)
    row_pos = (tokens // GRID).astype(jnp.float32)[:, None] * omegas[None, :]
    col_pos = (tokens % GRID).astype(jnp.float32)[:, None] * omegas[None, :]
    return jnp.concatenate(
        [jnp.sin(row_pos), jnp.cos(row_pos), jnp.sin(col_pos), jnp.cos(col_pos)], axis=1
    )


def layer_norm(x):
    average = jnp.mean(x, axis=-1, keepdims=True)
    centred = x - average
    variance = jnp.mean(centred * centred, axis=-1, keepdims=True)
    return centred * lax.rsqrt(variance + norm_floor)


def modulate(hidden, modulation, slot):
    offset = modulation[:, slot * D : (slot + 1) * D][:, None, :]
    stretch = modulation[:, (slot + 1) * D : (slot + 2) * D][:, None, :]
    return layer_norm(hidden) * (1.0 + stretch) + offset


def image_losses(output, noise, consts):
    log_beta = consts[2][:, None, None]
    post_log = consts[3][:, None, None]
    guess = output[..., :PIN]
    mixing = (output[..., PIN:] + 1.0) * 0.5
    log_var = mixing * log_beta + (1.0 - mixing) * post_log
    miss_noise = guess - noise
    squared = miss_noise * miss_noise
    diverge = 0.5 * (
        -1.0
        + log_var
        - post_log
        + jnp.exp(post_log - log_var)
        + consts[4][:, None, None] * squared * jnp.exp(-log_var)
    )
    return jnp.mean(squared + diverge, axis=(1, 2))


def token_dot(left, right):
    return jnp.einsum("ntd,de->nte", left, right, preferred_element_type=jnp.float32)


def token_back(grad16, right):
    return jnp.einsum("nte,de->ntd", grad16, right, preferred_element_type=jnp.float32)


def token_weight(left16, grad16):
    return jnp.einsum("ntd,nte->de", left16, grad16, preferred_element_type=jnp.float32)


def label_picks(labels):
    return (labels[:, None] == jnp.arange(CLASSES, dtype=jnp.int32)[None, :]).astype(jnp.float32)


def micro_step(weights, latents, noise, tsteps, labels):
    w_patch, w_time1, w_time2, w_table, w_mod, w_qkv, w_proj, w_fc1, w_fc2, w_out = weights
    images = latents.shape[0]
    heads_shape = (images, TOK_IMG, HEADS, HEAD_DIM)
    consts = step_constants(tsteps)
    noisy16 = (consts[0][:, None, None] * latents + consts[1][:, None, None] * noise).astype(
        jnp.bfloat16
    )
    hidden0 = token_dot(noisy16, w_patch) + grid_positions()[None]
    features16 = time_features(tsteps).astype(jnp.bfloat16)
    time_hidden = jnp.dot(features16, w_time1, preferred_element_type=jnp.float32)
    time_act, back_time_act = jax.vjp(jax.nn.silu, time_hidden)
    time_act16 = time_act.astype(jnp.bfloat16)
    time_emb = jnp.dot(time_act16, w_time2, preferred_element_type=jnp.float32)
    picks = label_picks(labels)
    label_emb = jnp.dot(picks.astype(jnp.bfloat16), w_table, preferred_element_type=jnp.float32)
    condition = time_emb + label_emb
    cond_act, back_cond_act = jax.vjp(jax.nn.silu, condition)
    cond_act16 = cond_act.astype(jnp.bfloat16)
    modulation = jnp.dot(cond_act16, w_mod, preferred_element_type=jnp.float32)
    attn_in, back_attn_in = jax.vjp(lambda h, m: modulate(h, m, 0), hidden0, modulation)
    attn16 = attn_in.astype(jnp.bfloat16)
    qkv16 = token_dot(attn16, w_qkv).astype(jnp.bfloat16)
    queries = qkv16[..., :D].reshape(heads_shape)
    keyset = qkv16[..., D : 2 * D].reshape(heads_shape)
    values = qkv16[..., 2 * D :].reshape(heads_shape)
    scores = (
        jnp.einsum("nqhd,nkhd->nhqk", queries, keyset, preferred_element_type=jnp.float32) * 0.125
    )
    top_score = jnp.max(scores, axis=-1, keepdims=True)
    log_total = top_score + jnp.log(jnp.sum(jnp.exp(scores - top_score), axis=-1, keepdims=True))
    attn_prob16 = jnp.exp(scores - log_total).astype(jnp.bfloat16)
    mixture16 = (
        jnp.einsum("nhqk,nkhd->nqhd", attn_prob16, values, preferred_element_type=jnp.float32)
        .reshape(images, TOK_IMG, D)
        .astype(jnp.bfloat16)
    )
    branch = token_dot(mixture16, w_proj)
    hidden1, back_res1 = jax.vjp(
        lambda h, b, m: h + m[:, None, 2 * D : 3 * D] * b, hidden0, branch, modulation
    )
    mlp_in, back_mlp_in = jax.vjp(lambda h, m: modulate(h, m, 3), hidden1, modulation)
    mlp16 = mlp_in.astype(jnp.bfloat16)
    inner_pre = token_dot(mlp16, w_fc1)
    activated, back_gelu = jax.vjp(lambda v: jax.nn.gelu(v, approximate=True), inner_pre)
    activated16 = activated.astype(jnp.bfloat16)
    outer_out = token_dot(activated16, w_fc2)
    hidden2, back_res2 = jax.vjp(
        lambda h, b, m: h + m[:, None, 5 * D : 6 * D] * b, hidden1, outer_out, modulation
    )
    final_in, back_final = jax.vjp(lambda h, m: modulate(h, m, 6), hidden2, modulation)
    final16 = final_in.astype(jnp.bfloat16)
    output = token_dot(final16, w_out)
    losses, back_loss = jax.vjp(lambda o: image_losses(o, noise, consts), output)
    (d_output,) = back_loss(jnp.ones_like(losses))
    d_output16 = d_output.astype(jnp.bfloat16)
    grad_out = token_weight(final16, d_output16)
    d_h2, d_mod_final = back_final(token_back(d_output16, w_out))
    d_h1, d_outer, d_mod_res2 = back_res2(d_h2)
    d_outer16 = d_outer.astype(jnp.bfloat16)
    grad_fc2 = token_weight(activated16, d_outer16)
    (d_inner,) = back_gelu(token_back(d_outer16, w_fc2))
    d_inner16 = d_inner.astype(jnp.bfloat16)
    grad_fc1 = token_weight(mlp16, d_inner16)
    d_h1_mlp, d_mod_mlp = back_mlp_in(token_back(d_inner16, w_fc1))
    d_h1 = d_h1 + d_h1_mlp
    d_h0, d_branch, d_mod_res1 = back_res1(d_h1)
    d_branch16 = d_branch.astype(jnp.bfloat16)
    grad_proj = token_weight(mixture16, d_branch16)
    d_mixture16 = token_back(d_branch16, w_proj).astype(jnp.bfloat16).reshape(heads_shape)
    scores = (
        jnp.einsum("nqhd,nkhd->nhqk", queries, keyset, preferred_element_type=jnp.float32) * 0.125
    )
    attn_prob = jnp.exp(scores - log_total)
    attn_prob16 = attn_prob.astype(jnp.bfloat16)
    d_values = jnp.einsum(
        "nhqk,nqhd->nkhd", attn_prob16, d_mixture16, preferred_element_type=jnp.float32
    )
    d_prob = jnp.einsum("nqhd,nkhd->nhqk", d_mixture16, values, preferred_element_type=jnp.float32)
    d_scores16 = (
        attn_prob * (d_prob - jnp.sum(d_prob * attn_prob, axis=-1, keepdims=True))
    ).astype(jnp.bfloat16)
    d_queries = (
        jnp.einsum("nhqk,nkhd->nqhd", d_scores16, keyset, preferred_element_type=jnp.float32)
        * 0.125
    )
    d_keyset = (
        jnp.einsum("nhqk,nqhd->nkhd", d_scores16, queries, preferred_element_type=jnp.float32)
        * 0.125
    )
    d_qkv16 = jnp.concatenate(
        [
            d_queries.reshape(images, TOK_IMG, D),
            d_keyset.reshape(images, TOK_IMG, D),
            d_values.reshape(images, TOK_IMG, D),
        ],
        axis=-1,
    ).astype(jnp.bfloat16)
    grad_qkv = token_weight(attn16, d_qkv16)
    d_h0_attn, d_mod_attn = back_attn_in(token_back(d_qkv16, w_qkv))
    d_h0 = d_h0 + d_h0_attn
    d_mod16 = (d_mod_attn + d_mod_res1 + d_mod_mlp + d_mod_res2 + d_mod_final).astype(jnp.bfloat16)
    (d_condition,) = back_cond_act(jnp.dot(d_mod16, w_mod.T, preferred_element_type=jnp.float32))
    d_time16 = d_condition.astype(jnp.bfloat16)
    (d_time_hidden,) = back_time_act(
        jnp.dot(d_time16, w_time2.T, preferred_element_type=jnp.float32)
    )
    d_time_hidden16 = d_time_hidden.astype(jnp.bfloat16)
    grad_patch = jnp.einsum(
        "ntp,ntd->pd", noisy16, d_h0.astype(jnp.bfloat16), preferred_element_type=jnp.float32
    )
    token_grads = (grad_patch, grad_qkv, grad_proj, grad_fc1, grad_fc2, grad_out)
    factors = (
        features16,
        d_time_hidden16,
        time_act16,
        d_time16,
        cond_act16,
        d_mod16,
        picks,
        d_condition,
    )
    return (jnp.sum(losses), token_grads, factors)


def local_image_grads(factors):
    features16, d_time_hidden16, time_act16, d_time16, cond_act16, d_mod16, picks, d_condition = (
        factors
    )
    grad_time1 = jnp.dot(features16.T, d_time_hidden16, preferred_element_type=jnp.float32)
    grad_time2 = jnp.dot(time_act16.T, d_time16, preferred_element_type=jnp.float32)
    grad_table = jnp.dot(picks.T, d_condition, precision=lax.Precision.HIGHEST)
    grad_mod = jnp.dot(cond_act16.T, d_mod16, preferred_element_type=jnp.float32)
    return (grad_time1, grad_time2, grad_table, grad_mod)


def pack_means(grad, previous, sharded_dim, position):
    squares = grad * grad + grad_floor
    if sharded_dim == 0:
        col_count = grad.shape[1]
        row_count = previous.shape[0] - col_count
        row_part = lax.dynamic_update_slice(
            jnp.zeros((row_count,), jnp.float32),
            jnp.mean(squares, axis=1),
            (position * grad.shape[0],),
        )
        col_part = jnp.sum(squares, axis=0) / row_count
    else:
        row_count = grad.shape[0]
        col_count = previous.shape[0] - row_count
        row_part = jnp.sum(squares, axis=1) / col_count
        col_part = lax.dynamic_update_slice(
            jnp.zeros((col_count,), jnp.float32),
            jnp.mean(squares, axis=0),
            (position * grad.shape[1],),
        )
    return jnp.concatenate([row_part, col_part])


def factored_update(grad, previous, fresh_means, sharded_dim, position):
    renewed = decay_rate * previous + (1.0 - decay_rate) * fresh_means
    if sharded_dim == 0:
        row_count = previous.shape[0] - grad.shape[1]
        row_part = renewed[:row_count]
        local_rows = lax.dynamic_slice(row_part, (position * grad.shape[0],), (grad.shape[0],))
        estimate = local_rows[:, None] * renewed[row_count:][None, :] / jnp.mean(row_part)
        element_count = row_count * grad.shape[1]
    else:
        row_count = grad.shape[0]
        row_part = renewed[:row_count]
        local_cols = lax.dynamic_slice(
            renewed[row_count:], (position * grad.shape[1],), (grad.shape[1],)
        )
        estimate = row_part[:, None] * local_cols[None, :] / jnp.mean(row_part)
        element_count = row_count * (previous.shape[0] - row_count)
    return (grad * lax.rsqrt(estimate), element_count)


def add_tuples(left, right):
    if left is None:
        return right
    return tuple((one + two for one, two in zip(left, right)))


def per_device(
    latents,
    noise,
    timesteps,
    labels,
    patch_state,
    time1_w,
    time1_f,
    time2_w,
    time2_f,
    table_w,
    table_f,
    mod_w,
    mod_f,
    qkv_w,
    qkv_f,
    proj_w,
    proj_f,
    fc1_w,
    fc1_f,
    fc2_w,
    fc2_f,
    out_state,
):
    masters = (
        patch_state[0],
        time1_w,
        time2_w,
        table_w,
        mod_w,
        qkv_w,
        proj_w,
        fc1_w,
        fc2_w,
        out_state[0],
    )
    halves = [master.astype(jnp.bfloat16) for master in masters]
    position = lax.axis_index("fsdp")
    whole = None
    owned = None
    loss_part = jnp.zeros((), jnp.float32)
    for micro_idx in range(MICRO):
        whole = (
            lax.all_gather(halves[0], "fsdp", axis=1, tiled=True),
            lax.all_gather(halves[1], "fsdp", axis=0, tiled=True),
            lax.all_gather(halves[2], "fsdp", axis=0, tiled=True),
            lax.all_gather(halves[3], "fsdp", axis=1, tiled=True),
            lax.all_gather(halves[4], "fsdp", axis=0, tiled=True),
            lax.all_gather(halves[5], "fsdp", axis=0, tiled=True),
            lax.all_gather(halves[6], "fsdp", axis=0, tiled=True),
            lax.all_gather(halves[7], "fsdp", axis=0, tiled=True),
            lax.all_gather(halves[8], "fsdp", axis=0, tiled=True),
            lax.all_gather(halves[9], "fsdp", axis=0, tiled=True),
        )
        piece_loss, tok, factors = micro_step(
            whole, latents[micro_idx], noise[micro_idx], timesteps[micro_idx], labels[micro_idx]
        )
        loss_part = loss_part + piece_loss
        image_part = local_image_grads(factors)
        gradients = (
            tok[0],
            image_part[0],
            image_part[1],
            image_part[2],
            image_part[3],
            tok[1],
            tok[2],
            tok[3],
            tok[4],
            tok[5],
        )
        scattered = (
            lax.psum_scatter(gradients[0], "fsdp", scatter_dimension=1, tiled=True),
            lax.psum_scatter(gradients[1], "fsdp", scatter_dimension=0, tiled=True),
            lax.psum_scatter(gradients[2], "fsdp", scatter_dimension=0, tiled=True),
            lax.psum_scatter(gradients[3], "fsdp", scatter_dimension=1, tiled=True),
            lax.psum_scatter(gradients[4], "fsdp", scatter_dimension=0, tiled=True),
            lax.psum_scatter(gradients[5], "fsdp", scatter_dimension=0, tiled=True),
            lax.psum_scatter(gradients[6], "fsdp", scatter_dimension=0, tiled=True),
            lax.psum_scatter(gradients[7], "fsdp", scatter_dimension=0, tiled=True),
            lax.psum_scatter(gradients[8], "fsdp", scatter_dimension=0, tiled=True),
            lax.psum_scatter(gradients[9], "fsdp", scatter_dimension=0, tiled=True),
        )
        owned = add_tuples(owned, scattered)
    summed = lax.psum(
        (
            owned[0],
            owned[1],
            owned[2],
            owned[3],
            owned[4],
            owned[5],
            owned[6],
            owned[7],
            owned[8],
            owned[9],
            loss_part,
        ),
        "rep",
    )
    grads = summed[:10]
    factor_olds = (time1_f, time2_f, table_f, mod_f, qkv_f, proj_f, fc1_f, fc2_f)
    factor_dims = (0, 0, 1, 0, 0, 0, 0, 0)
    packs = [
        pack_means(grads[slot + 1], factor_olds[slot], factor_dims[slot], position)
        for slot in range(8)
    ]
    squares = [jnp.sum(master * master) for master in masters]
    totals = lax.psum(
        (
            packs[0],
            packs[1],
            packs[2],
            packs[3],
            packs[4],
            packs[5],
            packs[6],
            packs[7],
            squares[0],
            squares[1],
            squares[2],
            squares[3],
            squares[4],
            squares[5],
            squares[6],
            squares[7],
            squares[8],
            squares[9],
            summed[10],
        ),
        "fsdp",
    )
    fresh_list = []
    updates = []
    counts_list = []
    plain_patch = decay_rate * patch_state[1] + (1.0 - decay_rate) * (
        grads[0] * grads[0] + grad_floor
    )
    updates.append(grads[0] * lax.rsqrt(plain_patch))
    counts_list.append(PIN * D)
    for slot in range(8):
        update, element_count = factored_update(
            grads[slot + 1], factor_olds[slot], totals[slot], factor_dims[slot], position
        )
        fresh_list.append(totals[slot])
        updates.append(update)
        counts_list.append(element_count)
    plain_out = decay_rate * out_state[1] + (1.0 - decay_rate) * (grads[9] * grads[9] + grad_floor)
    updates.append(grads[9] * lax.rsqrt(plain_out))
    counts_list.append(D * POUT)
    update_sq = [jnp.sum(update * update) for update in updates]
    update_tot = lax.psum(
        (
            update_sq[0],
            update_sq[1],
            update_sq[2],
            update_sq[3],
            update_sq[4],
            update_sq[5],
            update_sq[6],
            update_sq[7],
            update_sq[8],
            update_sq[9],
        ),
        "fsdp",
    )
    rms_list = []
    new_masters = []
    for slot in range(10):
        size_rms = jnp.sqrt(update_tot[slot] / counts_list[slot])
        weight_rms = jnp.sqrt(totals[8 + slot] / counts_list[slot])
        rms_list.append(size_rms)
        new_masters.append(
            masters[slot]
            - step_rate * weight_rms * updates[slot] / jnp.maximum(1.0, size_rms / clip_level)
        )
    image_count = MICRO * latents.shape[1] * lax.axis_size("rep") * lax.axis_size("fsdp")
    loss = totals[18] / image_count
    new_patch = jnp.stack([new_masters[0], plain_patch])
    new_out = jnp.stack([new_masters[9], plain_out])
    return (
        new_patch,
        new_masters[1],
        fresh_list[0],
        new_masters[2],
        fresh_list[1],
        new_masters[3],
        fresh_list[2],
        new_masters[4],
        fresh_list[3],
        new_masters[5],
        fresh_list[4],
        new_masters[6],
        fresh_list[5],
        new_masters[7],
        fresh_list[6],
        new_masters[8],
        fresh_list[7],
        new_out,
        loss,
        jnp.stack(rms_list),
    )


def solution(mesh):
    placed = (
        P(None, ("rep", "fsdp"), None, None),
        P(None, ("rep", "fsdp"), None, None),
        P(None, ("rep", "fsdp")),
        P(None, ("rep", "fsdp")),
        P(None, None, "fsdp"),
        P("fsdp", None),
        P(),
        P("fsdp", None),
        P(),
        P(None, "fsdp"),
        P(),
        P("fsdp", None),
        P(),
        P("fsdp", None),
        P(),
        P("fsdp", None),
        P(),
        P("fsdp", None),
        P(),
        P("fsdp", None),
        P(),
        P(None, "fsdp", None),
    )
    return jax.shard_map(
        per_device,
        mesh=mesh,
        in_specs=placed,
        out_specs=(
            P(None, None, "fsdp"),
            P("fsdp", None),
            P(),
            P("fsdp", None),
            P(),
            P(None, "fsdp"),
            P(),
            P("fsdp", None),
            P(),
            P("fsdp", None),
            P(),
            P("fsdp", None),
            P(),
            P("fsdp", None),
            P(),
            P("fsdp", None),
            P(),
            P(None, "fsdp", None),
            P(),
            P(),
        ),
        check_vma=False,
    )
```

profile of v0, /device:TPU:0, one launch (start us, length us, event | category | flops | bytes accessed | tf_op | source)
XLA Modules:
  0.0 765.8 jit_solution(6455603297908200261)
XLA Ops:
  7.3 2.8 multiply_reduce_fusion.3
  10.2 2.4 multiply_reduce_fusion.29
  33.8 2.6 select_reduce_fusion
  37.7 10.5 %all-gather = bf16[8,48,16]{1,2,0:T(8,128)(2,1)S(1)} all-gather(bf16[1,48,16]{1,2,0:T(8,128)(2,1)S(1)} %fusion.66), channel_id=1, replica_groups=mesh['rep'=4,'fsdp'=8] {'fsdp'}, dimensions={0}, use_global_device_ids=true | all-gather | bytes 13824 | tf_op jit(solution)/shard_map/all_gather | solution.py:345
  49.6 9.2 %all-gather.1 = bf16[8,48,32]{1,2,0:T(8,128)(2,1)S(1)} all-gather(bf16[1,48,32]{1,2,0:T(8,128)(2,1)S(1)} %fusion.61), channel_id=1, replica_groups=mesh['rep'=4,'fsdp'=8] {'fsdp'}, dimensions={0}, use_global_device_ids=true | all-gather | bytes 27648 | tf_op jit(solution)/shard_map/all_gather | solution.py:354
  60.9 8.4 %all_gather.41 = bf16[256,384]{1,0:T(8,128)(2,1)S(1)} all-gather(bf16[32,384]{1,0:T(8,128)(2,1)S(1)} %get-tuple-element.194), channel_id=1, replica_groups=mesh['rep'=4,'fsdp'=8] {'fsdp'}, dimensions={0}, use_global_device_ids=true | all-gather | bytes 221184 | tf_op jit(solution)/shard_map/all_gather | solution.py:346
  70.9 9.4 %all_gather.46 = bf16[384,384]{1,0:T(8,128)(2,1)S(1)} all-gather(bf16[48,384]{1,0:T(8,128)(2,1)S(1)} %get-tuple-element.183), channel_id=1, replica_groups=mesh['rep'=4,'fsdp'=8] {'fsdp'}, dimensions={0}, use_global_device_ids=true | all-gather | bytes 331776 | tf_op jit(solution)/shard_map/all_gather | solution.py:351
  80.3 8.5 %all_gather.42 = bf16[384,384]{1,0:T(8,128)(2,1)S(1)} all-gather(bf16[48,384]{1,0:T(8,128)(2,1)S(1)} %get-tuple-element.185), channel_id=1, replica_groups=mesh['rep'=4,'fsdp'=8] {'fsdp'}, dimensions={0}, use_global_device_ids=true | all-gather | bytes 331776 | tf_op jit(solution)/shard_map/all_gather | solution.py:347
  91.4 10.4 %all_gather.43 = bf16[1001,384]{0,1:T(8,128)(2,1)S(1)} all-gather(bf16[1001,48]{0,1:T(8,128)(2,1)S(1)} %get-tuple-element.181), channel_id=1, replica_groups=mesh['rep'=4,'fsdp'=8] {'fsdp'}, dimensions={1}, use_global_device_ids=true | all-gather | bytes 864864 | tf_op jit(solution)/shard_map/all_gather | solution.py:348
  103.7 9.9 %all_gather.45 = bf16[384,1152]{1,0:T(8,128)(2,1)S(1)} all-gather(bf16[48,1152]{1,0:T(8,128)(2,1)S(1)} %get-tuple-element.179), channel_id=1, replica_groups=mesh['rep'=4,'fsdp'=8] {'fsdp'}, dimensions={0}, use_global_device_ids=true | all-gather | bytes 995328 | tf_op jit(solution)/shard_map/all_gather | solution.py:350
  113.6 2.4 fusion.163
  124.5 3.1 fusion.123
  127.6 2.6 fusion.145
  135.7 2.0 add_reduce_fusion
  154.5 2.1 convolution_convert_fusion.4
  177.4 2.2 fusion.119
  179.6 2.4 convolution_add_fusion.1
  184.7 2.1 convolution_add_fusion.2
  187.7 2.8 multiply_add_fusion
  198.3 37.9 %reduce-scatter.17.cloned.1.call-done = f32[48,384]{1,0:T(8,128)} async-done(((f32[384,384]{1,0:T(8,128)}), f32[48,384]{1,0:T(8,128)}) %reduce-scatter.17.cloned.1.call-update) | async-done | bytes 73744 | tf_op jit(solution)/shard_map/reduce_scatter | solution.py:376
  236.2 41.6 %reduce-scatter.19.cloned.1.call-done = f32[1001,48]{0,1:T(8,128)} async-done(((f32[1001,384]{0,1:T(8,128)}), f32[1001,48]{0,1:T(8,128)}) %reduce-scatter.19.cloned.1.call-update) | async-done | bytes 192208 | tf_op jit(solution)/shard_map/reduce_scatter | solution.py:377
  277.8 42.8 %reduce-scatter.23.cloned.1.call-done = f32[48,1152]{1,0:T(8,128)} async-done(((f32[384,1152]{1,0:T(8,128)}), f32[48,1152]{1,0:T(8,128)}) %reduce-scatter.23.cloned.1.call-update) | async-done | bytes 221200 | tf_op jit(solution)/shard_map/reduce_scatter | solution.py:379
  320.6 45.9 %reduce-scatter.29.cloned.1.call-done = f32[192,384]{1,0:T(8,128)} async-done(((f32[1536,384]{1,0:T(8,128)}), f32[192,384]{1,0:T(8,128)}) %reduce-scatter.29.cloned.1.call-update) | async-done | bytes 294928 | tf_op jit(solution)/shard_map/reduce_scatter | solution.py:382
  366.5 46.3 %reduce-scatter.27.cloned.1.call-done = f32[48,1536]{1,0:T(8,128)} async-done(((f32[384,1536]{1,0:T(8,128)}), f32[48,1536]{1,0:T(8,128)}) %reduce-scatter.27.cloned.1.call-update) | async-done | bytes 294928 | tf_op jit(solution)/shard_map/reduce_scatter | solution.py:381
  412.7 57.2 %reduce-scatter.21.cloned.1.call-done = f32[48,3072]{1,0:T(8,128)} async-done(((f32[384,3072]{1,0:T(8,128)}), f32[48,3072]{1,0:T(8,128)}) %reduce-scatter.21.cloned.1.call-update) | async-done | bytes 589840 | tf_op jit(solution)/shard_map/reduce_scatter | solution.py:378
  471.5 35.9 %reduce-scatter.31.cloned.1.call-done = f32[48,16]{1,0:T(8,128)} async-done(((f32[384,16]{1,0:T(8,128)}), f32[48,16]{1,0:T(8,128)}) %reduce-scatter.31.cloned.1.call-update) | async-done | bytes 3088
  508.2 36.2 %reduce-scatter.33.cloned.1.call-done = f32[48,32]{1,0:T(8,128)} async-done(((f32[384,32]{1,0:T(8,128)}), f32[48,32]{1,0:T(8,128)}) %reduce-scatter.33.cloned.1.call-update) | async-done | bytes 6160
  545.2 36.4 %reduce-scatter.15.cloned.1.call-done = f32[32,384]{1,0:T(8,128)} async-done(((f32[256,384]{1,0:T(8,128)}), f32[32,384]{1,0:T(8,128)}) %reduce-scatter.15.cloned.1.call-update) | async-done | bytes 49168 | tf_op jit(solution)/shard_map/reduce_scatter | solution.py:375
  581.6 22.5 %all-reduce.23 = (f32[16,48]{1,0:T(8,128)S(1)}, f32[32,384]{1,0:T(8,128)S(1)}, f32[48,32]{0,1:T(8,128)S(1)}, f32[]{:T(128)}) all-reduce(f32[16,48]{1,0:T(8,128)S(1)} %copy.111, f32[32,384]{1,0:T(8,128)} %reduce-scatter.15.cloned.1.call-done, f32[48,32]{0,1:T(8,128)S(1)} %copy.113, ...), channel_id=1, replica_groups=mesh['rep'=4,'fsdp'=8] {'rep'}, use_global_device_ids=true, to_apply=%region_42.43 | all-reduce | flops 14593 | bytes 116744 | tf_op jit(solution)/shard_map/psum | solution.py:386
  605.6 57.7 %all-reduce.27.cloned.1.call-done = (f32[48,384]{1,0:T(8,128)}, f32[1001,48]{0,1:T(8,128)}, f32[48,3072]{1,0:T(8,128)}, f32[48,1152]{1,0:T(8,128)}, f32[48,384]{...) async-done(((f32[48,384]{1,0:T(8,128)}, f32[1001,48]{0,1:T(8,128)}, f32[48,3072]{1,0:T(8,128)}, f32[48,1152]{1,0:T(8,128)}, f32[48,384]{1,0:T(8,128)}, ...) | async-done | bytes 1740496 | tf_op jit(solution)/shard_map/psum | solution.py:386
  671.1 24.5 %all-reduce.22 = (f32[640]{0:T(1024)S(1)}, f32[768]{0:T(1024)S(1)}, f32[1385]{0:T(1024)S(1)}, f32[3456]{0:T(1024)S(1)}, f32[1536]{0:T(1024)S(1)}, /*index=5*/f32...) all-reduce(f32[640]{0:T(1024)S(1)} %pad_maximum_fusion.14, ...), channel_id=1, replica_groups=mesh['rep'=4,'fsdp'=8] {'fsdp'}, use_global_device_ids=true, to_apply=%region_68.69 | all-reduce | flops 12393 | bytes 99144 | tf_op jit(solution)/shard_map/psum | solution.py:410
  712.4 22.3 %all-reduce.21 = (f32[]{:T(128)}, f32[]{:T(128)}, f32[]{:T(128)}, f32[]{:T(128)}, f32[]{:T(128)}, /*index=5*/f32[]{:T(128)}, f32[]{:T(128)}, f32[]{:T(128)}, f32...) all-reduce(f32[]{:T(128)} %get-tuple-element.59, ...), channel_id=1, replica_groups=mesh['rep'=4,'fsdp'=8] {'fsdp'}, use_global_device_ids=true, to_apply=%region_44.45 | all-reduce | flops 21 | bytes 168 | tf_op jit(solution)/shard_map/psum | solution.py:453
  (786 shorter events, 113.4 us)
Async XLA Ops:
  7.3 106.3 %all-gather.6.cloned.1.call-start = ((), (), s32[]{:S(2)}) async-start(), calls=%async_computation.10 | async-start | bytes 2654208 | tf_op jit(solution)/shard_map/all_gather | solution.py:349
  10.2 114.2 %all-gather.8.cloned.1.call-start = ((), (), s32[]{:S(2)}) async-start(), calls=%async_computation.11 | async-start | bytes 1327104 | tf_op jit(solution)/shard_map/all_gather | solution.py:352
  12.6 114.9 %all-gather.10.cloned.1.call-start = ((), (), s32[]{:S(2)}) async-start(), calls=%async_computation.12 | async-start | bytes 1327104 | tf_op jit(solution)/shard_map/all_gather | solution.py:353
  14.0 184.2 %reduce-scatter.25.cloned.1.call-start = ((), (), s32[]{:S(2)}) async-start(), calls=%async_computation.18 | async-start | bytes 663552 | tf_op jit(solution)/shard_map/reduce_scatter | solution.py:380
  163.3 72.8 %reduce-scatter.17.cloned.1.call-start = ((), (), s32[]{:S(2)}) async-start(), calls=%async_computation.14 | async-start | bytes 663552 | tf_op jit(solution)/shard_map/reduce_scatter | solution.py:376
  171.2 106.6 %reduce-scatter.19.cloned.1.call-start = ((), (), s32[]{:S(2)}) async-start(), calls=%async_computation.15 | async-start | bytes 1769472 | tf_op jit(solution)/shard_map/reduce_scatter | solution.py:377
  173.9 146.7 %reduce-scatter.23.cloned.1.call-start = ((), (), s32[]{:S(2)}) async-start(), calls=%async_computation.17 | async-start | bytes 1990656 | tf_op jit(solution)/shard_map/reduce_scatter | solution.py:379
  176.5 190.0 %reduce-scatter.29.cloned.1.call-start = ((), (), s32[]{:S(2)}) async-start(), calls=%async_computation.20 | async-start | bytes 2654208 | tf_op jit(solution)/shard_map/reduce_scatter | solution.py:382
  182.1 230.6 %reduce-scatter.27.cloned.1.call-start = ((), (), s32[]{:S(2)}) async-start(), calls=%async_computation.19 | async-start | bytes 2654208 | tf_op jit(solution)/shard_map/reduce_scatter | solution.py:381
  187.0 283.0 %reduce-scatter.21.cloned.1.call-start = ((), (), s32[]{:S(2)}) async-start(), calls=%async_computation.16 | async-start | bytes 5308416 | tf_op jit(solution)/shard_map/reduce_scatter | solution.py:378
  190.7 316.6 %reduce-scatter.31.cloned.1.call-start = ((), (), s32[]{:S(2)}) async-start(), calls=%async_computation.21 | async-start | bytes 221184
  194.5 349.8 %reduce-scatter.33.cloned.1.call-start = ((), (), s32[]{:S(2)}) async-start(), calls=%async_computation.22 | async-start | bytes 221184
  195.4 408.9 %copy-start.92 = (f32[2,16,48]{2,1,0:T(8,128)S(1)}, f32[2,16,48]{2,1,0:T(8,128)}, u32[]{:S(2)}) copy-start(f32[2,16,48]{2,1,0:T(8,128)} %param.26) | copy-start | bytes 18436
  195.4 409.5 %copy-start.83 = (f32[2,48,32]{1,2,0:T(8,128)S(1)}, f32[2,48,32]{1,2,0:T(8,128)}, u32[]{:S(2)}) copy-start(f32[2,48,32]{1,2,0:T(8,128)} %param.43) | copy-start | bytes 36868
  195.4 386.2 %reduce-scatter.15.cloned.1.call-start = ((), (), s32[]{:S(2)}) async-start(), calls=%async_computation.13 | async-start | bytes 442368 | tf_op jit(solution)/shard_map/reduce_scatter | solution.py:375
  196.4 466.9 %all-reduce.27.cloned.1.call-start = ((), (), s32[]{:S(2)}) async-start(), calls=%async_computation.23 | async-start | bytes 3489792 | tf_op jit(solution)/shard_map/psum | solution.py:386
  470.0 225.7 %copy-start.215 = (f32[640]{0:T(1024)S(1)}, f32[640]{0:T(1024)}, u32[]{:S(2)}) copy-start(f32[640]{0:T(1024)} %param.28) | copy-start | bytes 7684
  470.0 226.4 %copy-start.202 = (f32[1385]{0:T(1024)S(1)}, f32[1385]{0:T(1024)}, u32[]{:S(2)}) copy-start(f32[1385]{0:T(1024)} %param.32) | copy-start | bytes 16624
  470.0 227.0 %copy-start.203 = (f32[1536]{0:T(1024)S(1)}, f32[1536]{0:T(1024)}, u32[]{:S(2)}) copy-start(f32[1536]{0:T(1024)} %param.36) | copy-start | bytes 18436
  470.0 227.6 %copy-start.204 = (f32[1920]{0:T(1024)S(1)}, f32[1920]{0:T(1024)}, u32[]{:S(2)}) copy-start(f32[1920]{0:T(1024)} %param.40) | copy-start | bytes 23044
  470.0 228.2 %copy-start.205 = (f32[1920]{0:T(1024)S(1)}, f32[1920]{0:T(1024)}, u32[]{:S(2)}) copy-start(f32[1920]{0:T(1024)} %param.42) | copy-start | bytes 23044
  470.0 228.8 %copy-start.142 = (f32[3456]{0:T(1024)S(1)}, f32[3456]{0:T(1024)}, u32[]{:S(2)}) copy-start(f32[3456]{0:T(1024)} %param.34) | copy-start | bytes 41476
  470.0 229.5 %copy-start.216 = (f32[768]{0:T(1024)S(1)}, f32[768]{0:T(1024)}, u32[]{:S(2)}) copy-start(f32[768]{0:T(1024)} %param.30) | copy-start | bytes 9220
  470.0 230.2 %copy-start.217 = (f32[768]{0:T(1024)S(1)}, f32[768]{0:T(1024)}, u32[]{:S(2)}) copy-start(f32[768]{0:T(1024)} %param.38) | copy-start | bytes 9220
  670.0 79.1 %copy-start.28 = (f32[48,3072]{1,0:T(8,128)S(1)}, f32[48,3072]{1,0:T(8,128)}, u32[]{:S(2)}) copy-start(f32[48,3072]{1,0:T(8,128)} %param.33) | copy-start | bytes 1769476
  695.6 54.6 %copy-start.143 = (f32[3456]{0:T(1024)}, f32[3456]{0:T(1024)S(1)}, u32[]{:S(2)}) copy-start(f32[3456]{0:T(1024)S(1)} %get-tuple-element.104) | copy-start | bytes 41476
  695.6 54.5 %copy-start.206 = (f32[1385]{0:T(1024)}, f32[1385]{0:T(1024)S(1)}, u32[]{:S(2)}) copy-start(f32[1385]{0:T(1024)S(1)} %get-tuple-element.103) | copy-start | bytes 16624
  695.6 54.5 %copy-start.207 = (f32[1536]{0:T(1024)}, f32[1536]{0:T(1024)S(1)}, u32[]{:S(2)}) copy-start(f32[1536]{0:T(1024)S(1)} %get-tuple-element.105) | copy-start | bytes 18436
  695.6 54.5 %copy-start.208 = (f32[1920]{0:T(1024)}, f32[1920]{0:T(1024)S(1)}, u32[]{:S(2)}) copy-start(f32[1920]{0:T(1024)S(1)} %get-tuple-element.107) | copy-start | bytes 23044
  695.7 54.5 %copy-start.209 = (f32[1920]{0:T(1024)}, f32[1920]{0:T(1024)S(1)}, u32[]{:S(2)}) copy-start(f32[1920]{0:T(1024)S(1)} %get-tuple-element.108) | copy-start | bytes 23044
  695.7 54.5 %copy-start.218 = (f32[640]{0:T(1024)}, f32[640]{0:T(1024)S(1)}, u32[]{:S(2)}) copy-start(f32[640]{0:T(1024)S(1)} %get-tuple-element.101) | copy-start | bytes 7684
  695.7 54.5 %copy-start.219 = (f32[768]{0:T(1024)}, f32[768]{0:T(1024)S(1)}, u32[]{:S(2)}) copy-start(f32[768]{0:T(1024)S(1)} %get-tuple-element.102) | copy-start | bytes 9220
  (216 other events, 1468.5 us)
Sparse Core Ops, SparseCore 0:
  10.6 31.7 all-gather.5
  44.2 24.5 all-gather.7
  70.7 23.9 all-gather.9
  163.5 34.7 reduce-scatter.24
  201.8 34.3 reduce-scatter.16
  239.3 38.4 reduce-scatter.18
  281.2 39.3 reduce-scatter.22
  323.9 42.5 reduce-scatter.28
  370.2 42.4 reduce-scatter.26
  416.0 53.8 reduce-scatter.20
  473.8 33.4 reduce-scatter.30
  510.8 33.4 reduce-scatter.32
  547.7 33.8 reduce-scatter.14
  584.7 78.6 all-reduce.26
where the time goes:
time: 774 us; the launch traced here: 766 us
  waiting for transfers between devices  440 us (57%)
  blocking collectives  136 us (18%)
  other arithmetic  70 us (9%)
  between operations  49.4 us (6%)
  matrix products  48.7 us (6%)
  local copies, waits for them, and re-layouts  21.3 us (3%)
    unnamed x16, waiting for transfers between devices  72.3 us
    psum x1, waiting for transfers between devices, per_device(): lax.psum((owned[0], owned[1], owned[2], owned[3], owned[4], owned[5], own...  57.7 us
    reduce_scatter x1, waiting for transfers between devices, per_device(): lax.psum_scatter(gradients[4], 'fsdp', scatter_dimension=0, tiled=True)  57.2 us
    reduce_scatter x1, waiting for transfers between devices, per_device(): lax.psum_scatter(gradients[7], 'fsdp', scatter_dimension=0, tiled=True)  46.3 us
    reduce_scatter x1, waiting for transfers between devices, per_device(): lax.psum_scatter(gradients[8], 'fsdp', scatter_dimension=0, tiled=True)  45.9 us
    reduce_scatter x1, waiting for transfers between devices, per_device(): lax.psum_scatter(gradients[5], 'fsdp', scatter_dimension=0, tiled=True)  42.8 us
    reduce_scatter x1, waiting for transfers between devices, per_device(): lax.psum_scatter(gradients[3], 'fsdp', scatter_dimension=1, tiled=True)  41.6 us
    reduce_scatter x1, waiting for transfers between devices, per_device(): lax.psum_scatter(gradients[2], 'fsdp', scatter_dimension=0, tiled=True)  37.9 us
  transfers between devices with their start and end apart: 14, of which 11 were waited for; matrix products, arithmetic and copies ran while one was open for 9% of the time, Pallas kernels for 0%

commit v1 on v0

v1 whole, which is shorter than its diff:
```python
import math

import jax
import jax.numpy as jnp
import numpy as np
from jax import lax
from jax.sharding import PartitionSpec as P

D = 384
HEADS = 6
HEAD_DIM = 64
FF = 1536
TFREQ = 256
GRID = 16
PIN = 16
POUT = 32
CLASSES = 1001
STEPS = 1000
TOK_IMG = 256

decay_rate = 0.5
clip_level = 1.0
step_rate = 0.5
grad_floor = 1e-30
norm_floor = 1e-06
f32 = jnp.float32
bf16 = jnp.bfloat16


def plan_table():
    s = np.arange(STEPS, dtype=np.float64)
    beta = 1e-4 + (0.02 - 1e-4) * s / (STEPS - 1)
    lbar = np.cumsum(np.log1p(-beta))
    lprev = np.concatenate([[0.0], lbar[:-1]])
    post = beta * -np.expm1(lprev) / -np.expm1(lbar)
    post[0] = post[1]
    remain = -np.expm1(lbar)
    coef = beta * beta / ((1.0 - beta) * remain)
    rows = [np.exp(0.5 * lbar), np.sqrt(remain), np.log(beta), np.log(post), coef]
    return np.stack(rows + [np.zeros(STEPS)] * 3, axis=1).astype(np.float32)


def time_table():
    half = TFREQ // 2
    freq = np.exp(np.float32(-math.log(10000.0)) * np.arange(half, dtype=np.float32) / np.float32(half)).astype(np.float32)
    angles = np.arange(STEPS, dtype=np.float32)[:, None] * freq[None, :]
    wide = angles.astype(np.float64)
    return np.concatenate([np.cos(wide), np.sin(wide)], axis=1).astype(np.float32)


def place_table():
    quarter = D // 4
    om = np.exp(np.float32(-math.log(10000.0)) * np.arange(quarter, dtype=np.float32) / np.float32(quarter)).astype(np.float32)
    n = np.arange(TOK_IMG)
    row = ((n // GRID).astype(np.float32)[:, None] * om[None, :]).astype(np.float64)
    col = ((n % GRID).astype(np.float32)[:, None] * om[None, :]).astype(np.float64)
    return np.concatenate([np.sin(row), np.cos(row), np.sin(col), np.cos(col)], axis=1).astype(np.float32)


def pick(index, count):
    return (index[:, None] == jnp.arange(count, dtype=jnp.int32)[None, :]).astype(bf16)


def silu_pair(v):
    s = 1.0 / (1.0 + jnp.exp(-v))
    return v * s, s * (1.0 + v * (1.0 - s))


def norm_parts(x):
    mean = jnp.mean(x, axis=-1, keepdims=True)
    cen = x - mean
    inv = lax.rsqrt(jnp.mean(cen * cen, axis=-1, keepdims=True) + norm_floor)
    return cen * inv, inv


def norm_back(d_norm, normed, inv):
    a = jnp.mean(d_norm, axis=-1, keepdims=True)
    b = jnp.mean(d_norm * normed, axis=-1, keepdims=True)
    return inv * (d_norm - a - normed * b)


def dot(a, b):
    return jnp.dot(a, b, preferred_element_type=f32)


def dot_nt(a, b):
    return lax.dot_general(a, b, (((1,), (1,)), ((), ())), preferred_element_type=f32)


def dot_tn(a, b):
    return lax.dot_general(a, b, (((0,), (0,)), ((), ())), preferred_element_type=f32)


def flip(x, bit, axis="fsdp"):
    size = lax.axis_size(axis)
    return lax.ppermute(x, axis, [(i, i ^ bit) for i in range(size)])


def rep_gather(x):
    size = lax.axis_size("rep")
    me = lax.axis_index("rep")
    parts = jnp.stack([x] + [flip(x, k, "rep") for k in range(1, size)])
    return jnp.stack([lax.dynamic_index_in_dim(parts, me ^ j, 0, keepdims=False) for j in range(size)])


def rep_sum(x16):
    size = lax.axis_size("rep")
    parts = [x16.astype(f32)] + [flip(x16, k, "rep").astype(f32) for k in range(1, size)]
    while len(parts) > 1:
        parts = [parts[i] + parts[i + 1] for i in range(0, len(parts), 2)]
    return parts[0]


def sum_scatter(grad):
    size = lax.axis_size("fsdp")
    rows = grad.shape[0] // size
    if size != 8:
        return lax.psum_scatter(grad.astype(f32), "fsdp", scatter_dimension=0, tiled=True)
    me = lax.axis_index("fsdp")
    core, chip = me & 1, me >> 1
    g = grad.reshape(4, 2, rows, -1)
    keep = lax.dynamic_index_in_dim(g, core, 1, keepdims=False)
    send = lax.dynamic_index_in_dim(g, 1 - core, 1, keepdims=False).astype(bf16)
    both = keep.astype(f32) + flip(send, 1).astype(f32)
    own = lax.dynamic_index_in_dim(both, chip, 0, keepdims=False)
    low = both.astype(bf16)
    total = own
    for k in range(1, 4):
        total = total + flip(lax.dynamic_index_in_dim(low, chip ^ k, 0, keepdims=False), 2 * k).astype(f32)
    return total


def gather_rows(x):
    return lax.all_gather(x, "fsdp", axis=0, tiled=True)


def modulated(normed, mod, slot):
    return normed * (1.0 + mod[:, None, (slot + 1) * D : (slot + 2) * D]) + mod[:, None, slot * D : (slot + 1) * D]


def per_device(
    latents,
    noise,
    timesteps,
    labels,
    patch_state,
    time1_w,
    time1_f,
    time2_w,
    time2_f,
    table_w,
    table_f,
    mod_w,
    mod_f,
    qkv_w,
    qkv_f,
    proj_w,
    proj_f,
    fc1_w,
    fc1_f,
    fc2_w,
    fc2_f,
    out_state,
):
    reps, parts = lax.axis_size("rep"), lax.axis_size("fsdp")
    position = lax.axis_index("fsdp")
    masters = (patch_state[0], time1_w, time2_w, table_w, mod_w, qkv_w, proj_w, fc1_w, fc2_w, out_state[0])
    images = latents.shape[0] * latents.shape[1]
    latents = latents.reshape(images, TOK_IMG, PIN)
    noise = noise.reshape(images, TOK_IMG, PIN)
    tsteps = timesteps.reshape(images)
    labels = labels.reshape(images)
    own_d = D // parts
    own_t = TFREQ // parts

    info = jnp.stack([tsteps // 32, tsteps % 32, labels // 32, labels % 32]).reshape(1, 4 * images)
    info_row = jnp.pad(info.astype(bf16), ((0, 0), (0, D - 4 * images)))
    bundle = jnp.concatenate([time1_w.astype(bf16), time2_w.astype(bf16), info_row], axis=0)
    bundle = gather_rows(bundle).reshape(parts, own_t + own_d + 1, D)
    w_time1 = bundle[:, :own_t].reshape(TFREQ, D)
    w_time2 = bundle[:, own_t : own_t + own_d].reshape(D, D)
    info_rep = bundle[:, own_t + own_d, : 4 * images]

    head = jnp.pad(
        jnp.concatenate([patch_state[0].T, out_state[0]], axis=1), ((0, 0), (0, 128 - PIN - POUT))
    )
    w_rows = gather_rows(jnp.concatenate([qkv_w, proj_w, fc1_w, head], axis=1).astype(bf16))
    w_fc2 = gather_rows(fc2_w.astype(bf16))
    w_qkv = w_rows[:, : 3 * D]
    w_proj = w_rows[:, 3 * D : 4 * D]
    w_fc1 = w_rows[:, 4 * D : 4 * D + FF]
    w_patch_t = w_rows[:, 4 * D + FF : 4 * D + FF + PIN]
    w_out = w_rows[:, 4 * D + FF + PIN : 4 * D + FF + PIN + POUT]

    info_all = rep_gather(info_rep).reshape(reps * parts, 4, images).astype(jnp.int32)
    w_mod16 = mod_w.astype(bf16)
    w_table16 = table_w.astype(bf16)
    times = jnp.asarray(time_table(), bf16)

    def condition_path(info_any):
        ts = (info_any[:, 0] * 32 + info_any[:, 1]).reshape(-1)
        lab = (info_any[:, 2] * 32 + info_any[:, 3]).reshape(-1)
        feats16 = dot(pick(ts, STEPS), times).astype(bf16)
        time_act, time_slope = silu_pair(dot(feats16, w_time1))
        time_act16 = time_act.astype(bf16)
        time_emb = dot(time_act16, w_time2)
        own_emb = lax.dynamic_slice(time_emb, (0, position * own_d), (time_emb.shape[0], own_d))
        picks = pick(lab, CLASSES)
        cond_act, cond_slope = silu_pair(own_emb + dot(picks, w_table16))
        return feats16, time_act16, time_slope, picks, cond_act.astype(bf16), cond_slope

    info_here = info_rep.reshape(parts, 4, images).astype(jnp.int32)
    cond_here = condition_path(info_here)[4]
    shares = dot(cond_here, w_mod16).reshape(parts, images * 8 * D)
    mod = jnp.sum(lax.all_to_all(shares, "fsdp", 0, 0, tiled=True).reshape(parts, images, 8 * D), axis=0)

    plan = jnp.asarray(plan_table())
    consts = jnp.stack([lax.dynamic_index_in_dim(plan, tsteps[i], 0, keepdims=False) for i in range(images)])
    keep_s, keep_n, log_beta, post_log, coef = (consts[:, i][:, None, None] for i in range(5))

    def tok(x):
        return x.reshape(images * TOK_IMG, -1)

    def img(x):
        return x.reshape(images, TOK_IMG, -1)

    noisy16 = tok((keep_s * latents + keep_n * noise).astype(bf16))
    hidden0 = img(dot_nt(noisy16, w_patch_t)) + jnp.asarray(place_table())[None]
    norm0, inv0 = norm_parts(hidden0)
    attn16 = modulated(norm0, mod, 0).astype(bf16)
    qkv16 = dot(tok(attn16), w_qkv).astype(bf16)
    heads = qkv16.reshape(images, TOK_IMG, 3, HEADS, HEAD_DIM)
    q, k, v = (heads[:, :, i].transpose(0, 2, 1, 3) for i in range(3))
    scores = jnp.einsum("nhqd,nhkd->nhqk", q, k, preferred_element_type=f32) * 0.125
    prob = jnp.exp(scores - jnp.max(scores, axis=-1, keepdims=True))
    prob = prob / jnp.sum(prob, axis=-1, keepdims=True)
    prob16 = prob.astype(bf16)
    mixture16 = (
        jnp.einsum("nhqk,nhkd->nhqd", prob16, v, preferred_element_type=f32)
        .transpose(0, 2, 1, 3)
        .reshape(images * TOK_IMG, D)
        .astype(bf16)
    )
    gate1 = mod[:, None, 2 * D : 3 * D]
    gate2 = mod[:, None, 5 * D : 6 * D]
    branch = img(dot(mixture16, w_proj))
    hidden1 = hidden0 + gate1 * branch
    norm1, inv1 = norm_parts(hidden1)
    mlp16 = modulated(norm1, mod, 3).astype(bf16)
    inner = dot(tok(mlp16), w_fc1)
    cube = inner * inner
    bend = jnp.tanh(math.sqrt(2.0 / math.pi) * inner * (1.0 + 0.044715 * cube))
    act16 = (0.5 * inner * (1.0 + bend)).astype(bf16)
    slope = 0.5 * (1.0 + bend) + 0.5 * inner * (1.0 - bend * bend) * math.sqrt(2.0 / math.pi) * (
        1.0 + 3 * 0.044715 * cube
    )
    outer = img(dot(act16, w_fc2))
    hidden2 = hidden1 + gate2 * outer
    norm2, inv2 = norm_parts(hidden2)
    fin16 = modulated(norm2, mod, 6).astype(bf16)
    output = img(dot(tok(fin16), w_out))

    miss = output[..., :PIN] - noise
    mixing = (output[..., PIN:] + 1.0) * 0.5
    log_var = mixing * log_beta + (1.0 - mixing) * post_log
    ratio = jnp.exp(post_log - log_var)
    weigh = coef * jnp.exp(-log_var)
    square = miss * miss
    loss_part = jnp.sum(square + 0.5 * (-1.0 + log_var - post_log + ratio + weigh * square)) / (TOK_IMG * PIN)
    share = 1.0 / (TOK_IMG * PIN)
    d_guess = share * miss * (2.0 + weigh)
    d_logvar = share * 0.5 * (1.0 - ratio - weigh * square)
    d_mixed = d_logvar * (log_beta - post_log) * 0.5
    d_output16 = tok(jnp.concatenate([d_guess, d_mixed], axis=-1)).astype(bf16)

    g_out = dot_tn(tok(fin16), d_output16)
    d_fin = img(dot_nt(d_output16, w_out))
    d_off3 = jnp.sum(d_fin, axis=1)
    d_str3 = jnp.sum(d_fin * norm2, axis=1)
    d_h2 = norm_back(d_fin * (1.0 + mod[:, None, 7 * D :]), norm2, inv2)
    d_gate2 = jnp.sum(d_h2 * outer, axis=1)
    d_outer16 = tok((gate2 * d_h2).astype(bf16))
    g_fc2 = dot_tn(act16, d_outer16)
    d_inner16 = (dot_nt(d_outer16, w_fc2) * slope).astype(bf16)
    g_fc1 = dot_tn(tok(mlp16), d_inner16)
    d_mlp = img(dot_nt(d_inner16, w_fc1))
    d_off2 = jnp.sum(d_mlp, axis=1)
    d_str2 = jnp.sum(d_mlp * norm1, axis=1)
    d_h1 = d_h2 + norm_back(d_mlp * (1.0 + mod[:, None, 4 * D : 5 * D]), norm1, inv1)
    d_gate1 = jnp.sum(d_h1 * branch, axis=1)
    d_branch16 = tok((gate1 * d_h1).astype(bf16))
    g_proj = dot_tn(mixture16, d_branch16)
    d_mix16 = dot_nt(d_branch16, w_proj).astype(bf16)
    d_mix = d_mix16.reshape(images, TOK_IMG, HEADS, HEAD_DIM).transpose(0, 2, 1, 3)
    d_v = jnp.einsum("nhqk,nhqd->nhkd", prob16, d_mix, preferred_element_type=f32)
    d_prob = jnp.einsum("nhqd,nhkd->nhqk", d_mix, v, preferred_element_type=f32)
    d_scores16 = (prob * (d_prob - jnp.sum(d_prob * prob, axis=-1, keepdims=True))).astype(bf16)
    d_q = jnp.einsum("nhqk,nhkd->nhqd", d_scores16, k, preferred_element_type=f32) * 0.125
    d_k = jnp.einsum("nhqk,nhqd->nhkd", d_scores16, q, preferred_element_type=f32) * 0.125
    d_qkv16 = (
        jnp.stack([d_q, d_k, d_v]).transpose(1, 3, 0, 2, 4).reshape(images * TOK_IMG, 3 * D).astype(bf16)
    )
    g_qkv = dot_tn(tok(attn16), d_qkv16)
    d_attn = img(dot_nt(d_qkv16, w_qkv))
    d_off1 = jnp.sum(d_attn, axis=1)
    d_str1 = jnp.sum(d_attn * norm0, axis=1)
    d_h0 = d_h1 + norm_back(d_attn * (1.0 + mod[:, None, D : 2 * D]), norm0, inv0)
    g_patch_t = dot_tn(tok(d_h0.astype(bf16)), noisy16)

    d_mod16 = jnp.concatenate([d_off1, d_str1, d_gate1, d_off2, d_str2, d_gate2, d_off3, d_str3], axis=1).astype(bf16)
    d_mod_all = rep_gather(d_mod16).reshape(1, -1)
    d_mod_all = gather_rows(d_mod_all).reshape(parts, reps, images, 8 * D)
    d_mod_all = d_mod_all.transpose(1, 0, 2, 3).reshape(reps * parts * images, 8 * D)
    feats16, time_act16, time_slope, picks, cond16, cond_slope = condition_path(info_all)
    d_cond = dot_nt(d_mod_all, w_mod16) * cond_slope
    g_mod = dot_tn(cond16, d_mod_all)
    g_table = lax.dot_general(
        picks.astype(f32), d_cond, (((0,), (0,)), ((), ())), precision=lax.Precision.HIGHEST
    )
    d_time16 = lax.all_gather(d_cond.astype(bf16), "fsdp", axis=0)
    d_time16 = d_time16.transpose(1, 0, 2).reshape(-1, D)
    own_act16 = lax.dynamic_slice(time_act16, (0, position * own_d), (time_act16.shape[0], own_d))
    g_time2 = dot_tn(own_act16, d_time16)
    d_hid16 = (dot_nt(d_time16, w_time2) * time_slope).astype(bf16)
    own_feat16 = lax.dynamic_slice(feats16, (0, position * own_t), (feats16.shape[0], own_t))
    g_time1 = dot_tn(own_feat16, d_hid16)

    g_tail = sum_scatter(jnp.concatenate([g_qkv, g_patch_t, g_out, jnp.zeros((D, 128 - PIN - POUT), f32)], axis=1))
    g_mid = sum_scatter(jnp.concatenate([g_fc1, g_proj], axis=1))
    g_big = sum_scatter(g_fc2)
    g_fc2 = rep_sum(g_big.astype(bf16))
    g_mid = rep_sum(g_mid.astype(bf16))
    g_tail = rep_sum(g_tail.astype(bf16))
    grads = (
        g_tail[:, 3 * D : 3 * D + PIN].T,
        g_time1,
        g_time2,
        g_table,
        g_mod,
        g_tail[:, : 3 * D],
        g_mid[:, FF:],
        g_mid[:, :FF],
        g_fc2,
        g_tail[:, 3 * D + PIN : 3 * D + PIN + POUT],
    )
    loss_part = lax.psum(loss_part, "rep")
    olds = (time1_f, time2_f, table_f, mod_f, qkv_f, proj_f, fc1_f, fc2_f)
    dims = (0, 0, 1, 0, 0, 0, 0, 0)

    packs = []
    for slot in range(8):
        grad, dim = grads[slot + 1], dims[slot]
        squares = grad * grad + grad_floor
        near = jnp.sum(squares, axis=1 - dim)
        far = jnp.sum(squares, axis=dim)
        spread = lax.dynamic_update_slice(
            jnp.zeros((near.shape[0] * parts,), f32), near / far.shape[0], (position * near.shape[0],)
        )
        far = far / (near.shape[0] * parts)
        packs.append(jnp.concatenate([spread, far] if dim == 0 else [far, spread]))
    tail = jnp.stack([jnp.sum(m * m) for m in masters] + [loss_part])
    lengths = [pack.shape[0] for pack in packs]
    totals = lax.psum(jnp.concatenate(packs + [tail]), "fsdp")
    fresh = []
    start = 0
    for length in lengths:
        fresh.append(totals[start : start + length])
        start += length
    square_tot = totals[start : start + 10]
    loss = totals[start + 10] / (images * reps * parts)

    updates, counts = [], []
    plain = []
    for slot in range(10):
        grad = grads[slot]
        if slot in (0, 9):
            state = patch_state if slot == 0 else out_state
            moment = decay_rate * state[1] + (1.0 - decay_rate) * (grad * grad + grad_floor)
            plain.append(moment)
            updates.append(grad * lax.rsqrt(moment))
            counts.append(grad.size * parts)
            continue
        dim = dims[slot - 1]
        renewed = decay_rate * olds[slot - 1] + (1.0 - decay_rate) * fresh[slot - 1]
        rows = grad.shape[0] * (parts if dim == 0 else 1)
        row, col = renewed[:rows], renewed[rows:]
        mean_row = jnp.mean(row)
        if dim == 0:
            row = lax.dynamic_slice(row, (position * grad.shape[0],), (grad.shape[0],))
        else:
            col = lax.dynamic_slice(col, (position * grad.shape[1],), (grad.shape[1],))
        updates.append(grad * lax.rsqrt(row[:, None] * col[None, :] / mean_row))
        counts.append(grad.size * parts)
    update_tot = lax.psum(jnp.stack([jnp.sum(u * u) for u in updates]), "fsdp")
    sizes = np.asarray(counts, np.float32)
    size_rms = jnp.sqrt(update_tot / sizes)
    factor = step_rate * jnp.sqrt(square_tot / sizes) / jnp.maximum(1.0, size_rms / clip_level)
    new = [masters[s] - factor[s] * updates[s] for s in range(10)]
    result = [jnp.stack([new[0], plain[0]])]
    for slot in range(8):
        result += [new[slot + 1], fresh[slot]]
    return tuple(result) + (jnp.stack([new[9], plain[1]]), loss, size_rms)


def solution(mesh):
    images = P(None, ("rep", "fsdp"), None, None)
    singles = P(None, ("rep", "fsdp"))
    rows, cols = P("fsdp", None), P(None, "fsdp")
    placed = (images, images, singles, singles, P(None, None, "fsdp"))
    placed += (rows, P(), rows, P(), cols, P()) + (rows, P()) * 5 + (P(None, "fsdp", None),)
    results = (P(None, None, "fsdp"), rows, P(), rows, P(), cols, P()) + (rows, P()) * 5
    results += (P(None, "fsdp", None), P(), P())
    return jax.shard_map(per_device, mesh=mesh, in_specs=placed, out_specs=results, check_vma=False)
```

time: 774 us -> 355 us (0.46)
  waiting for transfers between devices: 440 us -> 31 us
  blocking collectives: 136 us -> 81.2 us
  local copies, waits for them, and re-layouts: 21.3 us -> 58.6 us
  starting transfers between devices: 0.83 us -> 32.5 us
  between operations: 49.4 us -> 27 us
    reduce_scatter x8 -> x0, waiting for transfers between devices: 310 us -> none  [the longest x1 57.2 us: per_device(): lax.psum_scatter(gradients[4], 'fsdp', scatter_dimension=0, tiled=True)]
    unnamed x16 -> x2, waiting for transfers between devices: 72.3 us -> 0.03 us
    psum x1 -> x0, waiting for transfers between devices: 57.7 us -> none  [per_device(): lax.psum((owned[0], owned[1], owned[2], owned[3], owned[4], owned[5], own...]
    all_gather x7 -> x3, blocking collectives: 66.3 us -> 33 us  [the longest x2 23.7 us: gather_rows(): return lax.all_gather(x, 'fsdp', axis=0, tiled=True)]
    ppermute x0 -> x27, waiting for transfers between devices: none -> 31 us  [flip(): return lax.ppermute(x, axis, [(i, i ^ bit) for i in range(size)])]
    ppermute x0 -> x27, starting transfers between devices: none -> 29 us  [flip(): return lax.ppermute(x, axis, [(i, i ^ bit) for i in range(size)])]
    psum x3, blocking collectives: 69.3 us -> 48.2 us  [the longest x1 23.1 us: per_device(): totals = lax.psum(jnp.concatenate(packs + [tail]), 'fsdp')]
    reduce_sum x46 -> x33, other arithmetic: 37.4 us -> 23.5 us  [the longest x10 12.5 us: per_device(): tail = jnp.stack([jnp.sum(m * m) for m in masters] + [loss_part])]
  transfers between devices with their start and end apart: 14 -> 30, of which waited for: 11 -> 11; matrix products, arithmetic and copies ran while one was open for 9% -> 21% of each run, Pallas kernels for 0% -> 0%
where the time goes in v1:
time: 355 us; the launch traced here: 348 us
  blocking collectives  81.2 us (23%)
  other arithmetic  76.1 us (21%)
  local copies, waits for them, and re-layouts  58.6 us (17%)
  matrix products  41.7 us (12%)
  starting transfers between devices  32.5 us (9%)
  waiting for transfers between devices  31 us (9%)
  between operations  27 us (8%)
    ppermute x27, waiting for transfers between devices, flip(): return lax.ppermute(x, axis, [(i, i ^ bit) for i in range(size)])  31 us
    ppermute x27, starting transfers between devices, flip(): return lax.ppermute(x, axis, [(i, i ^ bit) for i in range(size)])  29 us
    all_gather x2, blocking collectives, gather_rows(): return lax.all_gather(x, 'fsdp', axis=0, tiled=True)  23.7 us
    psum x1, blocking collectives, per_device(): totals = lax.psum(jnp.concatenate(packs + [tail]), 'fsdp')  23.1 us
    unnamed x196, local copies, waits for them, and re-layouts  18.6 us
    sub x8, other arithmetic, per_device(): new = [masters[s] - factor[s] * updates[s] for s in range(10)]  16 us
    dot_general x9, matrix products, dot_tn(): lax.dot_general(a, b, (((0,), (0,)), ((), ())), preferred_element_type=f32)  13.8 us
    psum x1, blocking collectives, per_device(): loss_part = lax.psum(loss_part, 'rep')  13.4 us
  transfers between devices with their start and end apart: 30, of which 11 were waited for; matrix products, arithmetic and copies ran while one was open for 21% of the time, Pallas kernels for 0%

profile of v1, /device:TPU:0, one launch (start us, length us, event | category | flops | bytes accessed | tf_op | source)
XLA Modules:
  0.0 348.1 jit_solution(5461181253499068820)
XLA Ops:
  19.7 12.8 %all-gather.1 = bf16[8,81,384]{2,1,0:T(8,128)(2,1)S(1)} all-gather(bf16[1,81,384]{2,1,0:T(8,128)(2,1)S(1)} %fusion.69), channel_id=1, replica_groups=mesh['rep'=4,'fsdp'=8] {'fsdp'}, dimensions={0}, use_global_device_ids=true | all-gather | bytes 559872 | tf_op jit(solution)/shard_map/all_gather | solution.py:134
  32.5 3.8 %collective-permute-start.2 = (bf16[8,8]{1,0:T(8,128)(2,1)S(1)}, bf16[8,8]{1,0:T(8,128)(2,1)S(1)}, u32[]{:S(2)}, u32[]{:S(2)}) collective-permute-start(bf16[8,8]{1,0:T(8,128)(2,1)S(1)} %get-tuple-element.283), channel_id=1, source_target_pairs={{0,24},{8,16},{16,8},{24,0},{1,25},{9,17},{17,9},{25,1},{2,26},{10... | collective-permute-start | bytes 392 | tf_op jit(solution)/shard_map/ppermute | solution.py:96
  39.4 3.4 all-to-all-start
  63.1 2.9 reshape.676
  68.4 2.5 fusion.144
  80.6 3.4 fusion.124
  91.3 2.4 fusion.1
  93.7 2.2 fusion.148
  101.5 2.6 convolution_bitcast_fusion
  107.6 2.2 copy.255
  109.9 3.1 multiply_reduce_fusion.6
  113.1 3.8 %collective-permute-start.5 = (bf16[2,3072]{1,0:T(2,128)(2,1)S(1)}, bf16[2,3072]{1,0:T(2,128)(2,1)S(1)}, u32[]{:S(2)}, u32[]{:S(2)}) collective-permute-start(bf16[2,3072]{1,0:T(2,128)(2,1)S(1)} %constant_dynamic-update-slice_fusion.8), channel_id=1, source_target_pairs={{0,24},{8,16},{16,8},{24,0},{1,25},{9,17},{17,9},{25,1},{2,26},{10... | collective-permute-start | bytes 36872 | tf_op jit(solution)/shard_map/ppermute | solution.py:96
  119.5 13.4 %psum.21 = f32[1]{0:T(128)} all-reduce(f32[1]{0:T(128)} %bitcast.96), channel_id=1, replica_groups=mesh['rep'=4,'fsdp'=8] {'rep'}, use_global_device_ids=true, to_apply=%region_51.52 | all-reduce | flops 1 | bytes 8 | tf_op jit(solution)/shard_map/psum | solution.py:346
  142.6 2.9 concatenate.68
  147.9 10.9 %all-gather.2 = bf16[8,1,24576]{2,1,0:T(2,128)(2,1)S(1)} all-gather(bf16[1,1,24576]{2,1,0:T(2,128)(2,1)S(1)} %reshape.694), channel_id=1, replica_groups=mesh['rep'=4,'fsdp'=8] {'fsdp'}, dimensions={0}, use_global_device_ids=true | all-gather | bytes 442368 | tf_op jit(solution)/shard_map/all_gather | solution.py:134
  158.8 2.4 reduce.8
  165.5 9.3 %all-gather.3 = bf16[8,64,48]{1,2,0:T(8,128)(2,1)S(1)} all-gather(bf16[1,64,48]{1,2,0:T(8,128)(2,1)S(1)} %convert_bitcast_fusion), channel_id=2, replica_groups=mesh['rep'=4,'fsdp'=8] {'fsdp'}, dimensions={0}, use_global_device_ids=true | all-gather | bytes 55296 | tf_op jit(solution)/shard_map/all_gather | solution.py:320
  175.5 2.3 fusion.70
  178.3 2.7 fusion.77
  200.2 2.7 collective-permute-done.23
  207.9 3.0 collective-permute-start.24
  210.9 4.1 %collective-permute-done.11 = bf16[48,1280]{1,0:T(8,128)(2,1)S(1)} collective-permute-done((bf16[48,1280]{1,0:T(8,128)(2,1)S(1)}, bf16[48,1280]{1,0:T(8,128)(2,1)S(1)}, u32[]{:S(2)}, u32[]{:S(2)}) %collective-permute-start.11) | collective-permute-done | bytes 122912 | tf_op jit(solution)/shard_map/ppermute | solution.py:96
  225.5 3.6 %collective-permute-start.19 = (bf16[48,1920]{1,0:T(8,128)(2,1)S(1)}, bf16[48,1920]{1,0:T(8,128)(2,1)S(1)}, u32[]{:S(2)}, u32[]{:S(2)}) collective-permute-start(bf16[48,1920]{1,0:T(8,128)(2,1)S(1)} %fusion.31), channel_id=1, source_target_pairs={{0,24},{8,16},{16,8},{24,0},{1,25},{9,17},{17,9},{25,1},{2,26},{10... | collective-permute-start | bytes 552968 | tf_op jit(solution)/shard_map/ppermute | solution.py:96
  230.1 4.7 %collective-permute-done.19 = bf16[48,1920]{1,0:T(8,128)(2,1)S(1)} collective-permute-done((bf16[48,1920]{1,0:T(8,128)(2,1)S(1)}, bf16[48,1920]{1,0:T(8,128)(2,1)S(1)}, u32[]{:S(2)}, u32[]{:S(2)}) %collective-permute-start.19) | collective-permute-done | bytes 184352 | tf_op jit(solution)/shard_map/ppermute | solution.py:96
  234.7 9.4 %collective-permute-done.18 = bf16[48,1920]{1,0:T(8,128)(2,1)S(1)} collective-permute-done((bf16[48,1920]{1,0:T(8,128)(2,1)S(1)}, bf16[48,1920]{1,0:T(8,128)(2,1)S(1)}, u32[]{:S(2)}, u32[]{:S(2)}) %collective-permute-start.18) | collective-permute-done | bytes 184352 | tf_op jit(solution)/shard_map/ppermute | solution.py:96
  244.8 7.8 %concatenate.70 = f32[12404]{0:T(1024)S(1)} concatenate(f32[256]{0:T(256)} %copy-done.85, f32[384]{0:T(512)} %broadcast_multiply_fusion.7, f32[384]{0:T(512)S(1)} %copy-done.69, f32[384]{0:T(512)} %broadcast_multiply_fusion.6, f32[1001]{0:T(1024)S(1)} %broadcast_multiply_fusion.3, f32[384]{0:T(512)S(1)} %copy-done.71, f32[384]{0:T(512)S(1)} %copy-done.73, f32[3072]{0:T(1024)S(1)} %copy-done.58, ...), dimensions={0} | concatenate | bytes 99232 | tf_op jit(solution)/shard_map/concatenate | solution.py:363
  252.6 23.1 %psum.22 = f32[12404]{0:T(1024)S(1)} all-reduce(f32[12404]{0:T(1024)S(1)} %concatenate.70), channel_id=1, replica_groups=mesh['rep'=4,'fsdp'=8] {'fsdp'}, use_global_device_ids=true, to_apply=%region_52.53 | all-reduce | flops 12404 | bytes 99232 | tf_op jit(solution)/shard_map/psum | solution.py:363
  299.4 6.5 %stack.185 = f32[10]{0:T(128)S(1)} concatenate(f32[1]{0:T(128)} %bitcast.99, f32[1]{0:T(128)} %bitcast.100, f32[1]{0:T(128)} %bitcast.101, f32[1]{0:T(128)} %bitcast.102, f32[1]{0:T(128)} %bitcast.103, f32[1]{0:T(128)} %bitcast.104, f32[1]{0:T(128)} %bitcast.105, f32[1]{0:T(128)} %bitcast.106, f32[1]{0:T(128)} %bitcast.107, f32[1]{0:T(128)} %bitcast.109), dimensions={0} | concatenate | bytes 80 | tf_op jit(solution)/shard_map/stack | solution.py:394
  306.6 11.8 %psum.23 = f32[10]{0:T(128)S(1)} all-reduce(f32[10]{0:T(128)S(1)} %stack.185), channel_id=1, replica_groups=mesh['rep'=4,'fsdp'=8] {'fsdp'}, use_global_device_ids=true, to_apply=%region_71.72 | all-reduce | flops 10 | bytes 80 | tf_op jit(solution)/shard_map/psum | solution.py:394
  320.4 2.3 multiply_subtract_fusion
  328.2 2.2 multiply_subtract_fusion.7
  334.9 2.2 multiply_subtract_fusion.5
  (466 shorter events, 148.9 us)
Async XLA Ops:
  7.2 49.3 %all-gather.7.cloned.1.call-start = ((), (), s32[]{:S(2)}) async-start(), calls=%async_computation.1 | async-start | bytes 2764800 | tf_op jit(solution)/shard_map/all_gather | solution.py:134
  32.5 21.4 %collective-permute-start.2 = (bf16[8,8]{1,0:T(8,128)(2,1)S(1)}, bf16[8,8]{1,0:T(8,128)(2,1)S(1)}, u32[]{:S(2)}, u32[]{:S(2)}) collective-permute-start(bf16[8,8]{1,0:T(8,128)(2,1)S(1)} %get-tuple-element.283), channel_id=1, source_target_pairs={{0,24},{8,16},{16,8},{24,0},{1,25},{9,17},{17,9},{25,1},{2,26},{10... | collective-permute-start | bytes 392 | tf_op jit(solution)/shard_map/ppermute | solution.py:96
  36.3 17.6 %collective-permute-start.1 = (bf16[8,8]{1,0:T(8,128)(2,1)S(1)}, bf16[8,8]{1,0:T(8,128)(2,1)S(1)}, u32[]{:S(2)}, u32[]{:S(2)}) collective-permute-start(bf16[8,8]{1,0:T(8,128)(2,1)S(1)} %get-tuple-element.283), channel_id=1, source_target_pairs={{0,16},{8,24},{16,0},{24,8},{1,17},{9,25},{17,1},{25,9},{2,18},{10... | collective-permute-start | bytes 392 | tf_op jit(solution)/shard_map/ppermute | solution.py:96
  36.3 17.6 %collective-permute-start = (bf16[8,8]{1,0:T(8,128)(2,1)S(1)}, bf16[8,8]{1,0:T(8,128)(2,1)S(1)}, u32[]{:S(2)}, u32[]{:S(2)}) collective-permute-start(bf16[8,8]{1,0:T(8,128)(2,1)S(1)} %get-tuple-element.283), channel_id=1, source_target_pairs={{0,8},{8,0},{16,24},{24,16},{1,9},{9,1},{17,25},{25,17},{2,10},{10... | collective-permute-start | bytes 392 | tf_op jit(solution)/shard_map/ppermute | solution.py:96
  39.4 16.9 %all-to-all-start = ((f32[8,1,6144]{2,1,0:T(1,128)}), f32[8,1,6144]{2,1,0:T(1,128)S(1)}, u32[]{:S(2)}, u32[]{:S(2)}) async-start(f32[8,1,6144]{2,1,0:T(1,128)} %all_to_all.8), calls=%async_computation | async-start | bytes 393216 | tf_op jit(solution)/shard_map/all_to_all | solution.py:215
  42.8 37.8 %all-gather.9.cloned.1.call-start = ((), (), s32[]{:S(2)}) async-start(), calls=%async_computation.2 | async-start | bytes 1327104 | tf_op jit(solution)/shard_map/all_gather | solution.py:134
  56.3 105.6 %copy-start.51 = (f32[64,48]{0,1:T(8,128)}, f32[64,48]{0,1:T(8,128)S(1)}, u32[]{:S(2)}) copy-start(f32[64,48]{0,1:T(8,128)S(1)} %convolution_add_fusion.1) | copy-start | bytes 36868
  113.1 34.4 %collective-permute-start.5 = (bf16[2,3072]{1,0:T(2,128)(2,1)S(1)}, bf16[2,3072]{1,0:T(2,128)(2,1)S(1)}, u32[]{:S(2)}, u32[]{:S(2)}) collective-permute-start(bf16[2,3072]{1,0:T(2,128)(2,1)S(1)} %constant_dynamic-update-slice_fusion.8), channel_id=1, source_target_pairs={{0,24},{8,16},{16,8},{24,0},{1,25},{9,17},{17,9},{25,1},{2,26},{10... | collective-permute-start | bytes 36872 | tf_op jit(solution)/shard_map/ppermute | solution.py:96
  116.9 30.7 %collective-permute-start.4 = (bf16[2,3072]{1,0:T(2,128)(2,1)S(1)}, bf16[2,3072]{1,0:T(2,128)(2,1)S(1)}, u32[]{:S(2)}, u32[]{:S(2)}) collective-permute-start(bf16[2,3072]{1,0:T(2,128)(2,1)S(1)} %constant_dynamic-update-slice_fusion.8), channel_id=1, source_target_pairs={{0,16},{8,24},{16,0},{24,8},{1,17},{9,25},{17,1},{25,9},{2,18},{10... | collective-permute-start | bytes 36872 | tf_op jit(solution)/shard_map/ppermute | solution.py:96
  116.9 30.7 %collective-permute-start.3 = (bf16[2,3072]{1,0:T(2,128)(2,1)S(1)}, bf16[2,3072]{1,0:T(2,128)(2,1)S(1)}, u32[]{:S(2)}, u32[]{:S(2)}) collective-permute-start(bf16[2,3072]{1,0:T(2,128)(2,1)S(1)} %constant_dynamic-update-slice_fusion.8), channel_id=1, source_target_pairs={{0,8},{8,0},{16,24},{24,16},{1,9},{9,1},{17,25},{25,17},{2,10},{10... | collective-permute-start | bytes 36872 | tf_op jit(solution)/shard_map/ppermute | solution.py:96
  137.8 54.0 %collective-permute-start.20 = (bf16[4,192,384]{2,1,0:T(8,128)(2,1)}, bf16[4,192,384]{2,1,0:T(8,128)(2,1)}, u32[]{:S(2)}, u32[]{:S(2)}) collective-permute-start(bf16[4,192,384]{2,1,0:T(8,128)(2,1)} %fusion.25), channel_id=1, source_target_pairs={{0,1},{1,0},{2,3},{3,2},{4,5},{5,4},{6,7},{7,6},{8,9},{9,8},{10,11... | collective-permute-start | bytes 1769480 | tf_op jit(solution)/shard_map/ppermute | solution.py:96
  140.0 65.1 %collective-permute-start.13 = (bf16[4,48,1920]{2,1,0:T(8,128)(2,1)}, bf16[4,48,1920]{2,1,0:T(8,128)(2,1)}, u32[]{:S(2)}, u32[]{:S(2)}) collective-permute-start(bf16[4,48,1920]{2,1,0:T(8,128)(2,1)} %fusion.24), channel_id=1, source_target_pairs={{0,1},{1,0},{2,3},{3,2},{4,5},{5,4},{6,7},{7,6},{8,9},{9,8},{10,11... | collective-permute-start | bytes 2211848 | tf_op jit(solution)/shard_map/ppermute | solution.py:96
  147.5 39.1 %collective-permute-start.6 = (bf16[4,48,1280]{2,1,0:T(8,128)(2,1)}, bf16[4,48,1280]{2,1,0:T(8,128)(2,1)}, u32[]{:S(2)}, u32[]{:S(2)}) collective-permute-start(bf16[4,48,1280]{2,1,0:T(8,128)(2,1)} %fusion.28), channel_id=1, source_target_pairs={{0,1},{1,0},{2,3},{3,2},{4,5},{5,4},{6,7},{7,6},{8,9},{9,8},{10,11... | collective-permute-start | bytes 1474568 | tf_op jit(solution)/shard_map/ppermute | solution.py:96
  188.1 6.2 %collective-permute-start.7 = (bf16[48,1280]{1,0:T(8,128)(2,1)S(1)}, bf16[48,1280]{1,0:T(8,128)(2,1)S(1)}, u32[]{:S(2)}, u32[]{:S(2)}) collective-permute-start(bf16[48,1280]{1,0:T(8,128)(2,1)S(1)} %get-tuple-element.216), channel_id=1, source_target_pairs={{0,2},{1,3},{2,0},{3,1},{4,6},{5,7},{6,4},{7,5},{8,10},{9,11},{10,... | collective-permute-start | bytes 368648 | tf_op jit(solution)/shard_map/ppermute | solution.py:96
  188.8 8.3 %collective-permute-start.9 = (bf16[48,1280]{1,0:T(8,128)(2,1)S(1)}, bf16[48,1280]{1,0:T(8,128)(2,1)S(1)}, u32[]{:S(2)}, u32[]{:S(2)}) collective-permute-start(bf16[48,1280]{1,0:T(8,128)(2,1)S(1)} %get-tuple-element.217), channel_id=1, source_target_pairs={{0,6},{1,7},{2,4},{3,5},{4,2},{5,3},{6,0},{7,1},{8,14},{9,15},{10,... | collective-permute-start | bytes 368648 | tf_op jit(solution)/shard_map/ppermute | solution.py:96
  190.2 8.3 %collective-permute-start.8 = (bf16[48,1280]{1,0:T(8,128)(2,1)S(1)}, bf16[48,1280]{1,0:T(8,128)(2,1)S(1)}, u32[]{:S(2)}, u32[]{:S(2)}) collective-permute-start(bf16[48,1280]{1,0:T(8,128)(2,1)S(1)} %get-tuple-element.218), channel_id=1, source_target_pairs={{0,4},{1,5},{2,6},{3,7},{4,0},{5,1},{6,2},{7,3},{8,12},{9,13},{10,... | collective-permute-start | bytes 368648 | tf_op jit(solution)/shard_map/ppermute | solution.py:96
  193.0 7.2 %collective-permute-start.21 = (bf16[192,384]{1,0:T(8,128)(2,1)S(1)}, bf16[192,384]{1,0:T(8,128)(2,1)S(1)}, u32[]{:S(2)}, u32[]{:S(2)}) collective-permute-start(bf16[192,384]{1,0:T(8,128)(2,1)S(1)} %get-tuple-element.211), channel_id=1, source_target_pairs={{0,2},{1,3},{2,0},{3,1},{4,6},{5,7},{6,4},{7,5},{8,10},{9,11},{10,... | collective-permute-start | bytes 442376 | tf_op jit(solution)/shard_map/ppermute | solution.py:96
  194.4 8.5 %collective-permute-start.23 = (bf16[192,384]{1,0:T(8,128)(2,1)S(1)}, bf16[192,384]{1,0:T(8,128)(2,1)S(1)}, u32[]{:S(2)}, u32[]{:S(2)}) collective-permute-start(bf16[192,384]{1,0:T(8,128)(2,1)S(1)} %get-tuple-element.212), channel_id=1, source_target_pairs={{0,6},{1,7},{2,4},{3,5},{4,2},{5,3},{6,0},{7,1},{8,14},{9,15},{10,... | collective-permute-start | bytes 442376 | tf_op jit(solution)/shard_map/ppermute | solution.py:96
  197.0 7.9 %collective-permute-start.22 = (bf16[192,384]{1,0:T(8,128)(2,1)S(1)}, bf16[192,384]{1,0:T(8,128)(2,1)S(1)}, u32[]{:S(2)}, u32[]{:S(2)}) collective-permute-start(bf16[192,384]{1,0:T(8,128)(2,1)S(1)} %get-tuple-element.213), channel_id=1, source_target_pairs={{0,4},{1,5},{2,6},{3,7},{4,0},{5,1},{6,2},{7,3},{8,12},{9,13},{10,... | collective-permute-start | bytes 442376 | tf_op jit(solution)/shard_map/ppermute | solution.py:96
  198.6 9.4 %collective-permute-start.12 = (bf16[48,1280]{1,0:T(8,128)(2,1)S(1)}, bf16[48,1280]{1,0:T(8,128)(2,1)S(1)}, u32[]{:S(2)}, u32[]{:S(2)}) collective-permute-start(bf16[48,1280]{1,0:T(8,128)(2,1)S(1)} %fusion.48), channel_id=1, source_target_pairs={{0,24},{8,16},{16,8},{24,0},{1,25},{9,17},{17,9},{25,1},{2,26},{10... | collective-permute-start | bytes 368648 | tf_op jit(solution)/shard_map/ppermute | solution.py:96
  200.2 14.8 %collective-permute-start.11 = (bf16[48,1280]{1,0:T(8,128)(2,1)S(1)}, bf16[48,1280]{1,0:T(8,128)(2,1)S(1)}, u32[]{:S(2)}, u32[]{:S(2)}) collective-permute-start(bf16[48,1280]{1,0:T(8,128)(2,1)S(1)} %fusion.48), channel_id=1, source_target_pairs={{0,16},{8,24},{16,0},{24,8},{1,17},{9,25},{17,1},{25,9},{2,18},{10... | collective-permute-start | bytes 368648 | tf_op jit(solution)/shard_map/ppermute | solution.py:96
  202.9 13.6 %collective-permute-start.10 = (bf16[48,1280]{1,0:T(8,128)(2,1)S(1)}, bf16[48,1280]{1,0:T(8,128)(2,1)S(1)}, u32[]{:S(2)}, u32[]{:S(2)}) collective-permute-start(bf16[48,1280]{1,0:T(8,128)(2,1)S(1)} %fusion.48), channel_id=1, source_target_pairs={{0,8},{8,0},{16,24},{24,16},{1,9},{9,1},{17,25},{25,17},{2,10},{10... | collective-permute-start | bytes 368648 | tf_op jit(solution)/shard_map/ppermute | solution.py:96
  205.0 14.7 %collective-permute-start.26 = (bf16[192,384]{1,0:T(8,128)(2,1)S(1)}, bf16[192,384]{1,0:T(8,128)(2,1)S(1)}, u32[]{:S(2)}, u32[]{:S(2)}) collective-permute-start(bf16[192,384]{1,0:T(8,128)(2,1)S(1)} %fusion.38), channel_id=1, source_target_pairs={{0,24},{8,16},{16,8},{24,0},{1,25},{9,17},{17,9},{25,1},{2,26},{10... | collective-permute-start | bytes 442376 | tf_op jit(solution)/shard_map/ppermute | solution.py:96
  205.1 17.2 %collective-permute-start.25 = (bf16[192,384]{1,0:T(8,128)(2,1)S(1)}, bf16[192,384]{1,0:T(8,128)(2,1)S(1)}, u32[]{:S(2)}, u32[]{:S(2)}) collective-permute-start(bf16[192,384]{1,0:T(8,128)(2,1)S(1)} %fusion.38), channel_id=1, source_target_pairs={{0,16},{8,24},{16,0},{24,8},{1,17},{9,25},{17,1},{25,9},{2,18},{10... | collective-permute-start | bytes 442376 | tf_op jit(solution)/shard_map/ppermute | solution.py:96
  207.9 14.4 %collective-permute-start.24 = (bf16[192,384]{1,0:T(8,128)(2,1)S(1)}, bf16[192,384]{1,0:T(8,128)(2,1)S(1)}, u32[]{:S(2)}, u32[]{:S(2)}) collective-permute-start(bf16[192,384]{1,0:T(8,128)(2,1)S(1)} %fusion.38), channel_id=1, source_target_pairs={{0,8},{8,0},{16,24},{24,16},{1,9},{9,1},{17,25},{25,17},{2,10},{10... | collective-permute-start | bytes 442376 | tf_op jit(solution)/shard_map/ppermute | solution.py:96
  215.0 7.5 %collective-permute-start.14 = (bf16[48,1920]{1,0:T(8,128)(2,1)S(1)}, bf16[48,1920]{1,0:T(8,128)(2,1)S(1)}, u32[]{:S(2)}, u32[]{:S(2)}) collective-permute-start(bf16[48,1920]{1,0:T(8,128)(2,1)S(1)} %get-tuple-element.208), channel_id=1, source_target_pairs={{0,2},{1,3},{2,0},{3,1},{4,6},{5,7},{6,4},{7,5},{8,10},{9,11},{10,... | collective-permute-start | bytes 552968 | tf_op jit(solution)/shard_map/ppermute | solution.py:96
  216.5 7.0 %collective-permute-start.16 = (bf16[48,1920]{1,0:T(8,128)(2,1)S(1)}, bf16[48,1920]{1,0:T(8,128)(2,1)S(1)}, u32[]{:S(2)}, u32[]{:S(2)}) collective-permute-start(bf16[48,1920]{1,0:T(8,128)(2,1)S(1)} %get-tuple-element.209), channel_id=1, source_target_pairs={{0,6},{1,7},{2,4},{3,5},{4,2},{5,3},{6,0},{7,1},{8,14},{9,15},{10,... | collective-permute-start | bytes 552968 | tf_op jit(solution)/shard_map/ppermute | solution.py:96
  219.7 5.7 %collective-permute-start.15 = (bf16[48,1920]{1,0:T(8,128)(2,1)S(1)}, bf16[48,1920]{1,0:T(8,128)(2,1)S(1)}, u32[]{:S(2)}, u32[]{:S(2)}) collective-permute-start(bf16[48,1920]{1,0:T(8,128)(2,1)S(1)} %get-tuple-element.210), channel_id=1, source_target_pairs={{0,4},{1,5},{2,6},{3,7},{4,0},{5,1},{6,2},{7,3},{8,12},{9,13},{10,... | collective-permute-start | bytes 552968 | tf_op jit(solution)/shard_map/ppermute | solution.py:96
  225.5 9.2 %collective-permute-start.19 = (bf16[48,1920]{1,0:T(8,128)(2,1)S(1)}, bf16[48,1920]{1,0:T(8,128)(2,1)S(1)}, u32[]{:S(2)}, u32[]{:S(2)}) collective-permute-start(bf16[48,1920]{1,0:T(8,128)(2,1)S(1)} %fusion.31), channel_id=1, source_target_pairs={{0,24},{8,16},{16,8},{24,0},{1,25},{9,17},{17,9},{25,1},{2,26},{10... | collective-permute-start | bytes 552968 | tf_op jit(solution)/shard_map/ppermute | solution.py:96
  229.1 15.0 %collective-permute-start.18 = (bf16[48,1920]{1,0:T(8,128)(2,1)S(1)}, bf16[48,1920]{1,0:T(8,128)(2,1)S(1)}, u32[]{:S(2)}, u32[]{:S(2)}) collective-permute-start(bf16[48,1920]{1,0:T(8,128)(2,1)S(1)} %fusion.31), channel_id=1, source_target_pairs={{0,16},{8,24},{16,0},{24,8},{1,17},{9,25},{17,1},{25,9},{2,18},{10... | collective-permute-start | bytes 552968 | tf_op jit(solution)/shard_map/ppermute | solution.py:96
  229.7 14.4 %collective-permute-start.17 = (bf16[48,1920]{1,0:T(8,128)(2,1)S(1)}, bf16[48,1920]{1,0:T(8,128)(2,1)S(1)}, u32[]{:S(2)}, u32[]{:S(2)}) collective-permute-start(bf16[48,1920]{1,0:T(8,128)(2,1)S(1)} %fusion.31), channel_id=1, source_target_pairs={{0,8},{8,0},{16,24},{24,16},{1,9},{9,1},{17,25},{25,17},{2,10},{10... | collective-permute-start | bytes 552968 | tf_op jit(solution)/shard_map/ppermute | solution.py:96
  244.8 80.0 %copy-start.33 = (f32[192,384]{1,0:T(8,128)S(1)}, f32[192,384]{1,0:T(8,128)}, u32[]{:S(2)}) copy-start(f32[192,384]{1,0:T(8,128)} %param.45) | copy-start | bytes 884740
  (85 other events, 1390.8 us)
Sparse Core Ops, SparseCore 0:
  15.1 34.9 all-gather.6
  52.6 24.7 all-gather.8

commit v2 on v1

v2 whole, which is shorter than its diff:
```python
import math

import jax
import jax.numpy as jnp
import numpy as np
from jax import lax
from jax.experimental import pallas as pl
from jax.experimental.pallas import tpu as pltpu
from jax.sharding import PartitionSpec as P

D = 384
HEADS = 6
HEAD_DIM = 64
FF = 1536
TFREQ = 256
GRID = 16
PIN = 16
POUT = 32
CLASSES = 1001
STEPS = 1000
TOK_IMG = 256

decay_rate = 0.5
clip_level = 1.0
step_rate = 0.5
grad_floor = 1e-30
norm_floor = 1e-06
f32 = jnp.float32
bf16 = jnp.bfloat16


def plan_table():
    s = np.arange(STEPS, dtype=np.float64)
    beta = 1e-4 + (0.02 - 1e-4) * s / (STEPS - 1)
    lbar = np.cumsum(np.log1p(-beta))
    lprev = np.concatenate([[0.0], lbar[:-1]])
    post = beta * -np.expm1(lprev) / -np.expm1(lbar)
    post[0] = post[1]
    remain = -np.expm1(lbar)
    coef = beta * beta / ((1.0 - beta) * remain)
    rows = [np.exp(0.5 * lbar), np.sqrt(remain), np.log(beta), np.log(post), coef]
    return np.stack(rows + [np.zeros(STEPS)] * 3, axis=1).astype(np.float32)


def time_table():
    half = TFREQ // 2
    freq = np.exp(np.float32(-math.log(10000.0)) * np.arange(half, dtype=np.float32) / np.float32(half)).astype(np.float32)
    angles = np.arange(STEPS, dtype=np.float32)[:, None] * freq[None, :]
    wide = angles.astype(np.float64)
    return np.concatenate([np.cos(wide), np.sin(wide)], axis=1).astype(np.float32)


def place_table():
    quarter = D // 4
    om = np.exp(np.float32(-math.log(10000.0)) * np.arange(quarter, dtype=np.float32) / np.float32(quarter)).astype(np.float32)
    n = np.arange(TOK_IMG)
    row = ((n // GRID).astype(np.float32)[:, None] * om[None, :]).astype(np.float64)
    col = ((n % GRID).astype(np.float32)[:, None] * om[None, :]).astype(np.float64)
    return np.concatenate([np.sin(row), np.cos(row), np.sin(col), np.cos(col)], axis=1).astype(np.float32)


def pick(index, count):
    return (index[:, None] == jnp.arange(count, dtype=jnp.int32)[None, :]).astype(bf16)


def silu_pair(v):
    s = 1.0 / (1.0 + jnp.exp(-v))
    return v * s, s * (1.0 + v * (1.0 - s))


def norm_parts(x):
    mean = jnp.mean(x, axis=-1, keepdims=True)
    cen = x - mean
    inv = lax.rsqrt(jnp.mean(cen * cen, axis=-1, keepdims=True) + norm_floor)
    return cen * inv, inv


def norm_back(d_norm, normed, inv):
    a = jnp.mean(d_norm, axis=-1, keepdims=True)
    b = jnp.mean(d_norm * normed, axis=-1, keepdims=True)
    return inv * (d_norm - a - normed * b)


def dot(a, b):
    return jnp.dot(a, b, preferred_element_type=f32)


def dot_nt(a, b):
    return lax.dot_general(a, b, (((1,), (1,)), ((), ())), preferred_element_type=f32)


def dot_tn(a, b):
    return lax.dot_general(a, b, (((0,), (0,)), ((), ())), preferred_element_type=f32)


def flip(x, bit, axis="fsdp"):
    size = lax.axis_size(axis)
    return lax.ppermute(x, axis, [(i, i ^ bit) for i in range(size)])


def rep_gather(x):
    size = lax.axis_size("rep")
    me = lax.axis_index("rep")
    parts = jnp.stack([x] + [flip(x, k, "rep") for k in range(1, size)])
    return jnp.stack([lax.dynamic_index_in_dim(parts, me ^ j, 0, keepdims=False) for j in range(size)])


def rep_sum(x16):
    size = lax.axis_size("rep")
    parts = [x16.astype(f32)] + [flip(x16, k, "rep").astype(f32) for k in range(1, size)]
    while len(parts) > 1:
        parts = [parts[i] + parts[i + 1] for i in range(0, len(parts), 2)]
    return parts[0]


def sum_scatter(grad):
    return lax.psum_scatter(grad, "fsdp", scatter_dimension=0, tiled=True)


def gather_rows(x):
    return lax.all_gather(x, "fsdp", axis=0, tiled=True)


def lane_half(shape, which):
    lane = lax.broadcasted_iota(jnp.int32, shape, 1)
    return (lane < HEAD_DIM) if which == 0 else (lane >= HEAD_DIM)


FLOPS_US = 1_150_000_000


def kernel_call(body, outs, operands, micros, scratch=(), places=None, after=(), room=16):
    vmem = pl.BlockSpec(memory_space=pltpu.VMEM)
    smem = pl.BlockSpec(memory_space=pltpu.SMEM)
    places = places or "v" * len(operands)
    count = len(operands)

    def run(*refs):
        body(*refs[:count], *refs[count + len(after) :])

    return pl.pallas_call(
        run,
        out_shape=[jax.ShapeDtypeStruct(s, t) for s, t in outs],
        in_specs=[{"s": smem, "v": vmem, "h": pl.BlockSpec(memory_space=pltpu.HBM)}[p] for p in places] + [pl.BlockSpec(memory_space=pl.ANY)] * len(after),
        out_specs=[vmem] * len(outs),
        scratch_shapes=list(scratch),
        compiler_params=pltpu.CompilerParams(vmem_limit_bytes=room * 2**20),
        cost_estimate=pl.CostEstimate(flops=int(micros * FLOPS_US), bytes_accessed=1_000_000, transcendentals=0),
    )(*operands, *after)


HEAD = PIN + POUT
CAST_ROOM = 48
INFO = 80
BUNDLE = 96
TAIL = 3 * D + 128
SENT = TAIL + D + 2 * FF


def piece_owner(at, n):
    return jnp.bitwise_xor(at[0], 2 * (n % 4) + n // 4)


def attention_forward(tsteps, lat, noi, plan, grid, weights, shares, place, after=()):
    images = lat.shape[0]
    fast = len(weights) == 8

    def body(ts, at, lat_r, noi_r, plan_r, grid_r, share_r, *refs):
        if fast:
            wq_r, head_r, head_s = refs[8], refs[9], refs[-1]
            for n in range(8):
                owner = piece_owner(at, n)
                rows = pl.ds(pl.multiple_of(owner * 48, 48), 48)
                wq_r[rows, :] = refs[n][:, 0 : 3 * D]
                head_s[owner] = refs[n][:, 3 * D : 3 * D + 48]
            for p in range(8):
                head_r[:, p * 48 : (p + 1) * 48] = head_s[p]
            refs = refs[10:-1]
        else:
            wq_r, head_r = refs[:2]
            refs = refs[2:]
        mod_r, con_r, noisy_r, h0_r, attn_r, qkv_r, total_r, mix_r = refs
        total = share_r[0]
        for p in range(1, share_r.shape[0]):
            total = total + share_r[p]
        width = total.shape[1]
        for n in range(8):
            i, col = divmod(n * width, 8 * D)
            mod_r[i : i + 1, col : col + width] = total[n : n + 1]
        for i in range(images):
            row = plan_r[pl.ds(ts[i], 1), :]
            con_r[i : i + 1, :] = row
            noisy = (row[:, 0:1] * lat_r[i] + row[:, 1:2] * noi_r[i]).astype(bf16)
            noisy_r[i] = noisy
            h0 = dot_tn(noisy, head_r[0:PIN, :]) + grid_r[...]
            h0_r[i] = h0
            norm, _ = norm_parts(h0)
            attn = (norm * (1.0 + mod_r[i : i + 1, D : 2 * D]) + mod_r[i : i + 1, 0:D]).astype(bf16)
            attn_r[i] = attn
            for part in range(3):
                qkv_r[i, :, part * D : (part + 1) * D] = dot(attn, wq_r[:, part * D : (part + 1) * D]).astype(bf16)
        lane = lax.broadcasted_iota(jnp.int32, (TOK_IMG, 128), 1)
        logs = [jnp.zeros((TOK_IMG, 128), f32)] * images
        for pair in range(HEADS // 2):
            for i in range(images):
                q = qkv_r[i, :, pair * 128 : pair * 128 + 128]
                k = qkv_r[i, :, D + pair * 128 : D + pair * 128 + 128]
                v = qkv_r[i, :, 2 * D + pair * 128 : 2 * D + pair * 128 + 128]
                mixed = None
                for half in range(2):
                    own = lane_half(q.shape, half)
                    zero = jnp.zeros_like(q)
                    s = dot_nt(jnp.where(own, q, zero), k) * 0.125
                    top = jnp.max(s, axis=-1, keepdims=True)
                    p = jnp.exp(s - top)
                    total = jnp.sum(p, axis=-1, keepdims=True)
                    p = p * (1.0 / total)
                    logs[i] = jnp.where(lane == pair * 2 + half, top + jnp.log(total), logs[i])
                    o = dot(p.astype(bf16), jnp.where(own, v, zero))
                    mixed = o if mixed is None else mixed + o
                mix_r[i, :, pair * 128 : pair * 128 + 128] = mixed.astype(bf16)
        for i in range(images):
            total_r[i] = logs[i]

    outs = [
        ((images, 8 * D), f32),
        ((images, 8), f32),
        ((images, PIN, TOK_IMG), bf16),
        ((images, TOK_IMG, D), f32),
        ((images, TOK_IMG, D), bf16),
        ((images, TOK_IMG, 3 * D), bf16),
        ((images, TOK_IMG, 128), f32),
        ((images, TOK_IMG, D), bf16),
    ]
    scratch = []
    if fast:
        outs = [((D, 3 * D), bf16), ((HEAD, D), bf16)] + outs
        scratch = [pltpu.VMEM((8, HEAD, 48), bf16)]
    ops = (tsteps, place, lat, noi, plan, grid, shares, *weights)
    return kernel_call(
        body, outs, ops, 8, scratch=scratch, places="ss" + "v" * (len(ops) - 2), after=after
    )


BLOCK = 384


def mlp_pass(noi, con, mod, h0_all, mix_all, head, weights, place, after=()):
    images = noi.shape[0]
    bend_scale = math.sqrt(2.0 / math.pi)
    share = 1.0 / (TOK_IMG * PIN)

    fast = len(weights) == 8

    def body(at, noi_r, con_r, mod_r, h0_r, mix_r, head_r, *refs):
        if fast:
            wp_r, w1_r, w2_r = refs[-3:]
            for n in range(8):
                owner = piece_owner(at, n)
                rows = pl.ds(pl.multiple_of(owner * 48, 48), 48)
                wp_r[rows, :] = refs[n][:, TAIL : TAIL + D]
                w1_r[rows, :] = refs[n][:, TAIL + D : TAIL + D + FF]
                for b in range(4):
                    w2_r[pl.ds(pl.multiple_of(owner * 192 + b * 48, 48), 48), :] = refs[n][:, TAIL + D + FF + b * D : TAIL + D + FF + (b + 1) * D]
            refs = refs[8:-3]
        else:
            wp_r, w1_r, w2_r = refs[:3]
            refs = refs[3:]
        g_refs, refs = refs[: 2 if fast else 3], refs[2 if fast else 3 :]
        glast_r, dmix_r, dh1_r, dmod_r, loss_r, mlp_r, act_r, dinner_r, douter_r, dbr_r, slope_r = refs
        g_last = None
        wo = head_r[PIN:HEAD, :]
        losses = jnp.zeros((1, 1), f32)
        dmod_r[:, 0 : 2 * D] = jnp.zeros((images, 2 * D), f32)
        for i in range(images):
            def m(slot):
                return mod_r[i : i + 1, slot * D : (slot + 1) * D]

            def put(slot, value):
                dmod_r[i : i + 1, slot * D : (slot + 1) * D] = jnp.sum(value, axis=0, keepdims=True)

            branch = dot(mix_r[i], wp_r[...])
            h1 = h0_r[i] + m(2) * branch
            norm1, inv1 = norm_parts(h1)
            mlp = (norm1 * (1.0 + m(4)) + m(3)).astype(bf16)
            tokens = slice(i * TOK_IMG, (i + 1) * TOK_IMG)
            mlp_r[tokens, :] = mlp
            outer = None
            for b in range(FF // BLOCK):
                cols = slice(b * BLOCK, (b + 1) * BLOCK)
                x = dot(mlp, w1_r[:, cols])
                sq = x * x
                t = jnp.tanh(bend_scale * x * (1.0 + 0.044715 * sq))
                hx = 0.5 * x
                act = (hx * (1.0 + t)).astype(bf16)
                act_r[tokens, cols] = act
                slope_r[:, cols] = 0.5 * (1.0 + t) + hx * (1.0 - t * t) * (bend_scale + (3 * 0.044715 * bend_scale) * sq)
                part = dot(act, w2_r[cols, :])
                outer = part if outer is None else outer + part
            h2 = h1 + m(5) * outer
            norm2, inv2 = norm_parts(h2)
            fin = (norm2 * (1.0 + m(7)) + m(6)).astype(bf16)
            out = dot_nt(wo, fin)
            log_beta, post_log, coef = (con_r[i : i + 1, n : n + 1] for n in (2, 3, 4))
            miss = out[:PIN] - noi_r[i]
            mixing = (out[PIN:] + 1.0) * 0.5
            log_var = mixing * log_beta + (1.0 - mixing) * post_log
            ratio = jnp.exp(post_log - log_var)
            square = miss * miss
            weigh = coef * jnp.exp(-log_var)
            terms = square + 0.5 * (-1.0 + log_var - post_log + ratio + weigh * square)
            losses += share * jnp.sum(jnp.sum(terms, axis=0, keepdims=True), axis=1, keepdims=True)
            d_guess = share * miss * (2.0 + weigh)
            d_mixed = (share * 0.25) * (1.0 - ratio - weigh * square) * (log_beta - post_log)
            d_out = jnp.concatenate([d_guess, d_mixed], axis=0).astype(bf16)
            piece = dot(d_out, fin)
            g_last = piece if g_last is None else g_last + piece
            d_fin = dot_tn(d_out, wo)
            put(6, d_fin)
            put(7, d_fin * norm2)
            d_h2 = norm_back(d_fin * (1.0 + m(7)), norm2, inv2)
            put(5, d_h2 * outer)
            d_outer = (m(5) * d_h2).astype(bf16)
            douter_r[tokens, :] = d_outer
            d_mlp = None
            for b in range(FF // BLOCK):
                cols = slice(b * BLOCK, (b + 1) * BLOCK)
                d_in = (dot_nt(d_outer, w2_r[cols, :]) * slope_r[:, cols]).astype(bf16)
                dinner_r[tokens, cols] = d_in
                part = dot_nt(d_in, w1_r[:, cols])
                d_mlp = part if d_mlp is None else d_mlp + part
            put(3, d_mlp)
            put(4, d_mlp * norm1)
            d_h1 = d_h2 + norm_back(d_mlp * (1.0 + m(4)), norm1, inv1)
            dh1_r[i] = d_h1
            put(2, d_h1 * branch)
            d_br = (m(2) * d_h1).astype(bf16)
            dbr_r[tokens, :] = d_br
            dmix_r[i] = dot_nt(d_br, wp_r[...]).astype(bf16)
        loss_r[...] = jnp.broadcast_to(losses, loss_r.shape)
        glast_r[...] = g_last
        mix = jnp.concatenate([mix_r[i] for i in range(images)], axis=0)
        if not fast:
            g_refs[0][...] = dot_tn(mix, dbr_r[...])
        else:
            deal_rows(*g_refs, dot_tn(mix, dbr_r[...]), at[1], 0)
        for b in range(FF // BLOCK):
            cols = slice(b * BLOCK, (b + 1) * BLOCK)
            g_in = dot_tn(mlp_r[...], dinner_r[:, cols])
            g_out = dot_tn(act_r[:, cols], douter_r[...])
            if not fast:
                g_refs[1][:, cols] = g_in
                g_refs[2][cols, :] = g_out
                continue
            deal_rows(*g_refs, g_in, at[1], D + b * BLOCK)
            deal(*g_refs, g_out[0:192], g_out[192:384], at[1], b, D + FF, 4)

    if fast:
        outs = [((4, 48, D + 2 * FF), f32), ((4, 48, D + 2 * FF), bf16)]
    else:
        outs = [((D, D), f32), ((D, FF), f32), ((FF, D), f32)]
    outs += [
        ((POUT, D), f32),
        ((images, TOK_IMG, D), bf16),
        ((images, TOK_IMG, D), f32),
        ((images, 8 * D), f32),
        ((8, 128), f32),
    ]
    ops = (place, noi, con, mod, h0_all, mix_all, head, *weights)
    many = images * TOK_IMG
    scratch = [pltpu.VMEM((many, n), bf16) for n in (D, FF, FF, D, D)] + [pltpu.VMEM((TOK_IMG, FF), f32)]
    if fast:
        scratch += [pltpu.VMEM(shape, bf16) for shape in ((D, D), (D, FF), (FF, D))]
    return kernel_call(body, outs, ops, 13, scratch=scratch, places="s" + "v" * (len(ops) - 1), after=after, room=32)


def deal(keep_r, send_r, left, right, core, chip, lanes, blocks=1):
    rows, width = left.shape[0] // blocks, left.shape[1]
    kept = jnp.where(core == 0, left, right)
    sent = jnp.where(core == 0, right, left).astype(bf16)
    for b in range(blocks):
        cols = slice(lanes + b * width, lanes + (b + 1) * width)
        keep_r[chip, :, cols] = kept[b * rows : (b + 1) * rows]
        send_r[chip, :, cols] = sent[b * rows : (b + 1) * rows]


def deal_rows(keep_r, send_r, grad, core, lanes):
    for c in range(4):
        deal(keep_r, send_r, grad[c * 96 : c * 96 + 48], grad[c * 96 + 48 : c * 96 + 96], core, c, lanes)


MOD_ROWS, MOD_LANES = 16, 512


def attention_back(mod, h0_all, qkv_all, total_all, dmix_all, dh1_all, dmod_all, w_qkv, loss_tile, info, after=()):
    images = mod.shape[0]

    def body(mod_r, h0_r, qkv_r, total_r, dmix_r, dh1_r, dmod_in, wq_r, loss_r, *refs):
        dqkv_r, dmod_r, dh0_r, line = refs[-4:]
        for pair in range(HEADS // 2):
            at = slice(pair * 128, pair * 128 + 128)
            for i in range(images):
                q = qkv_r[i, :, pair * 128 : pair * 128 + 128]
                k = qkv_r[i, :, D + pair * 128 : D + pair * 128 + 128]
                v = qkv_r[i, :, 2 * D + pair * 128 : 2 * D + pair * 128 + 128]
                do = dmix_r[i, :, at]
                dq = dk = dv = None
                for half in range(2):
                    own = lane_half(q.shape, half)
                    zero = jnp.zeros_like(q)
                    do_h = jnp.where(own, do, zero)
                    q_h = jnp.where(own, q, zero)
                    head = pair * 2 + half
                    p = jnp.exp(dot_nt(q_h, k) * 0.125 - total_r[i, :, head : head + 1])
                    dp = dot_nt(do_h, v)
                    ds = (p * (dp - jnp.sum(dp * p, axis=-1, keepdims=True))).astype(bf16)
                    a = dot(ds, jnp.where(own, k, zero))
                    b = dot_tn(ds, q_h)
                    c = dot_tn(p.astype(bf16), do_h)
                    dq, dk, dv = (a, b, c) if dq is None else (dq + a, dk + b, dv + c)
                rows = slice(i * TOK_IMG, (i + 1) * TOK_IMG)
                for part, value in enumerate((dq * 0.125, dk * 0.125, dv)):
                    dqkv_r[rows, part * D + pair * 128 : part * D + pair * 128 + 128] = value.astype(bf16)
        for i in range(images):
            rows = slice(i * TOK_IMG, (i + 1) * TOK_IMG)
            d_attn = None
            for part in range(3):
                cols = slice(part * D, (part + 1) * D)
                piece = dot_nt(dqkv_r[rows, cols], wq_r[:, cols])
                d_attn = piece if d_attn is None else d_attn + piece
            norm, inv = norm_parts(h0_r[i])
            line[i : i + 1, 0:D] = jnp.sum(d_attn, axis=0, keepdims=True)
            line[i : i + 1, D : 2 * D] = jnp.sum(d_attn * norm, axis=0, keepdims=True)
            line[i : i + 1, 2 * D :] = dmod_in[i : i + 1, 2 * D :]
            dh0_r[i] = (dh1_r[i] + norm_back(d_attn * (1.0 + mod_r[i : i + 1, D : 2 * D]), norm, inv)).astype(bf16)
        if info is not None:
            each = 8 * D // MOD_LANES
            block = [line[i : i + 1, n * MOD_LANES : (n + 1) * MOD_LANES] for i in range(images) for n in range(each)]
            lane = lax.broadcasted_iota(jnp.int32, (1, MOD_LANES), 1)
            loss = loss_r[0:1, 0:1]
            high = loss.astype(bf16).astype(f32)
            mid = (loss - high).astype(bf16).astype(f32)
            low = loss - high - mid
            block.append(jnp.where(lane == 0, high, jnp.where(lane == 1, mid, jnp.where(lane == 2, low, 0.0))))
            told = refs[0][INFO:BUNDLE, :].astype(f32)[0:1]
            block.append(jnp.concatenate([told, jnp.zeros((1, MOD_LANES - D), f32)], axis=1))
            block.append(jnp.zeros((MOD_ROWS - len(block), MOD_LANES), f32))
            dmod_r[...] = jnp.concatenate(block, axis=0).astype(bf16)
        else:
            dmod_r[...] = line[...].astype(bf16)

    outs = [((images * TOK_IMG, 3 * D), bf16)]
    outs += [((images, 8 * D) if info is None else (MOD_ROWS, MOD_LANES), bf16), ((images, TOK_IMG, D), bf16)]
    ops = (mod, h0_all, qkv_all, total_all, dmix_all, dh1_all, dmod_all, w_qkv, loss_tile)
    if info is not None:
        ops += (info,)
    return kernel_call(body, outs, ops, 7, scratch=[pltpu.VMEM((images, 8 * D), f32)], after=after)


def tail_grad(attn_all, dqkv, noisy_all, dh0_all, g_last, place, fast, after=()):
    images = noisy_all.shape[0]

    def body(at, attn_r, dqkv_r, noisy_r, dh0_r, last_r, *refs):
        for part in range(3):
            cols = slice(part * D, (part + 1) * D)
            grad = dot_tn(attn_r[...], dqkv_r[:, cols])
            if fast:
                deal_rows(*refs[:2], grad, at[1], part * D)
            else:
                refs[0][:, cols] = grad
        patch = None
        for i in range(images):
            piece = dot(noisy_r[i], dh0_r[i])
            patch = piece if patch is None else patch + piece
        head = jnp.concatenate([patch, last_r[...]], axis=0)
        if not fast:
            refs[1][...] = head
            return
        none = jnp.zeros((HEAD, 128 - 48), f32)
        for c in range(4):
            left = jnp.concatenate([head[:, c * 96 : c * 96 + 48], none], axis=1)
            right = jnp.concatenate([head[:, c * 96 + 48 : c * 96 + 96], none], axis=1)
            deal(*refs[:2], left, right, at[1], c, 3 * D)

    outs = [((4, 48, TAIL), f32), ((4, 48, TAIL), bf16)] if fast else [((D, 3 * D), f32), ((HEAD, D), f32)]
    ops = (place, attn_all.reshape(-1, D), dqkv, noisy_all, dh0_all, g_last)
    return kernel_call(body, outs, ops, 2, places="s" + "v" * 5, after=after)


def bundle_rows(tsteps, labels, time1_w, time2_w):
    images = tsteps.shape[0]

    def body(ts_h, lab_h, t1_h, t2_h, out_r, ts, lab, t1_r, t2_r, sems):
        copies = [
            pltpu.make_async_copy(a, b, sems.at[n])
            for n, (a, b) in enumerate(((ts_h, ts), (lab_h, lab), (t1_h, t1_r), (t2_h, t2_r)))
        ]
        for copy in copies:
            copy.start()
        for copy in copies:
            copy.wait()
        rows = t1_r.shape[0]
        out_r[0:rows, :] = t1_r[...].astype(bf16)
        out_r[rows:INFO, :] = t2_r[...].astype(bf16)
        lane = lax.broadcasted_iota(jnp.int32, (BUNDLE - INFO, D), 1)
        info = jnp.zeros((BUNDLE - INFO, D), jnp.int32)
        for i in range(images):
            for n, value in enumerate((ts[i] // 32, ts[i] % 32, lab[i] // 32, lab[i] % 32)):
                info = jnp.where(lane == n * images + i, value, info)
        out_r[INFO:BUNDLE, :] = info.astype(f32).astype(bf16)

    ops = (tsteps, labels, time1_w, time2_w)
    scratch = [pltpu.SMEM((images,), jnp.int32)] * 2 + [pltpu.VMEM(a.shape, f32) for a in ops[2:]] + [pltpu.SemaphoreType.DMA((4,))]
    return kernel_call(body, [((BUNDLE, D), bf16)], ops, 1.5, places="hhhh", scratch=scratch)[0]


def cast_weights(patch_state, out_t, time1_w, time2_w, table_t, mod_w, qkv_w, proj_w, fc1_w, fc2_w, after=()):
    def body(pa, ou, t1, t2, ta, mo, qk, pr, f1, f2, w_r, mod16, tab16, sums):
        w_r[:, 0 : 3 * D] = qk[...].astype(bf16)
        head = jnp.concatenate([pa[0], ou[0]], axis=0)
        w_r[:, 3 * D : TAIL] = jnp.concatenate([head, jnp.zeros((HEAD, 128 - 48), f32)], axis=1).astype(bf16)
        w_r[:, TAIL : TAIL + D] = pr[...].astype(bf16)
        w_r[:, TAIL + D : TAIL + D + FF] = f1[...].astype(bf16)
        for b in range(4):
            w_r[:, TAIL + D + FF + b * D : TAIL + D + FF + (b + 1) * D] = f2[b * 48 : (b + 1) * 48, :].astype(bf16)
        mod16[...] = mo[...].astype(bf16)
        tab16[...] = ta[...].astype(bf16)
        lane = lax.broadcasted_iota(jnp.int32, (8, D), 1)
        line = jnp.zeros((8, D), f32)
        for n, m in enumerate((pa[0], t1[...], t2[...], ta[...], mo[...], qk[...], pr[...], f1[...], f2[...], ou[0])):
            line = jnp.where(lane == n, jnp.sum(jnp.sum(m * m, axis=0, keepdims=True), axis=1, keepdims=True), line)
        sums[...] = line

    outs = [((48, SENT), bf16), (mod_w.shape, bf16), (table_t.shape, bf16), ((8, D), f32)]
    ops = (patch_state, out_t, time1_w, time2_w, table_t, mod_w, qkv_w, proj_w, fc1_w, fc2_w)
    return kernel_call(body, outs, ops, 2.5, after=after, room=CAST_ROOM)


def picked(index, count):
    lane = lax.broadcasted_iota(jnp.int32, (index.shape[0], count), 1)
    return (lane == index).astype(f32).astype(bf16)


def one_hot(shape, test):
    row, col = lax.broadcasted_iota(jnp.int32, shape, 0), lax.broadcasted_iota(jnp.int32, shape, 1)
    return test(row, col).astype(f32).astype(bf16)


def condition_body(infos, images, w1, w2, times_r, tab_r, position):
    own_d = tab_r.shape[0]
    ts, lab = [], []
    for i in range(images):
        for whole in infos:
            ts.append((whole[:, i : i + 1] * 32.0 + whole[:, images + i : images + i + 1]).astype(jnp.int32))
            lab.append((whole[:, 2 * images + i : 2 * images + i + 1] * 32.0 + whole[:, 3 * images + i : 3 * images + i + 1]).astype(jnp.int32))
    ts, lab = jnp.concatenate(ts, axis=0), jnp.concatenate(lab, axis=0)
    feats = dot(picked(ts, STEPS), times_r[...]).astype(bf16)
    act, time_slope = silu_pair(dot(feats, w1))
    act = act.astype(bf16)
    own = one_hot((D, own_d), lambda r, c: r == c + position * own_d)
    emb = dot(act, dot(w2, own).astype(bf16))
    picks = picked(lab, CLASSES)
    cond, cond_slope = silu_pair(emb + dot_nt(picks, tab_r[...]))
    return feats, act, time_slope, picks, cond.astype(bf16), cond_slope, own


def modulation_shares(place, pieces, times, tab16, mod16, images):
    parts = 8
    width = images * D

    def body(at, *refs):
        times_r, tab_r, mod_r, out_r, w1_r, w2_r, info_r = refs[8:]
        for n in range(8):
            owner = piece_owner(at, n)
            w1_r[pl.ds(pl.multiple_of(owner * 32, 32), 32), :] = refs[n][0:32, :]
            w2_r[pl.ds(pl.multiple_of(owner * 48, 48), 48), :] = refs[n][32:INFO, :]
            info_r[pl.ds(owner, 1), :] = refs[n][INFO:BUNDLE, 0:128].astype(f32)[0:1]
        cond = condition_body([info_r[...]], images, w1_r[...], w2_r[...], times_r, tab_r, at[0])[4]
        for s in range(8):
            i, col = divmod(s * width, 8 * D)
            value = dot(cond[i * parts : (i + 1) * parts], mod_r[:, col : col + width])
            for p in range(parts):
                out_r[p, s : s + 1, :] = value[p : p + 1]

    outs = [((parts, 8, width), f32), ((TFREQ, D), bf16), ((D, D), bf16)]
    ops = (place, *pieces, times, tab16, mod16)
    return kernel_call(body, outs, ops, 3, places="s" + "v" * 11, scratch=[pltpu.VMEM((parts, 128), f32)])


def condition_back(place, own_mod, oth_mod, w1, w2, times, tab16, mod16, reps, parts, images):
    groups = own_mod.shape[0]
    devices = 2 * groups
    count = devices * images
    own_t, own_d = TFREQ // parts, D // parts
    each = 8 * D // MOD_LANES

    def body(at, own_r, oth_r, w1_r, w2_r, times_r, tab_r, mod_r, gm_r, gt_r, dc_r, loss_r, feat_r, act_r, slope_r, all_s, dmod_s):
        for g in range(groups):
            mine = pl.multiple_of((2 * g + at[1]) * MOD_ROWS, MOD_ROWS)
            its = pl.multiple_of((2 * g + 1 - at[1]) * MOD_ROWS, MOD_ROWS)
            all_s[pl.ds(mine, MOD_ROWS), :] = own_r[g]
            all_s[pl.ds(its, MOD_ROWS), :] = oth_r[g]
        rows = all_s[...]
        take = one_hot((devices, devices * MOD_ROWS), lambda r, c: c == r * MOD_ROWS + images * each + 1)
        infos = dot(take, rows)
        feats, act, time_slope, picks, cond, cond_slope, own = condition_body([infos], images, w1_r[...], w2_r[...], times_r, tab_r, at[0])
        near = one_hot((TFREQ, own_t), lambda r, c: r == c + at[0] * own_t)
        feat_r[...] = dot(feats, near).astype(bf16)
        act_r[...] = dot(act, own).astype(bf16)
        slope_r[...] = time_slope
        for n in range(each):
            take = one_hot((count, devices * MOD_ROWS), lambda r, c: c == (r % devices) * MOD_ROWS + (r // devices) * each + n)
            dmod_s[:, n * MOD_LANES : (n + 1) * MOD_LANES] = dot(take, rows).astype(bf16)
        take = one_hot((8, devices * MOD_ROWS), lambda r, c: c % MOD_ROWS == images * each)
        loss = dot(take, rows)
        loss_r[...] = jnp.broadcast_to(loss[:, 0:1] + loss[:, 1:2] + loss[:, 2:3], loss_r.shape)
        d_mod = dmod_s[...]
        d_cond = dot_nt(d_mod, mod_r[...]) * cond_slope
        wide = jnp.concatenate([d_cond, jnp.zeros((count, 128 - own_d), f32)], axis=1).astype(bf16)
        for p in range(parts):
            dc_r[p] = wide
        gm_r[...] = dot_tn(cond, d_mod)
        high = d_cond.astype(bf16)
        rest = d_cond - high.astype(f32)
        mid = rest.astype(bf16)
        low = (rest - mid.astype(f32)).astype(bf16)
        gt_r[...] = dot_tn(high, picks) + (dot_tn(mid, picks) + dot_tn(low, picks))

    outs = [((own_d, 8 * D), f32), ((own_d, CLASSES), f32), ((parts, count, 128), bf16), ((8, 128), f32)]
    outs += [((count, own_t), bf16), ((count, own_d), bf16), ((count, D), f32)]
    ops = (place, own_mod, oth_mod, w1, w2, times, tab16, mod16)
    scratch = [pltpu.VMEM((devices * MOD_ROWS, MOD_LANES), bf16), pltpu.VMEM((count, 8 * D), bf16)]
    return kernel_call(body, outs, ops, 4, scratch=scratch, places="s" + "v" * 7)


def time_back(d_time, w2, act16, slope, feat16):
    parts, own_d = d_time.shape[0], act16.shape[1]
    own_t = TFREQ // parts

    def body(dt_r, w2_r, act_r, slope_r, feat_r, g1_r, g2_r):
        d_all = jnp.concatenate([dt_r[p, :, 0:own_d].astype(f32) for p in range(parts)], axis=1).astype(bf16)
        g2_r[...] = dot_tn(act_r[...], d_all)
        d_hid = (dot_nt(d_all, w2_r[...]) * slope_r[...]).astype(bf16)
        g1_r[...] = dot_tn(feat_r[...], d_hid)

    outs = [((own_t, D), f32), ((own_d, D), f32)]
    return kernel_call(body, outs, (d_time, w2, act16, slope, feat16), 2)


FAR = {"time1": (0, 1), "time2": (1, 1), "mod": (2, 8), "qkv": (10, 3), "proj": (13, 1), "fc1": (14, 4), "fc2": (18, 1), "table": (26, 3)}
NEAR = {"time1": 19, "time2": 20, "mod": 21, "qkv": 22, "proj": 23, "fc1": 24, "fc2": 25, "table": 29}
SUMS, LINES = 30, 32
ORDER = ("time1", "time2", "table", "mod", "qkv", "proj", "fc1", "fc2")


def lanes_of(rows_by_cols):
    ones = jnp.ones((8, rows_by_cols.shape[1]), f32)
    return lax.dot_general(ones, rows_by_cols, (((1,), (1,)), ((), ())), precision=lax.Precision.HIGHEST, preferred_element_type=f32)[0:1]


def put_sums(pack, name, g):
    sq = g * g + grad_floor
    line, count = FAR[name]
    col = jnp.sum(sq, axis=0, keepdims=True)
    for n in range(count):
        size = min(D, g.shape[1] - n * D)
        pack[line + n : line + n + 1, 0:size] = col[:, n * D : n * D + size]
    pack[NEAR[name] : NEAR[name] + 1, 0 : g.shape[0]] = lanes_of(sq)


def copies_sum(refs):
    a, b, c, d = (r[...].astype(f32) for r in refs)
    return (a + b) + (c + d)


def sums_early(place, parts):
    def body(at, a, b, c, d, gm, gf, pack, cuts):
        for n, part in enumerate((a, b, c, d)):
            cuts[jnp.bitwise_xor(at[2], n)] = part[...].astype(f32)
        pack[...] = jnp.zeros((LINES, D), f32)
        gm[:, 0:D] = jnp.concatenate([cuts[j][:, 768 : 768 + 96] for j in range(4)], axis=1)
        for j in range(4):
            gm[:, D + j * 384 : D + (j + 1) * 384] = cuts[j][:, 0:384]
            gf[j * 48 : (j + 1) * 48, :] = cuts[j][:, 384:768]
        put_sums(pack, "proj", gm[:, 0:D])
        put_sums(pack, "fc1", gm[:, D : D + FF])
        put_sums(pack, "fc2", gf[...])

    outs = [((48, D + FF), f32), ((192, D), f32), ((LINES, D), f32)]
    return kernel_call(body, outs, (place, *parts), 2, scratch=[pltpu.VMEM((4, 48, Z_LANES), f32)], places="svvvv")


def sums_middle(pack, g_table, g_mod, sums, loss, after=()):
    def body(old, tab, mod, sums_r, loss_r, pack_r):
        pack_r[...] = old[...]
        put_sums(pack_r, "mod", mod[...])
        put_sums(pack_r, "table", tab[...])
        lane = lax.broadcasted_iota(jnp.int32, (1, D), 1)
        pack_r[SUMS : SUMS + 1, :] = jnp.where(lane == 10, loss_r[0:1, 0:1], sums_r[0:1, :])

    return kernel_call(body, [((LINES, D), f32)], (pack, g_table, g_mod, sums, loss), 2, after=after)[0]


def sums_late(pack, tail, g_time1, g_time2):
    def body(old, q0, q1, q2, q3, t1, t2, gq, pack_r):
        pack_r[...] = old[...]
        gq[...] = copies_sum((q0, q1, q2, q3))
        put_sums(pack_r, "qkv", gq[:, 0 : 3 * D])
        put_sums(pack_r, "time1", t1[...])
        put_sums(pack_r, "time2", t2[...])

    outs = [(tail[0].shape, f32), ((LINES, D), f32)]
    return kernel_call(body, outs, (pack, *tail, g_time1, g_time2), 2)


def scaled_updates(place, packs, g_time1, g_time2, g_table, g_mod, gq, gm, gf, olds, patch_state, out_t):
    parts = packs.shape[0]
    shapes = [(g_time1.shape), g_time2.shape, g_table.shape, g_mod.shape, (48, 3 * D), (48, D), (48, FF), gf.shape]

    def body(at, pk, t1, t2, tab, mod, q, m, f, *refs):
        old_rs, (pat, ost), fresh_rs, u_rs = refs[0:8], refs[8:10], refs[10:18], refs[18:26]
        u_pat, u_out, m_pat, m_out, usq, head, line_s = refs[26:]
        total = jnp.sum(pk[...], axis=0)
        lane = lax.broadcasted_iota(jnp.int32, (1, D), 1)
        grads = (t1[...], t2[...], tab[...], mod[...], q[:, 0 : 3 * D], m[:, 0:D], m[:, D : D + FF], f[...])
        sizes = []

        def size_of(u):
            return jnp.sum(jnp.sum(u * u, axis=0, keepdims=True), axis=1, keepdims=True)

        for name, g, old_r, fresh_r, u_r in zip(ORDER, grads, old_rs, fresh_rs, u_rs):
            rows, cols = g.shape
            many = rows * parts
            line, count = FAR[name]
            far_at, near_at = (0, cols) if name == "table" else (many, 0)
            for p in range(parts):
                line_s[:, near_at + p * rows : near_at + (p + 1) * rows] = pk[p, NEAR[name] : NEAR[name] + 1, 0:rows] / cols
            for n in range(count):
                wide = min(D, cols - n * D)
                line_s[:, far_at + n * D : far_at + n * D + wide] = total[line + n : line + n + 1, 0:wide] / many
            fresh = line_s[:, 0 : many + cols]
            fresh_r[...] = jnp.sum(fresh, axis=0)
            renewed = decay_rate * old_r[...].reshape(1, many + cols) + (1.0 - decay_rate) * fresh
            near, far = renewed[:, near_at : near_at + many], renewed[:, far_at : far_at + cols]
            mean = jnp.mean(far if name == "table" else near, axis=1, keepdims=True)
            shape = (rows, many)
            mine = lax.broadcasted_iota(jnp.int32, shape, 1) == lax.broadcasted_iota(jnp.int32, shape, 0) + at[0] * rows
            own = jnp.sum(jnp.where(mine, near, 0.0), axis=1, keepdims=True)
            u = g * lax.rsqrt(own / mean) * lax.rsqrt(far)
            u_r[...] = u
            sizes.append(size_of(u))
        ends = []
        for lo, wide, old, moment_r, u_r in ((0, PIN, pat, m_pat, u_pat), (PIN, POUT, ost, m_out, u_out)):
            g = q[lo : lo + wide, 3 * D : 3 * D + 48]
            moment = decay_rate * old[1] + (1.0 - decay_rate) * (g * g + grad_floor)
            moment_r[...] = moment
            u = g * lax.rsqrt(moment)
            u_r[...] = u
            ends.append(size_of(u))
        line = jnp.zeros((1, D), f32)
        for n, value in enumerate([ends[0], *sizes, ends[1]]):
            line = jnp.where(lane == n, value, line)
        for p in range(parts):
            usq[p] = jnp.broadcast_to(line[:, 0:128], (8, 128))
        head[...] = total[SUMS : SUMS + 1, :] * jnp.where(lane == 10, 1.0 / parts, 1.0)

    outs = [((o.shape[0],), f32) for o in olds] + [(s, f32) for s in shapes]
    outs += [((PIN, 48), f32), ((POUT, 48), f32)] * 2 + [((parts, 8, 128), f32), ((1, D), f32)]
    ops = (place, packs, g_time1, g_time2, g_table, g_mod, gq, gm, gf, *olds, patch_state, out_t)
    scratch = [pltpu.VMEM((1, 9 * D + 128), f32)]
    return kernel_call(body, outs, ops, 3.5, scratch=scratch, places="s" + "v" * (len(ops) - 1))


def new_weights(usq, head, counts, images, updates, weights, patch_state, out_t, m_patch, m_out):
    def body(usq_r, head_r, mp, mo, pat, ost, *refs):
        us, ms, news = refs[0:10], refs[10:18], refs[18:26]
        new_p, new_o, loss_r, rms_r = refs[26:]
        total = usq_r[0, 0:1, :]
        for p in range(1, usq_r.shape[0]):
            total = total + usq_r[p, 0:1, :]
        lane = lax.broadcasted_iota(jnp.int32, (1, 128), 1)
        size = jnp.ones((1, 128), f32)
        for n, count in enumerate(counts):
            size = jnp.where(lane == n, float(count), size)
        rms = jnp.sqrt(total / size)
        step = step_rate * jnp.sqrt(head_r[:, 0:128] / size) / jnp.maximum(1.0, rms / clip_level)
        for n in range(8):
            news[n][...] = ms[n][...] - step[:, n + 1 : n + 2] * us[n + 1][...]
        new_p[0] = pat[0] - step[:, 0:1] * us[0][...]
        new_p[1] = mp[...]
        new_o[0] = ost[0] - step[:, 9:10] * us[9][...]
        new_o[1] = mo[...]
        rms_r[...] = jnp.sum(rms[:, 0:10], axis=0)
        loss_r[...] = jnp.sum(head_r[:, 10:11], axis=0) / images

    outs = [(m.shape, f32) for m in weights] + [(patch_state.shape, f32), (out_t.shape, f32), ((1,), f32), ((10,), f32)]
    ops = (usq, head, m_patch, m_out, patch_state, out_t, *updates, *weights)
    return kernel_call(body, outs, ops, 3.5)


def gather_pieces(x):
    near = [x, flip(x, 2), flip(x, 4), flip(x, 6)]
    return near + [flip(a, 1) for a in near]


def chip_blocks(place, keep, sent, micros, spread=None, copies=0):
    def body(at, keep_r, sent_r, *refs):
        if copies:
            for c in range(copies):
                refs[-1][c] = refs[0][...]
            refs = refs[1:-1]
        for n, out in enumerate(refs):
            chip = jnp.bitwise_xor(at[0] // 2, n)
            out[...] = (keep_r[chip] + sent_r[chip].astype(f32)).astype(out.dtype)

    shape = keep.shape[1:]
    outs, ops = [(shape, f32)] + [(shape, bf16)] * 3, (place, keep, sent)
    if copies:
        outs.append(((copies,) + spread.shape, spread.dtype))
        ops += (spread,)
    return kernel_call(body, outs, ops, micros, places="s" + "v" * (len(ops) - 1))


Z_LANES = 384 + 384 + 128


def copy_blocks(place, parts, after=()):
    def body(at, a, b, c, d, own, one, two, three, cuts):
        total = (a[...] + b[...].astype(f32)) + (c[...].astype(f32) + d[...].astype(f32))
        none = jnp.zeros((48, 32), f32)
        for j in range(4):
            cuts[j, :, 0:384] = total[:, D + j * 384 : D + (j + 1) * 384]
            cuts[j, :, 384:768] = total[:, D + FF + j * 384 : D + FF + (j + 1) * 384]
            cuts[j, :, 768:] = jnp.concatenate([total[:, j * 96 : (j + 1) * 96], none], axis=1)
        for n, out in enumerate((own, one, two, three)):
            out[...] = cuts[jnp.bitwise_xor(at[2], n)].astype(out.dtype)

    outs = [((48, Z_LANES), f32)] + [((48, Z_LANES), bf16)] * 3
    return kernel_call(body, outs, (place, *parts), 2, scratch=[pltpu.VMEM((4, 48, Z_LANES), f32)], places="svvvv", after=after)


def chips_sum(blocks):
    total = blocks[0]
    for n in range(1, 4):
        total = total + flip(blocks[n], 2 * n).astype(f32)
    return total.astype(bf16)


def other_copies(total):
    return (total, flip(total, 1, "rep"), flip(total, 2, "rep"), flip(total, 3, "rep"))


def eight_by_four(
    latents, noise, tsteps, labels, patch_state, time1_w, time2_w, table_t, mod_w, qkv_w, proj_w, fc1_w, fc2_w, out_t, olds, place, plan, grid, times
):
    reps, parts = 4, 8
    images = tsteps.shape[0]
    bundle = bundle_rows(tsteps, labels, time1_w, time2_w)
    pieces = gather_pieces(bundle)
    w_own, mod16, tab16, sums = cast_weights(
        patch_state, out_t, time1_w, time2_w, table_t, mod_w, qkv_w, proj_w, fc1_w, fc2_w, after=pieces[1:4]
    )
    w_pieces = gather_pieces(w_own)
    shares, w1, w2 = modulation_shares(place, pieces, times, tab16, mod16, images)
    shares = lax.all_to_all(shares, "fsdp", 0, 0)

    w_qkv, head, mod, con, noisy, hidden0, attn16, qkv16, totals, mixture16 = attention_forward(
        tsteps, latents, noise, plan, grid, w_pieces, shares, place
    )
    keep, send, g_last, d_mix16, d_h1, d_mod, loss_tile = mlp_pass(
        noise, con, mod, hidden0, mixture16, head, w_pieces, place
    )
    send = flip(send, 1)
    d_qkv16, d_mod16, d_h0 = attention_back(
        mod, hidden0, qkv16, totals, d_mix16, d_h1, d_mod, w_qkv, loss_tile, bundle, after=(keep,)
    )
    *blocks, d_mod16 = chip_blocks(place, keep, send, 2, d_mod16, reps * parts // 2)
    everyone = [[r * parts + c * 2 + side for r in range(reps) for c in range(parts // 2)] for side in range(2)]
    own_mod = lax.all_to_all(d_mod16, ("rep", "fsdp"), 0, 0, axis_index_groups=everyone)
    oth_mod = flip(own_mod, 1)
    keep, send = tail_grad(attn16, d_qkv16, noisy, d_h0, g_last, place, True, after=(blocks[1],))
    send = flip(send, 1)
    g_mod, g_table, d_time, loss, feat16, act16_t, time_slope = condition_back(
        place, own_mod, oth_mod, w1, w2, times, tab16, mod16, reps, parts, images
    )
    cuts = copy_blocks(place, [blocks[0]] + [flip(blocks[n], 2 * n) for n in range(1, 4)], after=(loss,))
    mid = (cuts[0] + flip(cuts[1], 1, "rep").astype(f32)) + (flip(cuts[2], 2, "rep").astype(f32) + flip(cuts[3], 3, "rep").astype(f32))
    mid = other_copies(mid.astype(bf16))
    tail = other_copies(chips_sum(chip_blocks(place, keep, send, 1)))
    gm, gf, pack = sums_early(place, mid)
    d_time = lax.all_to_all(d_time, "fsdp", 0, 0)
    pack = sums_middle(pack, g_table, g_mod, sums, loss)
    g_time1, g_time2 = time_back(d_time, w2, act16_t, time_slope, feat16)
    gq, pack = sums_late(pack, tail, g_time1, g_time2)
    packs = gather_rows(pack).reshape(parts, LINES, D)
    result = scaled_updates(place, packs, g_time1, g_time2, g_table, g_mod, gq, gm, gf, olds, patch_state, out_t)
    fresh, updates = result[:8], result[8:16]
    u_patch, u_out, m_patch, m_out, usq, sums = result[16:]
    usq = lax.all_to_all(usq, "fsdp", 0, 0)
    weights = (time1_w, time2_w, table_t, mod_w, qkv_w, proj_w, fc1_w, fc2_w)
    counts = [w.size * parts for w in (patch_state[0], *weights, out_t[0])]
    *news, new_patch, new_out, loss, rms = new_weights(
        usq, sums, counts, images * reps * parts, (u_patch, *updates, u_out), weights, patch_state, out_t, m_patch, m_out
    )
    news[2] = news[2].T
    outs = [new_patch]
    for n in range(8):
        outs += [news[n], fresh[n]]
    return tuple(outs) + (new_out.transpose(0, 2, 1), loss.reshape(()), rms)


def per_device(
    latents,
    noise,
    timesteps,
    labels,
    patch_state,
    time1_w,
    time1_f,
    time2_w,
    time2_f,
    table_w,
    table_f,
    mod_w,
    mod_f,
    qkv_w,
    qkv_f,
    proj_w,
    proj_f,
    fc1_w,
    fc1_f,
    fc2_w,
    fc2_f,
    out_state,
):
    reps, parts = lax.axis_size("rep"), lax.axis_size("fsdp")
    position = lax.axis_index("fsdp")
    masters = (patch_state[0], time1_w, time2_w, table_w, mod_w, qkv_w, proj_w, fc1_w, fc2_w, out_state[0])
    images = latents.shape[0] * latents.shape[1]
    latents = latents.reshape(images, TOK_IMG, PIN).transpose(0, 2, 1)
    noise = noise.reshape(images, TOK_IMG, PIN).transpose(0, 2, 1)
    out_t = out_state.transpose(0, 2, 1)
    tsteps = timesteps.reshape(images)
    labels = labels.reshape(images)
    own_d = D // parts
    own_t = TFREQ // parts
    place = jnp.stack([position, position & 1, lax.axis_index("rep")]).astype(jnp.int32)
    plan, grid = jnp.asarray(plan_table()), jnp.asarray(place_table())
    times = jnp.asarray(time_table(), bf16)
    olds = (time1_f, time2_f, table_f, mod_f, qkv_f, proj_f, fc1_f, fc2_f)

    if parts == 8 and reps == 4:
        return eight_by_four(
            latents, noise, tsteps, labels, patch_state, time1_w, time2_w, table_w.T, mod_w, qkv_w, proj_w, fc1_w, fc2_w, out_t, olds, place, plan, grid, times
        )

    info = jnp.stack([tsteps // 32, tsteps % 32, labels // 32, labels % 32]).reshape(1, 4 * images)
    info_row = jnp.pad(info.astype(bf16), ((0, 0), (0, D - 4 * images)))
    bundle = jnp.concatenate([time1_w.astype(bf16), time2_w.astype(bf16), info_row], axis=0)
    bundle = gather_rows(bundle).reshape(parts, own_t + own_d + 1, D)
    w_time1 = bundle[:, :own_t].reshape(TFREQ, D)
    w_time2 = bundle[:, own_t : own_t + own_d].reshape(D, D)
    info_rep = bundle[:, own_t + own_d, : 4 * images]

    head = lax.all_gather(jnp.concatenate([patch_state[0], out_t[0]], axis=0).astype(bf16), "fsdp", axis=1, tiled=True)
    w_rows = gather_rows(jnp.concatenate([qkv_w, proj_w, fc1_w], axis=1).astype(bf16))
    w_fc2 = gather_rows(fc2_w.astype(bf16))
    w_qkv, w_proj, w_fc1 = w_rows[:, : 3 * D], w_rows[:, 3 * D : 4 * D], w_rows[:, 4 * D :]

    info_all = rep_gather(info_rep).reshape(reps * parts, 4, images).astype(jnp.int32)
    w_mod16 = mod_w.astype(bf16)
    w_table16 = table_w.astype(bf16)

    def condition_path(info_any):
        ts = (info_any[:, 0] * 32 + info_any[:, 1]).reshape(-1)
        lab = (info_any[:, 2] * 32 + info_any[:, 3]).reshape(-1)
        feats16 = dot(pick(ts, STEPS), times).astype(bf16)
        time_act, time_slope = silu_pair(dot(feats16, w_time1))
        time_act16 = time_act.astype(bf16)
        time_emb = dot(time_act16, w_time2)
        own_emb = lax.dynamic_slice(time_emb, (0, position * own_d), (time_emb.shape[0], own_d))
        picks = pick(lab, CLASSES)
        cond_act, cond_slope = silu_pair(own_emb + dot(picks, w_table16))
        return feats16, time_act16, time_slope, picks, cond_act.astype(bf16), cond_slope

    info_here = info_rep.reshape(parts, 4, images).astype(jnp.int32)
    cond_here = condition_path(info_here)[4]
    shares = dot(cond_here, w_mod16).reshape(parts, 8, images * D)
    shares = lax.all_to_all(shares, "fsdp", 0, 0, tiled=True)

    mod, con, noisy, hidden0, attn16, qkv16, totals, mixture16 = attention_forward(
        tsteps, latents, noise, plan, grid, (w_qkv, head), shares, place
    )
    g_proj, g_fc1, g_fc2, g_last, d_mix16, d_h1, d_mod, loss_tile = mlp_pass(
        noise, con, mod, hidden0, mixture16, head, (w_proj, w_fc1, w_fc2), place
    )
    loss_part = loss_tile[0, 0]
    d_qkv16, d_mod16, d_h0 = attention_back(
        mod, hidden0, qkv16, totals, d_mix16, d_h1, d_mod, w_qkv, loss_tile, None
    )
    g_tail, g_head = tail_grad(attn16, d_qkv16, noisy, d_h0, g_last, place, False)

    d_mod_all = rep_gather(d_mod16).reshape(1, -1)
    d_mod_all = gather_rows(d_mod_all).reshape(parts, reps, images, 8 * D)
    d_mod_all = d_mod_all.transpose(1, 0, 2, 3).reshape(reps * parts * images, 8 * D)
    feats16, time_act16, time_slope, picks, cond16, cond_slope = condition_path(info_all)
    d_cond = dot_nt(d_mod_all, w_mod16) * cond_slope
    g_mod = dot_tn(cond16, d_mod_all)
    g_table = lax.dot_general(
        picks.astype(f32), d_cond, (((0,), (0,)), ((), ())), precision=lax.Precision.HIGHEST
    )
    d_time16 = lax.all_gather(d_cond.astype(bf16), "fsdp", axis=0)
    d_time16 = d_time16.transpose(1, 0, 2).reshape(-1, D)
    own_act16 = lax.dynamic_slice(time_act16, (0, position * own_d), (time_act16.shape[0], own_d))
    g_time2 = dot_tn(own_act16, d_time16)
    d_hid16 = (dot_nt(d_time16, w_time2) * time_slope).astype(bf16)
    own_feat16 = lax.dynamic_slice(feats16, (0, position * own_t), (feats16.shape[0], own_t))
    g_time1 = dot_tn(own_feat16, d_hid16)

    g_head = lax.psum_scatter(g_head, "fsdp", scatter_dimension=1, tiled=True)
    g_tail, g_proj, g_fc1, g_fc2 = (sum_scatter(g) for g in (g_tail, g_proj, g_fc1, g_fc2))
    g_proj, g_fc1, g_fc2 = (rep_sum(g.astype(bf16)) for g in (g_proj, g_fc1, g_fc2))
    g_tail = rep_sum(g_tail.astype(bf16))
    g_head = rep_sum(g_head)
    grads = (
        g_head[:PIN],
        g_time1,
        g_time2,
        g_table,
        g_mod,
        g_tail,
        g_proj,
        g_fc1,
        g_fc2,
        g_head[PIN:].T,
    )
    loss_part = lax.psum(loss_part, "rep")
    dims = (0, 0, 1, 0, 0, 0, 0, 0)

    packs = []
    for slot in range(8):
        grad, dim = grads[slot + 1], dims[slot]
        squares = grad * grad + grad_floor
        near = jnp.sum(squares, axis=1 - dim)
        far = jnp.sum(squares, axis=dim)
        spread = lax.dynamic_update_slice(
            jnp.zeros((near.shape[0] * parts,), f32), near / far.shape[0], (position * near.shape[0],)
        )
        far = far / (near.shape[0] * parts)
        packs.append(jnp.concatenate([spread, far] if dim == 0 else [far, spread]))
    tail = jnp.stack([jnp.sum(m * m) for m in masters] + [loss_part])
    lengths = [pack.shape[0] for pack in packs]
    totals = lax.psum(jnp.concatenate(packs + [tail]), "fsdp")
    fresh = []
    start = 0
    for length in lengths:
        fresh.append(totals[start : start + length])
        start += length
    square_tot = totals[start : start + 10]
    loss = totals[start + 10] / (images * reps * parts)

    updates, counts = [], []
    plain = []
    for slot in range(10):
        grad = grads[slot]
        if slot in (0, 9):
            state = patch_state if slot == 0 else out_state
            moment = decay_rate * state[1] + (1.0 - decay_rate) * (grad * grad + grad_floor)
            plain.append(moment)
            updates.append(grad * lax.rsqrt(moment))
            counts.append(grad.size * parts)
            continue
        dim = dims[slot - 1]
        renewed = decay_rate * olds[slot - 1] + (1.0 - decay_rate) * fresh[slot - 1]
        rows = grad.shape[0] * (parts if dim == 0 else 1)
        row, col = renewed[:rows], renewed[rows:]
        mean_row = jnp.mean(row)
        if dim == 0:
            row = lax.dynamic_slice(row, (position * grad.shape[0],), (grad.shape[0],))
        else:
            col = lax.dynamic_slice(col, (position * grad.shape[1],), (grad.shape[1],))
        updates.append(grad * lax.rsqrt(row[:, None] * col[None, :] / mean_row))
        counts.append(grad.size * parts)
    update_tot = lax.psum(jnp.stack([jnp.sum(u * u) for u in updates]), "fsdp")
    sizes = np.asarray(counts, np.float32)
    size_rms = jnp.sqrt(update_tot / sizes)
    factor = step_rate * jnp.sqrt(square_tot / sizes) / jnp.maximum(1.0, size_rms / clip_level)
    new = [masters[s] - factor[s] * updates[s] for s in range(10)]
    result = [jnp.stack([new[0], plain[0]])]
    for slot in range(8):
        result += [new[slot + 1], fresh[slot]]
    return tuple(result) + (jnp.stack([new[9], plain[1]]), loss, size_rms)


def solution(mesh):
    images = P(None, ("rep", "fsdp"), None, None)
    singles = P(None, ("rep", "fsdp"))
    rows, cols = P("fsdp", None), P(None, "fsdp")
    placed = (images, images, singles, singles, P(None, None, "fsdp"))
    placed += (rows, P(), rows, P(), cols, P()) + (rows, P()) * 5 + (P(None, "fsdp", None),)
    results = (P(None, None, "fsdp"), rows, P(), rows, P(), cols, P()) + (rows, P()) * 5
    results += (P(None, "fsdp", None), P(), P())
    return jax.shard_map(per_device, mesh=mesh, in_specs=placed, out_specs=results, check_vma=False)
```

time: 355 us -> 165 us (0.46); the launches traced: 348 us -> 165 us
  other arithmetic: 76.1 us -> 0.18 us
  blocking collectives: 81.2 us -> 26.1 us
  local copies, waits for them, and re-layouts: 58.6 us -> 14.1 us
  matrix products: 41.7 us -> 0 us
  Pallas kernels: 0 us -> 38.5 us
  between operations: 27 us -> 1.5 us
  starting transfers between devices: 32.5 us -> 43 us
  waiting for transfers between devices: 31 us -> 41.3 us
    psum x3 -> x0, blocking collectives: 48.2 us -> none  [the longest x1 23.1 us: per_device(): totals = lax.psum(jnp.concatenate(packs + [tail]), 'fsdp')]
    dot_general x35 -> x0, matrix products: 41.7 us -> none  [the longest x9 13.8 us: dot_tn(): lax.dot_general(a, b, (((0,), (0,)), ((), ())), preferred_element_type=f32)]
    pallas_call x0 -> x17, Pallas kernels: none -> 38.5 us  [kernel_call(): pl.pallas_call(run, out_shape=[jax.ShapeDtypeStruct(s, t) for s, t in out...]
    reduce_sum x33 -> x0, other arithmetic: 23.5 us -> none  [the longest x10 12.5 us: per_device(): tail = jnp.stack([jnp.sum(m * m) for m in masters] + [loss_part])]
    sub x9 -> x0, other arithmetic: 18.5 us -> none  [the longest x8 16 us: per_device(): new = [masters[s] - factor[s] * updates[s] for s in range(10)]]
    all_to_all x0 -> x2, blocking collectives: none -> 16.1 us  [the longest x1 8.73 us: eight_by_four(): shares = lax.all_to_all(shares, 'fsdp', 0, 0)]
    all_gather x2 -> x1, blocking collectives: 23.7 us -> 9.96 us  [gather_rows(): return lax.all_gather(x, 'fsdp', axis=0, tiled=True)]
    convert_element_type x13 -> x0, local copies, waits for them, and re-layouts: 11 us -> none  [the longest x3 4.05 us: sum_scatter(): send = lax.dynamic_index_in_dim(g, 1 - core, 1, keepdims=False).astype(bf16)]
  transfers between devices with their start and end apart: 30 -> 34, of which waited for: 11 -> 13; matrix products, arithmetic and copies ran while one was open for 21% -> 0% of each run, Pallas kernels for 0% -> 9%
where the time goes in v2:
time: 165 us
  starting transfers between devices  43 us (26%)
  waiting for transfers between devices  41.3 us (25%)
  Pallas kernels  38.5 us (23%)
  blocking collectives  26.1 us (16%)
  local copies, waits for them, and re-layouts  14.1 us (9%)
    pallas_call x17, Pallas kernels, kernel_call(): pl.pallas_call(run, out_shape=[jax.ShapeDtypeStruct(s, t) for s, t in out...  38.5 us
    ppermute x32, waiting for transfers between devices, flip(): return lax.ppermute(x, axis, [(i, i ^ bit) for i in range(size)])  35.7 us
    ppermute x32, starting transfers between devices, flip(): return lax.ppermute(x, axis, [(i, i ^ bit) for i in range(size)])  34.3 us
    unnamed x126, local copies, waits for them, and re-layouts  14.1 us
    all_gather x1, blocking collectives, gather_rows(): return lax.all_gather(x, 'fsdp', axis=0, tiled=True)  9.96 us
    all_to_all x1, blocking collectives, eight_by_four(): shares = lax.all_to_all(shares, 'fsdp', 0, 0)  8.73 us
    all_to_all x1, blocking collectives, eight_by_four(): usq = lax.all_to_all(usq, 'fsdp', 0, 0)  7.38 us
    all_to_all x1, waiting for transfers between devices, eight_by_four(): lax.all_to_all(d_mod16, ('rep', 'fsdp'), 0, 0, axis_index_groups=everyone)  5.57 us
  transfers between devices with their start and end apart: 34, of which 13 were waited for; matrix products, arithmetic and copies ran while one was open for 0% of the time, Pallas kernels for 9%

profile of v2, /device:TPU:0, one launch (start us, length us, event | category | flops | bytes accessed | tf_op | source)
XLA Modules:
  0.0 164.7 jit_solution(11452650607009152065)
XLA Ops:
  4.4 4.0 %collective-permute-start.2 = (bf16[96,384]{1,0:T(8,128)(2,1)S(1)}, bf16[96,384]{1,0:T(8,128)(2,1)S(1)}, u32[]{:S(2)}, u32[]{:S(2)}) collective-permute-start(bf16[96,384]{1,0:T(8,128)(2,1)S(1)} %shard_map.392.refs_1_.refs_9_), channel_id=1, source_target_pairs={{0,6},{1,7},{2,4},{3,5},{4,2},{5,3},{6,0},{7,1},{8,14},{9,15},{10,... | collective-permute-start | bytes 221192 | tf_op jit(solution)/shard_map/ppermute | solution.py:98
  9.0 1.7 %collective-permute-done.2.refs_12_.refs_4_ = bf16[96,384]{1,0:T(8,128)(2,1)S(1)} collective-permute-done((bf16[96,384]{1,0:T(8,128)(2,1)S(1)}, bf16[96,384]{1,0:T(8,128)(2,1)S(1)}, u32[]{:S(2)}, u32[]{:S(2)}) %collective-permute-start.2) | collective-permute-done | bytes 73760 | tf_op jit(solution)/shard_map/ppermute | solution.py:98
  10.7 2.0 %collective-permute-done.1.refs_11_.refs_3_ = bf16[96,384]{1,0:T(8,128)(2,1)S(1)} collective-permute-done((bf16[96,384]{1,0:T(8,128)(2,1)S(1)}, bf16[96,384]{1,0:T(8,128)(2,1)S(1)}, u32[]{:S(2)}, u32[]{:S(2)}) %collective-permute-start.1) | collective-permute-done | bytes 73760 | tf_op jit(solution)/shard_map/ppermute | solution.py:98
  14.9 1.5 collective-permute-start.9
  21.1 8.1 %collective-permute-done.9.refs_10_ = bf16[48,4736]{1,0:T(8,128)(2,1)S(1)} collective-permute-done((bf16[48,4736]{1,0:T(8,128)(2,1)S(1)}, bf16[48,4736]{1,0:T(8,128)(2,1)S(1)}, u32[]{:S(2)}, u32[]{:S(2)}) %collective-permute-start.9) | collective-permute-done | bytes 454688 | tf_op jit(solution)/shard_map/ppermute | solution.py:98
  29.2 7.6 %collective-permute-done.8.refs_9_ = bf16[48,4736]{1,0:T(8,128)(2,1)S(1)} collective-permute-done((bf16[48,4736]{1,0:T(8,128)(2,1)S(1)}, bf16[48,4736]{1,0:T(8,128)(2,1)S(1)}, u32[]{:S(2)}, u32[]{:S(2)}) %collective-permute-start.8) | collective-permute-done | bytes 454688 | tf_op jit(solution)/shard_map/ppermute | solution.py:98
  40.2 1.6 shard_map.394
  42.5 8.7 %all_to_all.20.refs_6_ = f32[8,8,768]{2,1,0:T(8,128)S(1)} all-to-all(f32[8,8,768]{2,1,0:T(8,128)S(1)} %get-tuple-element.112), channel_id=1, replica_groups=mesh['rep'=4,'fsdp'=8] {'fsdp'}, dimensions={0} | all-to-all | bytes 393216 | tf_op jit(solution)/shard_map/all_to_all | solution.py:865
  51.3 5.0 %shard_map.395 = (bf16[384,1152]{1,0:T(8,128)(2,1)S(1)}, bf16[48,384]{1,0:T(8,128)(2,1)S(1)}, f32[2,3072]{1,0:T(2,128)S(1)}, f32[2,8]{1,0:T(2,128)S(1)}, bf16[2,...) custom-call(s32[2]{0:T(128)S(1)} %bitcast.29, ...), custom_call_target="tpu_custom_call" | custom-call | flops 9200000000 | bytes 1000000 | tf_op jit(solution)/shard_map/pallas_call | solution.py:141
  57.1 11.9 %shard_map.396 = (f32[4,48,3456]{2,1,0:T(8,128)S(1)}, bf16[4,48,3456]{2,1,0:T(8,128)(2,1)S(1)}, f32[32,384]{1,0:T(8,128)S(1)}, bf16[2,256,384]{2,1,0:T(8,128)(2,...) custom-call(s32[3]{0:T(128)S(1)} %pad_add_fusion.refs_0_.refs_1_, ...), custom_call_target="tpu_custom_call" | custom-call | flops 14949999616 | bytes 1000000 | tf_op jit(solution)/shard_map/pallas_call | solution.py:141
  69.1 5.3 %shard_map.397 = (bf16[512,1152]{1,0:T(8,128)(2,1)S(1)}, bf16[16,512]{1,0:T(8,128)(2,1)S(1)}, bf16[2,256,384]{2,1,0:T(8,128)(2,1)S(1)}) custom-call(f32[2,3072]{1,0:T(2,128)S(1)} %get-tuple-element.115.refs_3_.refs_0_, f32[2,256,384]{2,1,0:T(8,128)S(1)} %get-tuple-element.116.refs_4_.refs_1_, bf16[2,256,1152]{2,1,0:T(8,128)(2,1)S(1)} %get-tuple-element.121.refs_2_, ...), custom_call_target="tpu_custom_call" | custom-call | flops 8049999872 | bytes 1000000 | tf_op jit(solution)/shard_map/pallas_call | solution.py:141
  74.5 1.5 shard_map.398
  76.8 5.0 %all-to-all-start.1 = ((bf16[16,16,512]{2,1,0:T(8,128)(2,1)}), bf16[16,16,512]{2,1,0:T(8,128)(2,1)S(1)}, u32[]{:S(2)}, u32[]{:S(2)}) async-start(bf16[16,16,512]{2,1,0:T(8,128)(2,1)} %get-tuple-element.133), calls=%async_computation.1 | async-start | bytes 524288 | tf_op jit(solution)/shard_map/all_to_all | solution.py:879
  84.1 1.5 shard_map.403
  86.8 5.6 %all-to-all-done.1.refs_1_ = bf16[16,16,512]{2,1,0:T(8,128)(2,1)S(1)} async-done(((bf16[16,16,512]{2,1,0:T(8,128)(2,1)}), bf16[16,16,512]{2,1,0:T(8,128)(2,1)S(1)}, u32[]{:S(2)}, u32[]{:S(2)}) %all-to-all-start.1) | async-done | bytes 262176 | tf_op jit(solution)/shard_map/all_to_all | solution.py:879
  93.8 2.0 %collective-permute-start.17 = (bf16[48,3456]{1,0:T(8,128)(2,1)S(1)}, bf16[48,3456]{1,0:T(8,128)(2,1)S(1)}, u32[]{:S(2)}, u32[]{:S(2)}) collective-permute-start(bf16[48,3456]{1,0:T(8,128)(2,1)S(1)} %get-tuple-element.132), channel_id=1, source_target_pairs={{0,6},{1,7},{2,4},{3,5},{4,2},{5,3},{6,0},{7,1},{8,14},{9,15},{10,... | collective-permute-start | bytes 995336 | tf_op jit(solution)/shard_map/ppermute | solution.py:98
  99.3 2.9 %shard_map.399 = (f32[48,3072]{1,0:T(8,128)S(1)}, f32[48,1001]{1,0:T(8,128)S(1)}, bf16[8,64,128]{2,1,0:T(8,128)(2,1)}, f32[8,128]{1,0:T(8,128)S(1)}, bf16[64,32]...) custom-call(s32[3]{0:T(128)S(1)} %pad_add_fusion.refs_0_.refs_1_, ...), custom_call_target="tpu_custom_call" | custom-call | flops 4600000000 | bytes 1000000 | tf_op jit(solution)/shard_map/pallas_call | solution.py:141
  102.2 8.7 %collective-permute-done.16.refs_3_ = bf16[48,3456]{1,0:T(8,128)(2,1)S(1)} collective-permute-done((bf16[48,3456]{1,0:T(8,128)(2,1)S(1)}, bf16[48,3456]{1,0:T(8,128)(2,1)S(1)}, u32[]{:S(2)}, u32[]{:S(2)}) %collective-permute-start.16) | collective-permute-done | bytes 331808 | tf_op jit(solution)/shard_map/ppermute | solution.py:98
  110.8 1.6 collective-permute-start.28
  114.3 1.5 collective-permute-start.20
  115.8 2.0 %collective-permute-start.21 = (bf16[48,896]{1,0:T(8,128)(2,1)S(1)}, bf16[48,896]{1,0:T(8,128)(2,1)S(1)}, u32[]{:S(2)}, u32[]{:S(2)}) collective-permute-start(bf16[48,896]{1,0:T(8,128)(2,1)S(1)} %get-tuple-element.140), channel_id=1, source_target_pairs={{0,24},{8,16},{16,8},{24,0},{1,25},{9,17},{17,9},{25,1},{2,26},{10... | collective-permute-start | bytes 258056 | tf_op jit(solution)/shard_map/ppermute | solution.py:98
  117.9 1.9 %collective-permute-start.31 = (bf16[48,1280]{1,0:T(8,128)(2,1)S(1)}, bf16[48,1280]{1,0:T(8,128)(2,1)S(1)}, u32[]{:S(2)}, u32[]{:S(2)}) collective-permute-start(bf16[48,1280]{1,0:T(8,128)(2,1)S(1)} %add_convert_fusion.refs_1_), channel_id=1, source_target_pairs={{0,24},{8,16},{16,8},{24,0},{1,25},{9,17},{17,9},{25,1},{2,26},{10... | collective-permute-start | bytes 368648 | tf_op jit(solution)/shard_map/ppermute | solution.py:98
  119.8 3.6 %all-to-all-start.2 = ((bf16[8,64,128]{2,1,0:T(8,128)(2,1)}), bf16[8,64,128]{2,1,0:T(8,128)(2,1)S(1)}, u32[]{:S(2)}, u32[]{:S(2)}) async-start(bf16[8,64,128]{2,1,0:T(8,128)(2,1)} %get-tuple-element.156), calls=%async_computation.2 | async-start | bytes 262144 | tf_op jit(solution)/shard_map/all_to_all | solution.py:891
  123.4 4.4 %collective-permute-done.20 = bf16[48,896]{1,0:T(8,128)(2,1)S(1)} collective-permute-done((bf16[48,896]{1,0:T(8,128)(2,1)S(1)}, bf16[48,896]{1,0:T(8,128)(2,1)S(1)}, u32[]{:S(2)}, u32[]{:S(2)}) %collective-permute-start.20) | collective-permute-done | bytes 86048 | tf_op jit(solution)/shard_map/ppermute | solution.py:98
  127.9 1.3 collective-permute-start.24
  129.2 4.4 %collective-permute-start.23 = (bf16[48,896]{1,0:T(8,128)(2,1)S(1)}, bf16[48,896]{1,0:T(8,128)(2,1)S(1)}, u32[]{:S(2)}, u32[]{:S(2)}) collective-permute-start(bf16[48,896]{1,0:T(8,128)(2,1)S(1)} %add_convert_fusion.1.refs_1_), channel_id=1, source_target_pairs={{0,16},{8,24},{16,0},{24,8},{1,17},{9,25},{17,1},{25,9},{2,18},{10... | collective-permute-start | bytes 258056 | tf_op jit(solution)/shard_map/ppermute | solution.py:98
  134.3 5.5 %collective-permute-start.29 = (bf16[48,1280]{1,0:T(8,128)(2,1)S(1)}, bf16[48,1280]{1,0:T(8,128)(2,1)S(1)}, u32[]{:S(2)}, u32[]{:S(2)}) collective-permute-start(bf16[48,1280]{1,0:T(8,128)(2,1)S(1)} %add_convert_fusion.refs_1_), channel_id=1, source_target_pairs={{0,8},{8,0},{16,24},{24,16},{1,9},{9,1},{17,25},{25,17},{2,10},{10... | collective-permute-start | bytes 368648 | tf_op jit(solution)/shard_map/ppermute | solution.py:98
  140.9 1.3 shard_map.401
  143.6 10.0 %all_gather.3 = f32[256,384]{1,0:T(8,128)S(1)} all-gather(f32[32,384]{1,0:T(8,128)S(1)} %get-tuple-element.162), channel_id=1, replica_groups=mesh['rep'=4,'fsdp'=8] {'fsdp'}, dimensions={0}, use_global_device_ids=true | all-gather | bytes 442368 | tf_op jit(solution)/shard_map/all_gather | solution.py:121
  153.7 2.0 %shard_map.407 = (f32[640]{0:T(1024)}, f32[768]{0:T(1024)}, f32[1385]{0:T(1024)}, f32[3456]{0:T(1024)}, f32[1536]{0:T(1024)}, /*index=5*/f32[768]{0:T(1024)}, f3...) custom-call(s32[3]{0:T(128)S(1)} %pad_add_fusion.refs_0_.refs_1_, ...), custom_call_target="tpu_custom_call" | custom-call | flops 4024999936 | bytes 1000000 | tf_op jit(solution)/shard_map/pallas_call | solution.py:141
  155.7 7.4 %all_to_all.21.refs_0_ = f32[8,8,128]{2,1,0:T(8,128)S(1)} all-to-all(f32[8,8,128]{2,1,0:T(8,128)S(1)} %get-tuple-element.166), channel_id=1, replica_groups=mesh['rep'=4,'fsdp'=8] {'fsdp'}, dimensions={0} | all-to-all | bytes 65536 | tf_op jit(solution)/shard_map/all_to_all | solution.py:899
  163.1 1.5 shard_map.408
  (185 shorter events, 30.2 us)
Async XLA Ops:
  4.4 6.3 %collective-permute-start.2 = (bf16[96,384]{1,0:T(8,128)(2,1)S(1)}, bf16[96,384]{1,0:T(8,128)(2,1)S(1)}, u32[]{:S(2)}, u32[]{:S(2)}) collective-permute-start(bf16[96,384]{1,0:T(8,128)(2,1)S(1)} %shard_map.392.refs_1_.refs_9_), channel_id=1, source_target_pairs={{0,6},{1,7},{2,4},{3,5},{4,2},{5,3},{6,0},{7,1},{8,14},{9,15},{10,... | collective-permute-start | bytes 221192 | tf_op jit(solution)/shard_map/ppermute | solution.py:98
  8.3 4.4 %collective-permute-start.1 = (bf16[96,384]{1,0:T(8,128)(2,1)S(1)}, bf16[96,384]{1,0:T(8,128)(2,1)S(1)}, u32[]{:S(2)}, u32[]{:S(2)}) collective-permute-start(bf16[96,384]{1,0:T(8,128)(2,1)S(1)} %shard_map.392.refs_1_.refs_9_), channel_id=1, source_target_pairs={{0,4},{1,5},{2,6},{3,7},{4,0},{5,1},{6,2},{7,3},{8,12},{9,13},{10,... | collective-permute-start | bytes 221192 | tf_op jit(solution)/shard_map/ppermute | solution.py:98
  8.8 4.4 %collective-permute-start = (bf16[96,384]{1,0:T(8,128)(2,1)S(1)}, bf16[96,384]{1,0:T(8,128)(2,1)S(1)}, u32[]{:S(2)}, u32[]{:S(2)}) collective-permute-start(bf16[96,384]{1,0:T(8,128)(2,1)S(1)} %shard_map.392.refs_1_.refs_9_), channel_id=1, source_target_pairs={{0,2},{1,3},{2,0},{3,1},{4,6},{5,7},{6,4},{7,5},{8,10},{9,11},{10,... | collective-permute-start | bytes 221192 | tf_op jit(solution)/shard_map/ppermute | solution.py:98
  14.9 14.3 %collective-permute-start.9 = (bf16[48,4736]{1,0:T(8,128)(2,1)S(1)}, bf16[48,4736]{1,0:T(8,128)(2,1)S(1)}, u32[]{:S(2)}, u32[]{:S(2)}) collective-permute-start(bf16[48,4736]{1,0:T(8,128)(2,1)S(1)} %get-tuple-element.113.refs_7_), channel_id=1, source_target_pairs={{0,6},{1,7},{2,4},{3,5},{4,2},{5,3},{6,0},{7,1},{8,14},{9,15},{10,... | collective-permute-start | bytes 1363976 | tf_op jit(solution)/shard_map/ppermute | solution.py:98
  16.4 20.4 %collective-permute-start.8 = (bf16[48,4736]{1,0:T(8,128)(2,1)S(1)}, bf16[48,4736]{1,0:T(8,128)(2,1)S(1)}, u32[]{:S(2)}, u32[]{:S(2)}) collective-permute-start(bf16[48,4736]{1,0:T(8,128)(2,1)S(1)} %get-tuple-element.113.refs_7_), channel_id=1, source_target_pairs={{0,4},{1,5},{2,6},{3,7},{4,0},{5,1},{6,2},{7,3},{8,12},{9,13},{10,... | collective-permute-start | bytes 1363976 | tf_op jit(solution)/shard_map/ppermute | solution.py:98
  17.1 19.7 %collective-permute-start.7 = (bf16[48,4736]{1,0:T(8,128)(2,1)S(1)}, bf16[48,4736]{1,0:T(8,128)(2,1)S(1)}, u32[]{:S(2)}, u32[]{:S(2)}) collective-permute-start(bf16[48,4736]{1,0:T(8,128)(2,1)S(1)} %get-tuple-element.113.refs_7_), channel_id=1, source_target_pairs={{0,2},{1,3},{2,0},{3,1},{4,6},{5,7},{6,4},{7,5},{8,10},{9,11},{10,... | collective-permute-start | bytes 1363976 | tf_op jit(solution)/shard_map/ppermute | solution.py:98
  18.4 1.4 collective-permute-start.6
  19.8 17.5 %collective-permute-start.4 = (bf16[96,384]{1,0:T(8,128)(2,1)S(1)}, bf16[96,384]{1,0:T(8,128)(2,1)S(1)}, u32[]{:S(2)}, u32[]{:S(2)}) collective-permute-start(bf16[96,384]{1,0:T(8,128)(2,1)S(1)} %collective-permute-done.refs_10_.refs_2_), channel_id=1, source_target_pairs={{0,1},{1,0},{2,3},{3,2},{4,5},{5,4},{6,7},{7,6},{8,9},{9,8},{10,11... | collective-permute-start | bytes 221192 | tf_op jit(solution)/shard_map/ppermute | solution.py:98
  20.9 30.3 %collective-permute-start.10 = (bf16[48,4736]{1,0:T(8,128)(2,1)S(1)}, bf16[48,4736]{1,0:T(8,128)(2,1)S(1)}, u32[]{:S(2)}, u32[]{:S(2)}) collective-permute-start(bf16[48,4736]{1,0:T(8,128)(2,1)S(1)} %get-tuple-element.113.refs_7_), channel_id=1, source_target_pairs={{0,1},{1,0},{2,3},{3,2},{4,5},{5,4},{6,7},{7,6},{8,9},{9,8},{10,11... | collective-permute-start | bytes 1363976 | tf_op jit(solution)/shard_map/ppermute | solution.py:98
  29.2 22.1 %collective-permute-start.13 = (bf16[48,4736]{1,0:T(8,128)(2,1)S(1)}, bf16[48,4736]{1,0:T(8,128)(2,1)S(1)}, u32[]{:S(2)}, u32[]{:S(2)}) collective-permute-start(bf16[48,4736]{1,0:T(8,128)(2,1)S(1)} %collective-permute-done.9.refs_10_), channel_id=1, source_target_pairs={{0,1},{1,0},{2,3},{3,2},{4,5},{5,4},{6,7},{7,6},{8,9},{9,8},{10,11... | collective-permute-start | bytes 1363976 | tf_op jit(solution)/shard_map/ppermute | solution.py:98
  36.8 14.5 %collective-permute-start.12 = (bf16[48,4736]{1,0:T(8,128)(2,1)S(1)}, bf16[48,4736]{1,0:T(8,128)(2,1)S(1)}, u32[]{:S(2)}, u32[]{:S(2)}) collective-permute-start(bf16[48,4736]{1,0:T(8,128)(2,1)S(1)} %collective-permute-done.8.refs_9_), channel_id=1, source_target_pairs={{0,1},{1,0},{2,3},{3,2},{4,5},{5,4},{6,7},{7,6},{8,9},{9,8},{10,11... | collective-permute-start | bytes 1363976 | tf_op jit(solution)/shard_map/ppermute | solution.py:98
  36.8 14.5 %collective-permute-start.11 = (bf16[48,4736]{1,0:T(8,128)(2,1)S(1)}, bf16[48,4736]{1,0:T(8,128)(2,1)S(1)}, u32[]{:S(2)}, u32[]{:S(2)}) collective-permute-start(bf16[48,4736]{1,0:T(8,128)(2,1)S(1)} %collective-permute-done.7.refs_8_), channel_id=1, source_target_pairs={{0,1},{1,0},{2,3},{3,2},{4,5},{5,4},{6,7},{7,6},{8,9},{9,8},{10,11... | collective-permute-start | bytes 1363976 | tf_op jit(solution)/shard_map/ppermute | solution.py:98
  69.0 5.4 %collective-permute-start.14 = (bf16[4,48,3456]{2,1,0:T(8,128)(2,1)S(1)}, bf16[4,48,3456]{2,1,0:T(8,128)(2,1)S(1)}, u32[]{:S(2)}, u32[]{:S(2)}) collective-permute-start(bf16[4,48,3456]{2,1,0:T(8,128)(2,1)S(1)} %get-tuple-element.120), channel_id=1, source_target_pairs={{0,1},{1,0},{2,3},{3,2},{4,5},{5,4},{6,7},{7,6},{8,9},{9,8},{10,11... | collective-permute-start | bytes 3981320 | tf_op jit(solution)/shard_map/ppermute | solution.py:98
  76.8 15.5 %all-to-all-start.1 = ((bf16[16,16,512]{2,1,0:T(8,128)(2,1)}), bf16[16,16,512]{2,1,0:T(8,128)(2,1)S(1)}, u32[]{:S(2)}, u32[]{:S(2)}) async-start(bf16[16,16,512]{2,1,0:T(8,128)(2,1)} %get-tuple-element.133), calls=%async_computation.1 | async-start | bytes 524288 | tf_op jit(solution)/shard_map/all_to_all | solution.py:879
  86.5 9.3 %collective-permute-start.25 = (bf16[4,48,1280]{2,1,0:T(8,128)(2,1)S(1)}, bf16[4,48,1280]{2,1,0:T(8,128)(2,1)S(1)}, u32[]{:S(2)}, u32[]{:S(2)}) collective-permute-start(bf16[4,48,1280]{2,1,0:T(8,128)(2,1)S(1)} %get-tuple-element.151), channel_id=1, source_target_pairs={{0,1},{1,0},{2,3},{3,2},{4,5},{5,4},{6,7},{7,6},{8,9},{9,8},{10,11... | collective-permute-start | bytes 1474568 | tf_op jit(solution)/shard_map/ppermute | solution.py:98
  92.3 6.2 %collective-permute-start.18 = (bf16[16,16,512]{2,1,0:T(8,128)(2,1)S(1)}, bf16[16,16,512]{2,1,0:T(8,128)(2,1)S(1)}, u32[]{:S(2)}, u32[]{:S(2)}) collective-permute-start(bf16[16,16,512]{2,1,0:T(8,128)(2,1)S(1)} %all-to-all-done.1.refs_1_), channel_id=1, source_target_pairs={{0,1},{1,0},{2,3},{3,2},{4,5},{5,4},{6,7},{7,6},{8,9},{9,8},{10,11... | collective-permute-start | bytes 786440 | tf_op jit(solution)/shard_map/ppermute | solution.py:98
  92.3 20.1 %collective-permute-start.15 = (bf16[48,3456]{1,0:T(8,128)(2,1)S(1)}, bf16[48,3456]{1,0:T(8,128)(2,1)S(1)}, u32[]{:S(2)}, u32[]{:S(2)}) collective-permute-start(bf16[48,3456]{1,0:T(8,128)(2,1)S(1)} %get-tuple-element.130.refs_6_), channel_id=1, source_target_pairs={{0,2},{1,3},{2,0},{3,1},{4,6},{5,7},{6,4},{7,5},{8,10},{9,11},{10,... | collective-permute-start | bytes 995336 | tf_op jit(solution)/shard_map/ppermute | solution.py:98
  93.1 17.7 %collective-permute-start.16 = (bf16[48,3456]{1,0:T(8,128)(2,1)S(1)}, bf16[48,3456]{1,0:T(8,128)(2,1)S(1)}, u32[]{:S(2)}, u32[]{:S(2)}) collective-permute-start(bf16[48,3456]{1,0:T(8,128)(2,1)S(1)} %get-tuple-element.131), channel_id=1, source_target_pairs={{0,4},{1,5},{2,6},{3,7},{4,0},{5,1},{6,2},{7,3},{8,12},{9,13},{10,... | collective-permute-start | bytes 995336 | tf_op jit(solution)/shard_map/ppermute | solution.py:98
  93.8 18.6 %collective-permute-start.17 = (bf16[48,3456]{1,0:T(8,128)(2,1)S(1)}, bf16[48,3456]{1,0:T(8,128)(2,1)S(1)}, u32[]{:S(2)}, u32[]{:S(2)}) collective-permute-start(bf16[48,3456]{1,0:T(8,128)(2,1)S(1)} %get-tuple-element.132), channel_id=1, source_target_pairs={{0,6},{1,7},{2,4},{3,5},{4,2},{5,3},{6,0},{7,1},{8,14},{9,15},{10,... | collective-permute-start | bytes 995336 | tf_op jit(solution)/shard_map/ppermute | solution.py:98
  97.7 18.1 %collective-permute-start.26 = (bf16[48,1280]{1,0:T(8,128)(2,1)S(1)}, bf16[48,1280]{1,0:T(8,128)(2,1)S(1)}, u32[]{:S(2)}, u32[]{:S(2)}) collective-permute-start(bf16[48,1280]{1,0:T(8,128)(2,1)S(1)} %get-tuple-element.153), channel_id=1, source_target_pairs={{0,2},{1,3},{2,0},{3,1},{4,6},{5,7},{6,4},{7,5},{8,10},{9,11},{10,... | collective-permute-start | bytes 368648 | tf_op jit(solution)/shard_map/ppermute | solution.py:98
  98.5 19.3 %collective-permute-start.27 = (bf16[48,1280]{1,0:T(8,128)(2,1)S(1)}, bf16[48,1280]{1,0:T(8,128)(2,1)S(1)}, u32[]{:S(2)}, u32[]{:S(2)}) collective-permute-start(bf16[48,1280]{1,0:T(8,128)(2,1)S(1)} %get-tuple-element.154), channel_id=1, source_target_pairs={{0,4},{1,5},{2,6},{3,7},{4,0},{5,1},{6,2},{7,3},{8,12},{9,13},{10,... | collective-permute-start | bytes 368648 | tf_op jit(solution)/shard_map/ppermute | solution.py:98
  110.8 7.0 %collective-permute-start.28 = (bf16[48,1280]{1,0:T(8,128)(2,1)S(1)}, bf16[48,1280]{1,0:T(8,128)(2,1)S(1)}, u32[]{:S(2)}, u32[]{:S(2)}) collective-permute-start(bf16[48,1280]{1,0:T(8,128)(2,1)S(1)} %get-tuple-element.155), channel_id=1, source_target_pairs={{0,6},{1,7},{2,4},{3,5},{4,2},{5,3},{6,0},{7,1},{8,14},{9,15},{10,... | collective-permute-start | bytes 368648 | tf_op jit(solution)/shard_map/ppermute | solution.py:98
  113.4 10.1 %collective-permute-start.19 = (bf16[48,896]{1,0:T(8,128)(2,1)S(1)}, bf16[48,896]{1,0:T(8,128)(2,1)S(1)}, u32[]{:S(2)}, u32[]{:S(2)}) collective-permute-start(bf16[48,896]{1,0:T(8,128)(2,1)S(1)} %get-tuple-element.138), channel_id=1, source_target_pairs={{0,8},{8,0},{16,24},{24,16},{1,9},{9,1},{17,25},{25,17},{2,10},{10... | collective-permute-start | bytes 258056 | tf_op jit(solution)/shard_map/ppermute | solution.py:98
  114.3 13.5 %collective-permute-start.20 = (bf16[48,896]{1,0:T(8,128)(2,1)S(1)}, bf16[48,896]{1,0:T(8,128)(2,1)S(1)}, u32[]{:S(2)}, u32[]{:S(2)}) collective-permute-start(bf16[48,896]{1,0:T(8,128)(2,1)S(1)} %get-tuple-element.139), channel_id=1, source_target_pairs={{0,16},{8,24},{16,0},{24,8},{1,17},{9,25},{17,1},{25,9},{2,18},{10... | collective-permute-start | bytes 258056 | tf_op jit(solution)/shard_map/ppermute | solution.py:98
  115.8 12.0 %collective-permute-start.21 = (bf16[48,896]{1,0:T(8,128)(2,1)S(1)}, bf16[48,896]{1,0:T(8,128)(2,1)S(1)}, u32[]{:S(2)}, u32[]{:S(2)}) collective-permute-start(bf16[48,896]{1,0:T(8,128)(2,1)S(1)} %get-tuple-element.140), channel_id=1, source_target_pairs={{0,24},{8,16},{16,8},{24,0},{1,25},{9,17},{17,9},{25,1},{2,26},{10... | collective-permute-start | bytes 258056 | tf_op jit(solution)/shard_map/ppermute | solution.py:98
  117.9 25.1 %collective-permute-start.31 = (bf16[48,1280]{1,0:T(8,128)(2,1)S(1)}, bf16[48,1280]{1,0:T(8,128)(2,1)S(1)}, u32[]{:S(2)}, u32[]{:S(2)}) collective-permute-start(bf16[48,1280]{1,0:T(8,128)(2,1)S(1)} %add_convert_fusion.refs_1_), channel_id=1, source_target_pairs={{0,24},{8,16},{16,8},{24,0},{1,25},{9,17},{17,9},{25,1},{2,26},{10... | collective-permute-start | bytes 368648 | tf_op jit(solution)/shard_map/ppermute | solution.py:98
  119.8 23.2 %collective-permute-start.30 = (bf16[48,1280]{1,0:T(8,128)(2,1)S(1)}, bf16[48,1280]{1,0:T(8,128)(2,1)S(1)}, u32[]{:S(2)}, u32[]{:S(2)}) collective-permute-start(bf16[48,1280]{1,0:T(8,128)(2,1)S(1)} %add_convert_fusion.refs_1_), channel_id=1, source_target_pairs={{0,16},{8,24},{16,0},{24,8},{1,17},{9,25},{17,1},{25,9},{2,18},{10... | collective-permute-start | bytes 368648 | tf_op jit(solution)/shard_map/ppermute | solution.py:98
  119.8 13.9 %all-to-all-start.2 = ((bf16[8,64,128]{2,1,0:T(8,128)(2,1)}), bf16[8,64,128]{2,1,0:T(8,128)(2,1)S(1)}, u32[]{:S(2)}, u32[]{:S(2)}) async-start(bf16[8,64,128]{2,1,0:T(8,128)(2,1)} %get-tuple-element.156), calls=%async_computation.2 | async-start | bytes 262144 | tf_op jit(solution)/shard_map/all_to_all | solution.py:891
  127.9 6.5 %collective-permute-start.24 = (bf16[48,896]{1,0:T(8,128)(2,1)S(1)}, bf16[48,896]{1,0:T(8,128)(2,1)S(1)}, u32[]{:S(2)}, u32[]{:S(2)}) collective-permute-start(bf16[48,896]{1,0:T(8,128)(2,1)S(1)} %add_convert_fusion.1.refs_1_), channel_id=1, source_target_pairs={{0,24},{8,16},{16,8},{24,0},{1,25},{9,17},{17,9},{25,1},{2,26},{10... | collective-permute-start | bytes 258056 | tf_op jit(solution)/shard_map/ppermute | solution.py:98
  129.2 11.1 %collective-permute-start.23 = (bf16[48,896]{1,0:T(8,128)(2,1)S(1)}, bf16[48,896]{1,0:T(8,128)(2,1)S(1)}, u32[]{:S(2)}, u32[]{:S(2)}) collective-permute-start(bf16[48,896]{1,0:T(8,128)(2,1)S(1)} %add_convert_fusion.1.refs_1_), channel_id=1, source_target_pairs={{0,16},{8,24},{16,0},{24,8},{1,17},{9,25},{17,1},{25,9},{2,18},{10... | collective-permute-start | bytes 258056 | tf_op jit(solution)/shard_map/ppermute | solution.py:98
  133.6 7.2 %collective-permute-start.22 = (bf16[48,896]{1,0:T(8,128)(2,1)S(1)}, bf16[48,896]{1,0:T(8,128)(2,1)S(1)}, u32[]{:S(2)}, u32[]{:S(2)}) collective-permute-start(bf16[48,896]{1,0:T(8,128)(2,1)S(1)} %add_convert_fusion.1.refs_1_), channel_id=1, source_target_pairs={{0,8},{8,0},{16,24},{24,16},{1,9},{9,1},{17,25},{25,17},{2,10},{10... | collective-permute-start | bytes 258056 | tf_op jit(solution)/shard_map/ppermute | solution.py:98
  134.3 8.7 %collective-permute-start.29 = (bf16[48,1280]{1,0:T(8,128)(2,1)S(1)}, bf16[48,1280]{1,0:T(8,128)(2,1)S(1)}, u32[]{:S(2)}, u32[]{:S(2)}) collective-permute-start(bf16[48,1280]{1,0:T(8,128)(2,1)S(1)} %add_convert_fusion.refs_1_), channel_id=1, source_target_pairs={{0,8},{8,0},{16,24},{24,16},{1,9},{9,1},{17,25},{25,17},{2,10},{10... | collective-permute-start | bytes 368648 | tf_op jit(solution)/shard_map/ppermute | solution.py:98
  (65 other events, 439.1 us)

commit v3 on v2

--- a/solution.py
+++ b/solution.py
@@ -146,7 +146,7 @@
         scratch_shapes=list(scratch),
         compiler_params=pltpu.CompilerParams(vmem_limit_bytes=room * 2**20),
         cost_estimate=pl.CostEstimate(flops=int(micros * FLOPS_US), bytes_accessed=1_000_000, transcendentals=0),
-    )(*operands, *after)
+    )(*(pltpu.with_memory_space_constraint(x, pltpu.HBM) if p == "h" else x for x, p in zip(operands, places)), *after)
 
 
 HEAD = PIN + POUT
@@ -161,21 +161,26 @@
     return jnp.bitwise_xor(at[0], 2 * (n % 4) + n // 4)
 
 
+def shards_of(refs):
+    return list(refs[:5]) + [refs[5].at[n] for n in range(3)]
+
+
 def attention_forward(tsteps, lat, noi, plan, grid, weights, shares, place, after=()):
     images = lat.shape[0]
-    fast = len(weights) == 8
+    fast = len(weights) == 6
 
     def body(ts, at, lat_r, noi_r, plan_r, grid_r, share_r, *refs):
         if fast:
-            wq_r, head_r, head_s = refs[8], refs[9], refs[-1]
+            wq_r, head_r, head_s = refs[6], refs[7], refs[-1]
+            shards = shards_of(refs)
             for n in range(8):
                 owner = piece_owner(at, n)
                 rows = pl.ds(pl.multiple_of(owner * 48, 48), 48)
-                wq_r[rows, :] = refs[n][:, 0 : 3 * D]
-                head_s[owner] = refs[n][:, 3 * D : 3 * D + 48]
+                wq_r[rows, :] = shards[n][:, 0 : 3 * D]
+                head_s[owner] = shards[n][:, 3 * D : 3 * D + 48]
             for p in range(8):
                 head_r[:, p * 48 : (p + 1) * 48] = head_s[p]
-            refs = refs[10:-1]
+            refs = refs[8:-1]
         else:
             wq_r, head_r = refs[:2]
             refs = refs[2:]
@@ -243,6 +248,7 @@
 
 
 BLOCK = 384
+WIDE = 768
 
 
 def mlp_pass(noi, con, mod, h0_all, mix_all, head, weights, place, after=()):
@@ -250,19 +256,20 @@
     bend_scale = math.sqrt(2.0 / math.pi)
     share = 1.0 / (TOK_IMG * PIN)
 
-    fast = len(weights) == 8
+    fast = len(weights) == 6
 
     def body(at, noi_r, con_r, mod_r, h0_r, mix_r, head_r, *refs):
         if fast:
             wp_r, w1_r, w2_r = refs[-3:]
+            shards = shards_of(refs)
             for n in range(8):
                 owner = piece_owner(at, n)
                 rows = pl.ds(pl.multiple_of(owner * 48, 48), 48)
-                wp_r[rows, :] = refs[n][:, TAIL : TAIL + D]
-                w1_r[rows, :] = refs[n][:, TAIL + D : TAIL + D + FF]
+                wp_r[rows, :] = shards[n][:, TAIL : TAIL + D]
+                w1_r[rows, :] = shards[n][:, TAIL + D : TAIL + D + FF]
                 for b in range(4):
-                    w2_r[pl.ds(pl.multiple_of(owner * 192 + b * 48, 48), 48), :] = refs[n][:, TAIL + D + FF + b * D : TAIL + D + FF + (b + 1) * D]
-            refs = refs[8:-3]
+                    w2_r[pl.ds(pl.multiple_of(owner * 192 + b * 48, 48), 48), :] = shards[n][:, TAIL + D + FF + b * D : TAIL + D + FF + (b + 1) * D]
+            refs = refs[6:-3]
         else:
             wp_r, w1_r, w2_r = refs[:3]
             refs = refs[3:]
@@ -286,8 +293,8 @@
             tokens = slice(i * TOK_IMG, (i + 1) * TOK_IMG)
             mlp_r[tokens, :] = mlp
             outer = None
-            for b in range(FF // BLOCK):
-                cols = slice(b * BLOCK, (b + 1) * BLOCK)
+            for b in range(FF // WIDE):
+                cols = slice(b * WIDE, (b + 1) * WIDE)
                 x = dot(mlp, w1_r[:, cols])
                 sq = x * x
                 t = jnp.tanh(bend_scale * x * (1.0 + 0.044715 * sq))
@@ -323,8 +330,8 @@
             d_outer = (m(5) * d_h2).astype(bf16)
             douter_r[tokens, :] = d_outer
             d_mlp = None
-            for b in range(FF // BLOCK):
-                cols = slice(b * BLOCK, (b + 1) * BLOCK)
+            for b in range(FF // WIDE):
+                cols = slice(b * WIDE, (b + 1) * WIDE)
                 d_in = (dot_nt(d_outer, w2_r[cols, :]) * slope_r[:, cols]).astype(bf16)
                 dinner_r[tokens, cols] = d_in
                 part = dot_nt(d_in, w1_r[:, cols])
@@ -392,18 +399,17 @@
 MOD_ROWS, MOD_LANES = 16, 512
 
 
-def attention_back(mod, h0_all, qkv_all, total_all, dmix_all, dh1_all, dmod_all, w_qkv, loss_tile, info, after=()):
-    images = mod.shape[0]
-
-    def body(mod_r, h0_r, qkv_r, total_r, dmix_r, dh1_r, dmod_in, wq_r, loss_r, *refs):
-        dqkv_r, dmod_r, dh0_r, line = refs[-4:]
+def heads_back(qkv_all, total_all, dmix_all, after=()):
+    images = qkv_all.shape[0]
+
+    def body(qkv_r, total_r, dmix_r, dqkv_r):
         for pair in range(HEADS // 2):
-            at = slice(pair * 128, pair * 128 + 128)
+            lanes = slice(pair * 128, pair * 128 + 128)
             for i in range(images):
                 q = qkv_r[i, :, pair * 128 : pair * 128 + 128]
                 k = qkv_r[i, :, D + pair * 128 : D + pair * 128 + 128]
                 v = qkv_r[i, :, 2 * D + pair * 128 : 2 * D + pair * 128 + 128]
-                do = dmix_r[i, :, at]
+                do = dmix_r[i, :, lanes]
                 dq = dk = dv = None
                 for half in range(2):
                     own = lane_half(q.shape, half)
@@ -421,6 +427,17 @@
                 rows = slice(i * TOK_IMG, (i + 1) * TOK_IMG)
                 for part, value in enumerate((dq * 0.125, dk * 0.125, dv)):
                     dqkv_r[rows, part * D + pair * 128 : part * D + pair * 128 + 128] = value.astype(bf16)
+
+    outs = [((images * TOK_IMG, 3 * D), bf16)]
+    return kernel_call(body, outs, (qkv_all, total_all, dmix_all), 4, after=after)[0]
+
+
+def attention_back(place, mod, h0_all, attn_all, dqkv, dh1_all, dmod_all, w_qkv, noisy_all, g_last, loss_tile, info, after=()):
+    images = mod.shape[0]
+
+    def body(at, mod_r, h0_r, attn_r, dqkv_r, dh1_r, dmod_in, wq_r, noisy_r, last_r, loss_r, *refs):
+        *g_refs, dmod_r, line = refs if info is None else refs[1:]
+        patch = None
         for i in range(images):
             rows = slice(i * TOK_IMG, (i + 1) * TOK_IMG)
             d_attn = None
@@ -432,7 +449,9 @@
             line[i : i + 1, 0:D] = jnp.sum(d_attn, axis=0, keepdims=True)
             line[i : i + 1, D : 2 * D] = jnp.sum(d_attn * norm, axis=0, keepdims=True)
             line[i : i + 1, 2 * D :] = dmod_in[i : i + 1, 2 * D :]
-            dh0_r[i] = (dh1_r[i] + norm_back(d_attn * (1.0 + mod_r[i : i + 1, D : 2 * D]), norm, inv)).astype(bf16)
+            d_h0 = (dh1_r[i] + norm_back(d_attn * (1.0 + mod_r[i : i + 1, D : 2 * D]), norm, inv)).astype(bf16)
+            piece = dot(noisy_r[i], d_h0)
+            patch = piece if patch is None else patch + piece
         if info is not None:
             each = 8 * D // MOD_LANES
             block = [line[i : i + 1, n * MOD_LANES : (n + 1) * MOD_LANES] for i in range(images) for n in range(each)]
@@ -445,46 +464,37 @@
             told = refs[0][INFO:BUNDLE, :].astype(f32)[0:1]
             block.append(jnp.concatenate([told, jnp.zeros((1, MOD_LANES - D), f32)], axis=1))
             block.append(jnp.zeros((MOD_ROWS - len(block), MOD_LANES), f32))
-            dmod_r[...] = jnp.concatenate(block, axis=0).astype(bf16)
+            block = jnp.concatenate(block, axis=0).astype(bf16)
+            for c in range(4):
+                dmod_r[c] = block
         else:
             dmod_r[...] = line[...].astype(bf16)
-
-    outs = [((images * TOK_IMG, 3 * D), bf16)]
-    outs += [((images, 8 * D) if info is None else (MOD_ROWS, MOD_LANES), bf16), ((images, TOK_IMG, D), bf16)]
-    ops = (mod, h0_all, qkv_all, total_all, dmix_all, dh1_all, dmod_all, w_qkv, loss_tile)
-    if info is not None:
-        ops += (info,)
-    return kernel_call(body, outs, ops, 7, scratch=[pltpu.VMEM((images, 8 * D), f32)], after=after)
-
-
-def tail_grad(attn_all, dqkv, noisy_all, dh0_all, g_last, place, fast, after=()):
-    images = noisy_all.shape[0]
-
-    def body(at, attn_r, dqkv_r, noisy_r, dh0_r, last_r, *refs):
         for part in range(3):
             cols = slice(part * D, (part + 1) * D)
             grad = dot_tn(attn_r[...], dqkv_r[:, cols])
-            if fast:
-                deal_rows(*refs[:2], grad, at[1], part * D)
+            if info is not None:
+                deal_rows(*g_refs, grad, at[1], part * D)
             else:
-                refs[0][:, cols] = grad
-        patch = None
-        for i in range(images):
-            piece = dot(noisy_r[i], dh0_r[i])
-            patch = piece if patch is None else patch + piece
+                g_refs[0][:, cols] = grad
         head = jnp.concatenate([patch, last_r[...]], axis=0)
-        if not fast:
-            refs[1][...] = head
+        if info is None:
+            g_refs[1][...] = head
             return
         none = jnp.zeros((HEAD, 128 - 48), f32)
         for c in range(4):
             left = jnp.concatenate([head[:, c * 96 : c * 96 + 48], none], axis=1)
             right = jnp.concatenate([head[:, c * 96 + 48 : c * 96 + 96], none], axis=1)
-            deal(*refs[:2], left, right, at[1], c, 3 * D)
-
-    outs = [((4, 48, TAIL), f32), ((4, 48, TAIL), bf16)] if fast else [((D, 3 * D), f32), ((HEAD, D), f32)]
-    ops = (place, attn_all.reshape(-1, D), dqkv, noisy_all, dh0_all, g_last)
-    return kernel_call(body, outs, ops, 2, places="s" + "v" * 5, after=after)
+            deal(*g_refs, left, right, at[1], c, 3 * D)
+
+    if info is None:
+        outs = [((D, 3 * D), f32), ((HEAD, D), f32), ((images, 8 * D), bf16)]
+    else:
+        outs = [((4, 48, TAIL), f32), ((4, 48, TAIL), bf16), ((4, MOD_ROWS, MOD_LANES), bf16)]
+    ops = (place, mod, h0_all, attn_all.reshape(-1, D), dqkv, dh1_all, dmod_all, w_qkv, noisy_all, g_last, loss_tile)
+    if info is not None:
+        ops += (info,)
+    scratch = [pltpu.VMEM((images, 8 * D), f32)]
+    return kernel_call(body, outs, ops, 4, scratch=scratch, places="s" + "v" * (len(ops) - 1), after=after)
 
 
 def bundle_rows(tsteps, labels, time1_w, time2_w):
@@ -587,19 +597,21 @@
     return kernel_call(body, outs, ops, 3, places="s" + "v" * 11, scratch=[pltpu.VMEM((parts, 128), f32)])
 
 
-def condition_back(place, own_mod, oth_mod, w1, w2, times, tab16, mod16, reps, parts, images):
-    groups = own_mod.shape[0]
-    devices = 2 * groups
+def condition_back(place, own_mod, oth_mod, w1, w2, times, tab16, mod16, passed, reps, parts, images):
+    devices = reps * parts
     count = devices * images
     own_t, own_d = TFREQ // parts, D // parts
     each = 8 * D // MOD_LANES
 
-    def body(at, own_r, oth_r, w1_r, w2_r, times_r, tab_r, mod_r, gm_r, gt_r, dc_r, loss_r, feat_r, act_r, slope_r, all_s, dmod_s):
-        for g in range(groups):
-            mine = pl.multiple_of((2 * g + at[1]) * MOD_ROWS, MOD_ROWS)
-            its = pl.multiple_of((2 * g + 1 - at[1]) * MOD_ROWS, MOD_ROWS)
-            all_s[pl.ds(mine, MOD_ROWS), :] = own_r[g]
-            all_s[pl.ds(its, MOD_ROWS), :] = oth_r[g]
+    def body(at, own_r, oth_r, w1_r, w2_r, times_r, tab_r, mod_r, in_r, gm_r, gt_r, dc_r, loss_r, feat_r, act_r, slope_r, out_r, all_s, dmod_s):
+        out_r[...] = in_r[...]
+        for r in range(reps):
+            block = slice(r * MOD_ROWS, (r + 1) * MOD_ROWS)
+            for c in range(parts // 2):
+                mine = pl.multiple_of((r * parts + 2 * c + at[1]) * MOD_ROWS, MOD_ROWS)
+                its = pl.multiple_of((r * parts + 2 * c + 1 - at[1]) * MOD_ROWS, MOD_ROWS)
+                all_s[pl.ds(mine, MOD_ROWS), :] = own_r[c, block, :]
+                all_s[pl.ds(its, MOD_ROWS), :] = oth_r[c, block, :]
         rows = all_s[...]
         take = one_hot((devices, devices * MOD_ROWS), lambda r, c: c == r * MOD_ROWS + images * each + 1)
         infos = dot(take, rows)
@@ -627,10 +639,10 @@
         gt_r[...] = dot_tn(high, picks) + (dot_tn(mid, picks) + dot_tn(low, picks))
 
     outs = [((own_d, 8 * D), f32), ((own_d, CLASSES), f32), ((parts, count, 128), bf16), ((8, 128), f32)]
-    outs += [((count, own_t), bf16), ((count, own_d), bf16), ((count, D), f32)]
-    ops = (place, own_mod, oth_mod, w1, w2, times, tab16, mod16)
+    outs += [((count, own_t), bf16), ((count, own_d), bf16), ((count, D), f32), (passed.shape, passed.dtype)]
+    ops = (place, own_mod, oth_mod, w1, w2, times, tab16, mod16, passed)
     scratch = [pltpu.VMEM((devices * MOD_ROWS, MOD_LANES), bf16), pltpu.VMEM((count, 8 * D), bf16)]
-    return kernel_call(body, outs, ops, 4, scratch=scratch, places="s" + "v" * 7)
+    return kernel_call(body, outs, ops, 4, scratch=scratch, places="s" + "v" * 8)
 
 
 def time_back(d_time, w2, act16, slope, feat16):
@@ -803,22 +815,57 @@
     return near + [flip(a, 1) for a in near]
 
 
-def chip_blocks(place, keep, sent, micros, spread=None, copies=0):
+def stacked_pieces(pieces, after=()):
+    def body(*refs):
+        for n, ref in enumerate(refs[:-1]):
+            refs[-1][n] = ref[...]
+
+    shape = (len(pieces),) + pieces[0].shape
+    return kernel_call(body, [(shape, pieces[0].dtype)], pieces, 1, after=after)[0]
+
+
+def chip_blocks(place, keep, sent, micros, after=()):
     def body(at, keep_r, sent_r, *refs):
-        if copies:
-            for c in range(copies):
-                refs[-1][c] = refs[0][...]
-            refs = refs[1:-1]
         for n, out in enumerate(refs):
             chip = jnp.bitwise_xor(at[0] // 2, n)
             out[...] = (keep_r[chip] + sent_r[chip].astype(f32)).astype(out.dtype)
 
     shape = keep.shape[1:]
-    outs, ops = [(shape, f32)] + [(shape, bf16)] * 3, (place, keep, sent)
-    if copies:
-        outs.append(((copies,) + spread.shape, spread.dtype))
-        ops += (spread,)
-    return kernel_call(body, outs, ops, micros, places="s" + "v" * (len(ops) - 1))
+    return kernel_call(body, [(shape, f32)] + [(shape, bf16)] * 3, (place, keep, sent), micros, places="svv", after=after)
+
+
+def tail_blocks(place, keep, sent, d_mods, after=()):
+    side = 4 * MOD_ROWS
+
+    def body(at, keep_r, sent_r, *refs):
+        outs, mods = refs[1:5], refs[5]
+        for n in range(4):
+            mods[n * MOD_ROWS : (n + 1) * MOD_ROWS, :] = refs[0][n]
+        for n, out in enumerate(outs):
+            chip = jnp.bitwise_xor(at[0] // 2, n)
+            value = (keep_r[chip] + sent_r[chip].astype(f32)).astype(out.dtype)
+            if n == 0:
+                out[...] = value
+                continue
+            out[0:48, 0:TAIL] = value
+            out[48:side, 0:TAIL] = jnp.zeros((side - 48, TAIL), bf16)
+            out[:, TAIL:] = mods[...]
+
+    outs = [((48, TAIL), f32)] + [((side, TAIL + MOD_LANES), bf16)] * 3 + [((side, MOD_LANES), bf16)]
+    return kernel_call(body, outs, (place, keep, sent, d_mods), 1, places="svvv", after=after)
+
+
+def tail_sum(place, own, arrived, mods, after=()):
+    def body(at, own_r, a, b, c, mod_r, out, all_r):
+        total = own_r[...] + a[0:48, 0:TAIL].astype(f32)
+        out[...] = (total + (b[0:48, 0:TAIL].astype(f32) + c[0:48, 0:TAIL].astype(f32))).astype(bf16)
+        chip = at[0] // 2
+        all_r[chip] = mod_r[...]
+        for n, ref in enumerate((a, b, c)):
+            all_r[jnp.bitwise_xor(chip, n + 1)] = ref[:, TAIL:]
+
+    outs = [((48, TAIL), bf16), ((4,) + mods.shape, bf16)]
+    return kernel_call(body, outs, (place, own, *arrived, mods), 1, places="svvvvv", after=after)
 
 
 Z_LANES = 384 + 384 + 128
@@ -839,11 +886,11 @@
     return kernel_call(body, outs, (place, *parts), 2, scratch=[pltpu.VMEM((4, 48, Z_LANES), f32)], places="svvvv", after=after)
 
 
-def chips_sum(blocks):
-    total = blocks[0]
-    for n in range(1, 4):
-        total = total + flip(blocks[n], 2 * n).astype(f32)
-    return total.astype(bf16)
+def four_sum(parts, after=()):
+    def body(a, b, c, d, out):
+        out[...] = ((a[...].astype(f32) + b[...].astype(f32)) + (c[...].astype(f32) + d[...].astype(f32))).astype(bf16)
+
+    return kernel_call(body, [(parts[0].shape, bf16)], parts, 1, after=after)[0]
 
 
 def other_copies(total):
@@ -860,9 +907,11 @@
     w_own, mod16, tab16, sums = cast_weights(
         patch_state, out_t, time1_w, time2_w, table_t, mod_w, qkv_w, proj_w, fc1_w, fc2_w, after=pieces[1:4]
     )
-    w_pieces = gather_pieces(w_own)
+    w_near = [flip(w_own, k) for k in (2, 4, 6)]
+    w_core = flip(w_own, 1)
     shares, w1, w2 = modulation_shares(place, pieces, times, tab16, mod16, images)
     shares = lax.all_to_all(shares, "fsdp", 0, 0)
+    w_pieces = [w_own, *w_near, w_core, flip(stacked_pieces(w_near, after=(shares,)), 1)]
 
     w_qkv, head, mod, con, noisy, hidden0, attn16, qkv16, totals, mixture16 = attention_forward(
         tsteps, latents, noise, plan, grid, w_pieces, shares, place
@@ -871,22 +920,23 @@
         noise, con, mod, hidden0, mixture16, head, w_pieces, place
     )
     send = flip(send, 1)
-    d_qkv16, d_mod16, d_h0 = attention_back(
-        mod, hidden0, qkv16, totals, d_mix16, d_h1, d_mod, w_qkv, loss_tile, bundle, after=(keep,)
+    d_qkv16 = heads_back(qkv16, totals, d_mix16, after=(keep,))
+    blocks = chip_blocks(place, keep, send, 2, after=(d_qkv16,))
+    q_keep, q_send, d_mod16 = attention_back(
+        place, mod, hidden0, attn16, d_qkv16, d_h1, d_mod, w_qkv, noisy, g_last, loss_tile, bundle, after=(blocks[1],)
     )
-    *blocks, d_mod16 = chip_blocks(place, keep, send, 2, d_mod16, reps * parts // 2)
-    everyone = [[r * parts + c * 2 + side for r in range(reps) for c in range(parts // 2)] for side in range(2)]
-    own_mod = lax.all_to_all(d_mod16, ("rep", "fsdp"), 0, 0, axis_index_groups=everyone)
+    q_send = flip(q_send, 1)
+    arrived = [flip(blocks[n], 2 * n) for n in range(1, 4)]
+    cuts = copy_blocks(place, [blocks[0]] + arrived)
+    q_own, *q_blocks, d_mods = tail_blocks(place, q_keep, q_send, lax.all_to_all(d_mod16, "rep", 0, 0), after=(cuts[1],))
+    q_sum, own_mod = tail_sum(place, q_own, [flip(q_blocks[n], 2 * (n + 1)) for n in range(3)], d_mods)
     oth_mod = flip(own_mod, 1)
-    keep, send = tail_grad(attn16, d_qkv16, noisy, d_h0, g_last, place, True, after=(blocks[1],))
-    send = flip(send, 1)
-    g_mod, g_table, d_time, loss, feat16, act16_t, time_slope = condition_back(
-        place, own_mod, oth_mod, w1, w2, times, tab16, mod16, reps, parts, images
+    g_mod, g_table, d_time, loss, feat16, act16_t, time_slope, q_sum = condition_back(
+        place, own_mod, oth_mod, w1, w2, times, tab16, mod16, q_sum, reps, parts, images
     )
-    cuts = copy_blocks(place, [blocks[0]] + [flip(blocks[n], 2 * n) for n in range(1, 4)], after=(loss,))
-    mid = (cuts[0] + flip(cuts[1], 1, "rep").astype(f32)) + (flip(cuts[2], 2, "rep").astype(f32) + flip(cuts[3], 3, "rep").astype(f32))
-    mid = other_copies(mid.astype(bf16))
-    tail = other_copies(chips_sum(chip_blocks(place, keep, send, 1)))
+    mid = four_sum([cuts[0]] + [flip(cuts[n], n, "rep") for n in range(1, 4)])
+    mid = other_copies(mid)
+    tail = other_copies(q_sum)
     gm, gf, pack = sums_early(place, mid)
     d_time = lax.all_to_all(d_time, "fsdp", 0, 0)
     pack = sums_middle(pack, g_table, g_mod, sums, loss)
@@ -995,10 +1045,9 @@
         noise, con, mod, hidden0, mixture16, head, (w_proj, w_fc1, w_fc2), place
     )
     loss_part = loss_tile[0, 0]
-    d_qkv16, d_mod16, d_h0 = attention_back(
-        mod, hidden0, qkv16, totals, d_mix16, d_h1, d_mod, w_qkv, loss_tile, None
+    g_tail, g_head, d_mod16 = attention_back(
+        place, mod, hidden0, attn16, heads_back(qkv16, totals, d_mix16), d_h1, d_mod, w_qkv, noisy, g_last, loss_tile, None
     )
-    g_tail, g_head = tail_grad(attn16, d_qkv16, noisy, d_h0, g_last, place, False)
 
     d_mod_all = rep_gather(d_mod16).reshape(1, -1)
     d_mod_all = gather_rows(d_mod_all).reshape(parts, reps, images, 8 * D)

time: 165 us -> 146 us (0.88)
  waiting for transfers between devices: 41.3 us -> 26.4 us
  blocking collectives: 26.1 us -> 35 us
  local copies, waits for them, and re-layouts: 14.1 us -> 6.44 us
  starting transfers between devices: 43 us -> 37.5 us
    ppermute x32 -> x30, waiting for transfers between devices: 35.7 us -> 21.7 us  [flip(): return lax.ppermute(x, axis, [(i, i ^ bit) for i in range(size)])]
    all_to_all x1, blocking collectives: 8.73 us -> 19 us  [eight_by_four(): shares = lax.all_to_all(shares, 'fsdp', 0, 0)]
    unnamed x126 -> x94, local copies, waits for them, and re-layouts: 14.1 us -> 6.44 us
    all_to_all x1, waiting for transfers between devices: 5.57 us -> 0.01 us  [eight_by_four(): lax.all_to_all(d_mod16, 'rep', 0, 0)]
    ppermute x32 -> x30, starting transfers between devices: 34.3 us -> 29.2 us  [flip(): return lax.ppermute(x, axis, [(i, i ^ bit) for i in range(size)])]
    all_to_all x1, waiting for transfers between devices: 0.01 us -> 4.72 us  [eight_by_four(): d_time = lax.all_to_all(d_time, 'fsdp', 0, 0)]
    pallas_call x17 -> x20, Pallas kernels: 38.5 us -> 38.7 us  [kernel_call(): pl.pallas_call(run, out_shape=[jax.ShapeDtypeStruct(s, t) for s, t in out...]
  transfers between devices with their start and end apart: 34 -> 32, of which waited for: 13 -> 11; matrix products, arithmetic and copies ran while one was open for 0% -> 0% of each run, Pallas kernels for 9% -> 10%
where the time goes in v3:
time: 146 us; the launch traced here: 145 us
  Pallas kernels  38.7 us (27%)
  starting transfers between devices  37.5 us (26%)
  blocking collectives  35 us (24%)
  waiting for transfers between devices  26.4 us (18%)
  local copies, waits for them, and re-layouts  6.44 us (4%)
    pallas_call x20, Pallas kernels, kernel_call(): pl.pallas_call(run, out_shape=[jax.ShapeDtypeStruct(s, t) for s, t in out...  38.7 us
    ppermute x30, starting transfers between devices, flip(): return lax.ppermute(x, axis, [(i, i ^ bit) for i in range(size)])  29.2 us
    ppermute x30, waiting for transfers between devices, flip(): return lax.ppermute(x, axis, [(i, i ^ bit) for i in range(size)])  21.7 us
    all_to_all x1, blocking collectives, eight_by_four(): shares = lax.all_to_all(shares, 'fsdp', 0, 0)  19 us
    all_gather x1, blocking collectives, gather_rows(): return lax.all_gather(x, 'fsdp', axis=0, tiled=True)  8.62 us
    all_to_all x1, blocking collectives, eight_by_four(): usq = lax.all_to_all(usq, 'fsdp', 0, 0)  7.4 us
    unnamed x94, local copies, waits for them, and re-layouts  6.44 us
    all_to_all x1, starting transfers between devices, eight_by_four(): lax.all_to_all(d_mod16, 'rep', 0, 0)  4.86 us
  transfers between devices with their start and end apart: 32, of which 11 were waited for; matrix products, arithmetic and copies ran while one was open for 0% of the time, Pallas kernels for 10%

profile of v3, /device:TPU:0, one launch (start us, length us, event | category | flops | bytes accessed | tf_op | source)
XLA Modules:
  0.0 145.5 jit_solution(1663932591835898790)
XLA Ops:
  2.4 3.5 %collective-permute-start.2 = (bf16[96,384]{1,0:T(8,128)(2,1)S(1)}, bf16[96,384]{1,0:T(8,128)(2,1)S(1)}, u32[]{:S(2)}, u32[]{:S(2)}) collective-permute-start(bf16[96,384]{1,0:T(8,128)(2,1)S(1)} %shard_map.392.refs_1_.refs_11_), channel_id=1, source_target_pairs={{0,6},{1,7},{2,4},{3,5},{4,2},{5,3},{6,0},{7,1},{8,14},{9,15},{10,... | collective-permute-start | bytes 221192 | tf_op jit(solution)/shard_map/ppermute | solution.py:98
  6.6 2.1 %collective-permute-done.2.refs_12_.refs_4_ = bf16[96,384]{1,0:T(8,128)(2,1)S(1)} collective-permute-done((bf16[96,384]{1,0:T(8,128)(2,1)S(1)}, bf16[96,384]{1,0:T(8,128)(2,1)S(1)}, u32[]{:S(2)}, u32[]{:S(2)}) %collective-permute-start.2) | collective-permute-done | bytes 73760 | tf_op jit(solution)/shard_map/ppermute | solution.py:98
  8.8 1.6 %collective-permute-done.1.refs_11_.refs_3_ = bf16[96,384]{1,0:T(8,128)(2,1)S(1)} collective-permute-done((bf16[96,384]{1,0:T(8,128)(2,1)S(1)}, bf16[96,384]{1,0:T(8,128)(2,1)S(1)}, u32[]{:S(2)}, u32[]{:S(2)}) %collective-permute-start.1) | collective-permute-done | bytes 73760 | tf_op jit(solution)/shard_map/ppermute | solution.py:98
  11.3 1.8 %collective-permute-start.9 = (bf16[48,4736]{1,0:T(8,128)(2,1)S(1)}, bf16[48,4736]{1,0:T(8,128)(2,1)S(1)}, u32[]{:S(2)}, u32[]{:S(2)}) collective-permute-start(bf16[48,4736]{1,0:T(8,128)(2,1)S(1)} %get-tuple-element.114.refs_7_), channel_id=1, source_target_pairs={{0,6},{1,7},{2,4},{3,5},{4,2},{5,3},{6,0},{7,1},{8,14},{9,15},{10,... | collective-permute-start | bytes 1363976 | tf_op jit(solution)/shard_map/ppermute | solution.py:98
  13.1 1.4 collective-permute-start.8
  14.8 1.6 %shard_map.394 = (f32[8,8,768]{2,1,0:T(8,128)S(1)}, bf16[256,384]{1,0:T(8,128)(2,1)S(1)}, bf16[384,384]{1,0:T(8,128)(2,1)S(1)}) custom-call(s32[3]{0:T(128)S(1)} %pad_add_fusion.refs_0_.refs_1_, bf16[96,384]{1,0:T(8,128)(2,1)S(1)} %shard_map.392.refs_1_.refs_11_, bf16[96,384]{1,0:T(8,128)(2,1)S(1)} %collective-permute-done.refs_10_.refs_2_, ...), custom_call_target="tpu_custom_call" | custom-call | flops 3449999872 | bytes 1000000 | tf_op jit(solution)/shard_map/pallas_call | solution.py:141
  17.9 19.0 %all_to_all.20.refs_3_.refs_6_ = f32[8,8,768]{2,1,0:T(8,128)S(1)} all-to-all(f32[8,8,768]{2,1,0:T(8,128)S(1)} %get-tuple-element.113), channel_id=1, replica_groups=mesh['rep'=4,'fsdp'=8] {'fsdp'}, dimensions={0} | all-to-all | bytes 393216 | tf_op jit(solution)/shard_map/all_to_all | solution.py:913
  37.6 3.3 %collective-permute-done.10.refs_11_ = bf16[48,4736]{1,0:T(8,128)(2,1)S(1)} collective-permute-done((bf16[48,4736]{1,0:T(8,128)(2,1)S(1)}, bf16[48,4736]{1,0:T(8,128)(2,1)S(1)}, u32[]{:S(2)}, u32[]{:S(2)}) %collective-permute-start.10) | collective-permute-done | bytes 454688 | tf_op jit(solution)/shard_map/ppermute | solution.py:98
  40.9 5.0 %shard_map.396 = (bf16[384,1152]{1,0:T(8,128)(2,1)S(1)}, bf16[48,384]{1,0:T(8,128)(2,1)S(1)}, f32[2,3072]{1,0:T(2,128)S(1)}, f32[2,8]{1,0:T(2,128)S(1)}, bf16[2,...) custom-call(s32[2]{0:T(128)S(1)} %bitcast.28, ...), custom_call_target="tpu_custom_call" | custom-call | flops 9200000000 | bytes 1000000 | tf_op jit(solution)/shard_map/pallas_call | solution.py:141
  45.9 10.3 %shard_map.397 = (f32[4,48,3456]{2,1,0:T(8,128)S(1)}, bf16[4,48,3456]{2,1,0:T(8,128)(2,1)S(1)}, f32[32,384]{1,0:T(8,128)S(1)}, bf16[2,256,384]{2,1,0:T(8,128)(2,...) custom-call(s32[3]{0:T(128)S(1)} %pad_add_fusion.refs_0_.refs_1_, ...), custom_call_target="tpu_custom_call" | custom-call | flops 14949999616 | bytes 1000000 | tf_op jit(solution)/shard_map/pallas_call | solution.py:141
  56.4 4.4 %shard_map.398.refs_3_.refs_4_ = bf16[512,1152]{1,0:T(8,128)(2,1)S(1)} custom-call(bf16[2,256,1152]{2,1,0:T(8,128)(2,1)S(1)} %get-tuple-element.122.refs_0_, f32[2,256,128]{2,1,0:T(8,128)S(1)} %get-tuple-element.123.refs_1_, bf16[2,256,384]{2,1,0:T(8,128)(2,1)S(1)} %get-tuple-element.124.refs_2_, f32[4,48,3456]{2,1,0:T(8,128)S(1)} %get-tuple-element.120.refs_3_.refs_1_), custom_call_target="tpu_custom_call" | custom-call | flops 4600000000 | bytes 1000000 | tf_op jit(solution)/shard_map/pallas_call | solution.py:141
  60.8 1.5 %shard_map.399 = (f32[48,3456]{1,0:T(8,128)S(1)}, bf16[48,3456]{1,0:T(8,128)(2,1)S(1)}, bf16[48,3456]{1,0:T(8,128)(2,1)}, bf16[48,3456]{1,0:T(8,128)(2,1)S(1)}) custom-call(s32[3]{0:T(128)S(1)} %pad_add_fusion.refs_0_.refs_1_, f32[4,48,3456]{2,1,0:T(8,128)S(1)} %get-tuple-element.120.refs_3_.refs_1_, ...), custom_call_target="tpu_custom_call" | custom-call | flops 2300000000 | bytes 1000000 | tf_op jit(solution)/shard_map/pallas_call | solution.py:141
  63.1 1.5 %collective-permute-start.14 = (bf16[48,3456]{1,0:T(8,128)(2,1)}, bf16[48,3456]{1,0:T(8,128)(2,1)S(1)}, u32[]{:S(2)}, u32[]{:S(2)}) collective-permute-start(bf16[48,3456]{1,0:T(8,128)(2,1)} %get-tuple-element.127), channel_id=1, source_target_pairs={{0,4},{1,5},{2,6},{3,7},{4,0},{5,1},{6,2},{7,3},{8,12},{9,13},{10,... | collective-permute-start | bytes 995336 | tf_op jit(solution)/shard_map/ppermute | solution.py:98
  66.6 3.0 %shard_map.403 = (f32[4,48,1280]{2,1,0:T(8,128)S(1)}, bf16[4,48,1280]{2,1,0:T(8,128)(2,1)S(1)}, bf16[4,16,512]{2,1,0:T(8,128)(2,1)}) custom-call(s32[3]{0:T(128)S(1)} %pad_add_fusion.refs_0_.refs_1_, f32[2,3072]{1,0:T(2,128)S(1)} %get-tuple-element.116.refs_3_.refs_1_, f32[2,256,384]{2,1,0:T(8,128)S(1)} %get-tuple-element.117.refs_4_.refs_2_, ...), custom_call_target="tpu_custom_call" | custom-call | flops 4600000000 | bytes 1000000 | tf_op jit(solution)/shard_map/pallas_call | solution.py:141
  70.6 4.9 %all-to-all-start.1 = ((bf16[4,16,512]{2,1,0:T(8,128)(2,1)}), bf16[4,16,512]{2,1,0:T(8,128)(2,1)S(1)}, u32[]{:S(2)}, u32[]{:S(2)}) async-start(bf16[4,16,512]{2,1,0:T(8,128)(2,1)} %get-tuple-element.143), calls=%async_computation.1 | async-start | bytes 131072 | tf_op jit(solution)/shard_map/all_to_all | solution.py:931
  75.4 5.1 %collective-permute-done.14.refs_3_ = bf16[48,3456]{1,0:T(8,128)(2,1)S(1)} collective-permute-done((bf16[48,3456]{1,0:T(8,128)(2,1)}, bf16[48,3456]{1,0:T(8,128)(2,1)S(1)}, u32[]{:S(2)}, u32[]{:S(2)}) %collective-permute-start.14) | collective-permute-done | bytes 331808 | tf_op jit(solution)/shard_map/ppermute | solution.py:98
  84.2 2.6 %collective-permute-start.17 = (bf16[48,896]{1,0:T(8,128)(2,1)S(1)}, bf16[48,896]{1,0:T(8,128)(2,1)S(1)}, u32[]{:S(2)}, u32[]{:S(2)}) collective-permute-start(bf16[48,896]{1,0:T(8,128)(2,1)S(1)} %get-tuple-element.131), channel_id=1, source_target_pairs={{0,16},{8,24},{16,0},{24,8},{1,17},{9,25},{17,1},{25,9},{2,18},{10... | collective-permute-start | bytes 258056 | tf_op jit(solution)/shard_map/ppermute | solution.py:98
  88.6 1.4 collective-permute-start.23
  92.2 1.3 collective-permute-start.18
  93.8 4.9 %collective-permute-done.18.refs_3_ = bf16[48,896]{1,0:T(8,128)(2,1)S(1)} collective-permute-done((bf16[48,896]{1,0:T(8,128)(2,1)S(1)}, bf16[48,896]{1,0:T(8,128)(2,1)S(1)}, u32[]{:S(2)}, u32[]{:S(2)}) %collective-permute-start.18) | collective-permute-done | bytes 86048 | tf_op jit(solution)/shard_map/ppermute | solution.py:98
  99.0 1.9 %collective-permute-start.21 = (bf16[48,896]{1,0:T(8,128)(2,1)S(1)}, bf16[48,896]{1,0:T(8,128)(2,1)S(1)}, u32[]{:S(2)}, u32[]{:S(2)}) collective-permute-start(bf16[48,896]{1,0:T(8,128)(2,1)S(1)} %shard_map.401.refs_1_), channel_id=1, source_target_pairs={{0,24},{8,16},{16,8},{24,0},{1,25},{9,17},{17,9},{25,1},{2,26},{10... | collective-permute-start | bytes 258056 | tf_op jit(solution)/shard_map/ppermute | solution.py:98
  100.8 2.6 %collective-permute-start.19 = (bf16[48,896]{1,0:T(8,128)(2,1)S(1)}, bf16[48,896]{1,0:T(8,128)(2,1)S(1)}, u32[]{:S(2)}, u32[]{:S(2)}) collective-permute-start(bf16[48,896]{1,0:T(8,128)(2,1)S(1)} %shard_map.401.refs_1_), channel_id=1, source_target_pairs={{0,8},{8,0},{16,24},{24,16},{1,9},{9,1},{17,25},{25,17},{2,10},{10... | collective-permute-start | bytes 258056 | tf_op jit(solution)/shard_map/ppermute | solution.py:98
  105.4 1.8 %collective-permute-done.20.refs_3_ = bf16[48,896]{1,0:T(8,128)(2,1)S(1)} collective-permute-done((bf16[48,896]{1,0:T(8,128)(2,1)S(1)}, bf16[48,896]{1,0:T(8,128)(2,1)S(1)}, u32[]{:S(2)}, u32[]{:S(2)}) %collective-permute-start.20) | collective-permute-done | bytes 86048 | tf_op jit(solution)/shard_map/ppermute | solution.py:98
  108.6 2.9 %shard_map.406 = (f32[48,3072]{1,0:T(8,128)S(1)}, f32[48,1001]{1,0:T(8,128)S(1)}, bf16[8,64,128]{2,1,0:T(8,128)(2,1)}, f32[8,128]{1,0:T(8,128)S(1)}, bf16[64,32]...) custom-call(s32[3]{0:T(128)S(1)} %pad_add_fusion.refs_0_.refs_1_, ...), custom_call_target="tpu_custom_call" | custom-call | flops 4600000000 | bytes 1000000 | tf_op jit(solution)/shard_map/pallas_call | solution.py:141
  111.5 1.8 %collective-permute-start.29 = (bf16[48,1280]{1,0:T(8,128)(2,1)S(1)}, bf16[48,1280]{1,0:T(8,128)(2,1)S(1)}, u32[]{:S(2)}, u32[]{:S(2)}) collective-permute-start(bf16[48,1280]{1,0:T(8,128)(2,1)S(1)} %get-tuple-element.157.refs_1_), channel_id=1, source_target_pairs={{0,24},{8,16},{16,8},{24,0},{1,25},{9,17},{17,9},{25,1},{2,26},{10... | collective-permute-start | bytes 368648 | tf_op jit(solution)/shard_map/ppermute | solution.py:98
  113.7 2.2 %collective-permute-start.27 = (bf16[48,1280]{1,0:T(8,128)(2,1)S(1)}, bf16[48,1280]{1,0:T(8,128)(2,1)S(1)}, u32[]{:S(2)}, u32[]{:S(2)}) collective-permute-start(bf16[48,1280]{1,0:T(8,128)(2,1)S(1)} %get-tuple-element.157.refs_1_), channel_id=1, source_target_pairs={{0,8},{8,0},{16,24},{24,16},{1,9},{9,1},{17,25},{25,17},{2,10},{10... | collective-permute-start | bytes 368648 | tf_op jit(solution)/shard_map/ppermute | solution.py:98
  115.9 3.4 %all-to-all-start.2 = ((bf16[8,64,128]{2,1,0:T(8,128)(2,1)}), bf16[8,64,128]{2,1,0:T(8,128)(2,1)S(1)}, u32[]{:S(2)}, u32[]{:S(2)}) async-start(bf16[8,64,128]{2,1,0:T(8,128)(2,1)} %get-tuple-element.158), calls=%async_computation.2 | async-start | bytes 262144 | tf_op jit(solution)/shard_map/all_to_all | solution.py:941
  120.0 4.7 %all-to-all-done.2.refs_0_ = bf16[8,64,128]{2,1,0:T(8,128)(2,1)S(1)} async-done(((bf16[8,64,128]{2,1,0:T(8,128)(2,1)}), bf16[8,64,128]{2,1,0:T(8,128)(2,1)S(1)}, u32[]{:S(2)}, u32[]{:S(2)}) %all-to-all-start.2) | async-done | bytes 131104 | tf_op jit(solution)/shard_map/all_to_all | solution.py:941
  125.8 8.6 %all_gather.3 = f32[256,384]{1,0:T(8,128)S(1)} all-gather(f32[32,384]{1,0:T(8,128)S(1)} %get-tuple-element.164), channel_id=1, replica_groups=mesh['rep'=4,'fsdp'=8] {'fsdp'}, dimensions={0}, use_global_device_ids=true | all-gather | bytes 442368 | tf_op jit(solution)/shard_map/all_gather | solution.py:121
  134.5 2.0 %shard_map.410 = (f32[640]{0:T(1024)}, f32[768]{0:T(1024)}, f32[1385]{0:T(1024)}, f32[3456]{0:T(1024)}, f32[1536]{0:T(1024)}, /*index=5*/f32[768]{0:T(1024)}, f3...) custom-call(s32[3]{0:T(128)S(1)} %pad_add_fusion.refs_0_.refs_1_, ...), custom_call_target="tpu_custom_call" | custom-call | flops 4024999936 | bytes 1000000 | tf_op jit(solution)/shard_map/pallas_call | solution.py:141
  136.5 7.4 %all_to_all.21.refs_0_ = f32[8,8,128]{2,1,0:T(8,128)S(1)} all-to-all(f32[8,8,128]{2,1,0:T(8,128)S(1)} %get-tuple-element.168), channel_id=1, replica_groups=mesh['rep'=4,'fsdp'=8] {'fsdp'}, dimensions={0} | all-to-all | bytes 65536 | tf_op jit(solution)/shard_map/all_to_all | solution.py:949
  144.0 1.5 %shard_map.411 = (f32[32,384]{1,0:T(8,128)}, f32[48,384]{1,0:T(8,128)}, f32[48,1001]{1,0:T(8,128)}, f32[48,3072]{1,0:T(8,128)}, f32[48,1152]{1,0:T(8,128)}, /*in...) custom-call(f32[8,8,128]{2,1,0:T(8,128)S(1)} %all_to_all.21.refs_0_,, ...), custom_call_target="tpu_custom_call" | custom-call | flops 4024999936 | bytes 1000000 | tf_op jit(solution)/shard_map/pallas_call | solution.py:141
  (150 shorter events, 23.2 us)
Async XLA Ops:
  1.9 11.2 %collective-permute-start.3 = (bf16[96,384]{1,0:T(8,128)(2,1)S(1)}, bf16[96,384]{1,0:T(8,128)(2,1)S(1)}, u32[]{:S(2)}, u32[]{:S(2)}) collective-permute-start(bf16[96,384]{1,0:T(8,128)(2,1)S(1)} %shard_map.392.refs_1_.refs_11_), channel_id=1, source_target_pairs={{0,1},{1,0},{2,3},{3,2},{4,5},{5,4},{6,7},{7,6},{8,9},{9,8},{10,11... | collective-permute-start | bytes 221192 | tf_op jit(solution)/shard_map/ppermute | solution.py:98
  2.4 6.4 %collective-permute-start.2 = (bf16[96,384]{1,0:T(8,128)(2,1)S(1)}, bf16[96,384]{1,0:T(8,128)(2,1)S(1)}, u32[]{:S(2)}, u32[]{:S(2)}) collective-permute-start(bf16[96,384]{1,0:T(8,128)(2,1)S(1)} %shard_map.392.refs_1_.refs_11_), channel_id=1, source_target_pairs={{0,6},{1,7},{2,4},{3,5},{4,2},{5,3},{6,0},{7,1},{8,14},{9,15},{10,... | collective-permute-start | bytes 221192 | tf_op jit(solution)/shard_map/ppermute | solution.py:98
  5.9 4.4 %collective-permute-start.1 = (bf16[96,384]{1,0:T(8,128)(2,1)S(1)}, bf16[96,384]{1,0:T(8,128)(2,1)S(1)}, u32[]{:S(2)}, u32[]{:S(2)}) collective-permute-start(bf16[96,384]{1,0:T(8,128)(2,1)S(1)} %shard_map.392.refs_1_.refs_11_), channel_id=1, source_target_pairs={{0,4},{1,5},{2,6},{3,7},{4,0},{5,1},{6,2},{7,3},{8,12},{9,13},{10,... | collective-permute-start | bytes 221192 | tf_op jit(solution)/shard_map/ppermute | solution.py:98
  6.4 4.4 %collective-permute-start = (bf16[96,384]{1,0:T(8,128)(2,1)S(1)}, bf16[96,384]{1,0:T(8,128)(2,1)S(1)}, u32[]{:S(2)}, u32[]{:S(2)}) collective-permute-start(bf16[96,384]{1,0:T(8,128)(2,1)S(1)} %shard_map.392.refs_1_.refs_11_), channel_id=1, source_target_pairs={{0,2},{1,3},{2,0},{3,1},{4,6},{5,7},{6,4},{7,5},{8,10},{9,11},{10,... | collective-permute-start | bytes 221192 | tf_op jit(solution)/shard_map/ppermute | solution.py:98
  8.8 5.7 %collective-permute-start.6 = (bf16[96,384]{1,0:T(8,128)(2,1)S(1)}, bf16[96,384]{1,0:T(8,128)(2,1)S(1)}, u32[]{:S(2)}, u32[]{:S(2)}) collective-permute-start(bf16[96,384]{1,0:T(8,128)(2,1)S(1)} %collective-permute-done.2.refs_12_.refs_4_), channel_id=1, source_target_pairs={{0,1},{1,0},{2,3},{3,2},{4,5},{5,4},{6,7},{7,6},{8,9},{9,8},{10,11... | collective-permute-start | bytes 221192 | tf_op jit(solution)/shard_map/ppermute | solution.py:98
  10.3 4.5 %collective-permute-start.5 = (bf16[96,384]{1,0:T(8,128)(2,1)S(1)}, bf16[96,384]{1,0:T(8,128)(2,1)S(1)}, u32[]{:S(2)}, u32[]{:S(2)}) collective-permute-start(bf16[96,384]{1,0:T(8,128)(2,1)S(1)} %collective-permute-done.1.refs_11_.refs_3_), channel_id=1, source_target_pairs={{0,1},{1,0},{2,3},{3,2},{4,5},{5,4},{6,7},{7,6},{8,9},{9,8},{10,11... | collective-permute-start | bytes 221192 | tf_op jit(solution)/shard_map/ppermute | solution.py:98
  10.8 4.1 %collective-permute-start.4 = (bf16[96,384]{1,0:T(8,128)(2,1)S(1)}, bf16[96,384]{1,0:T(8,128)(2,1)S(1)}, u32[]{:S(2)}, u32[]{:S(2)}) collective-permute-start(bf16[96,384]{1,0:T(8,128)(2,1)S(1)} %collective-permute-done.refs_10_.refs_2_), channel_id=1, source_target_pairs={{0,1},{1,0},{2,3},{3,2},{4,5},{5,4},{6,7},{7,6},{8,9},{9,8},{10,11... | collective-permute-start | bytes 221192 | tf_op jit(solution)/shard_map/ppermute | solution.py:98
  11.3 25.6 %collective-permute-start.9 = (bf16[48,4736]{1,0:T(8,128)(2,1)S(1)}, bf16[48,4736]{1,0:T(8,128)(2,1)S(1)}, u32[]{:S(2)}, u32[]{:S(2)}) collective-permute-start(bf16[48,4736]{1,0:T(8,128)(2,1)S(1)} %get-tuple-element.114.refs_7_), channel_id=1, source_target_pairs={{0,6},{1,7},{2,4},{3,5},{4,2},{5,3},{6,0},{7,1},{8,14},{9,15},{10,... | collective-permute-start | bytes 1363976 | tf_op jit(solution)/shard_map/ppermute | solution.py:98
  13.1 23.8 %collective-permute-start.8 = (bf16[48,4736]{1,0:T(8,128)(2,1)S(1)}, bf16[48,4736]{1,0:T(8,128)(2,1)S(1)}, u32[]{:S(2)}, u32[]{:S(2)}) collective-permute-start(bf16[48,4736]{1,0:T(8,128)(2,1)S(1)} %get-tuple-element.114.refs_7_), channel_id=1, source_target_pairs={{0,4},{1,5},{2,6},{3,7},{4,0},{5,1},{6,2},{7,3},{8,12},{9,13},{10,... | collective-permute-start | bytes 1363976 | tf_op jit(solution)/shard_map/ppermute | solution.py:98
  14.5 22.4 %collective-permute-start.7 = (bf16[48,4736]{1,0:T(8,128)(2,1)S(1)}, bf16[48,4736]{1,0:T(8,128)(2,1)S(1)}, u32[]{:S(2)}, u32[]{:S(2)}) collective-permute-start(bf16[48,4736]{1,0:T(8,128)(2,1)S(1)} %get-tuple-element.114.refs_7_), channel_id=1, source_target_pairs={{0,2},{1,3},{2,0},{3,1},{4,6},{5,7},{6,4},{7,5},{8,10},{9,11},{10,... | collective-permute-start | bytes 1363976 | tf_op jit(solution)/shard_map/ppermute | solution.py:98
  37.0 3.8 %collective-permute-start.11 = (bf16[3,48,4736]{2,1,0:T(8,128)(2,1)S(1)}, bf16[3,48,4736]{2,1,0:T(8,128)(2,1)S(1)}, u32[]{:S(2)}, u32[]{:S(2)}) collective-permute-start(bf16[3,48,4736]{2,1,0:T(8,128)(2,1)S(1)} %shard_map.395), channel_id=1, source_target_pairs={{0,1},{1,0},{2,3},{3,2},{4,5},{5,4},{6,7},{7,6},{8,9},{9,8},{10,11... | collective-permute-start | bytes 4091912 | tf_op jit(solution)/shard_map/ppermute | solution.py:98
  37.1 3.7 %collective-permute-start.10 = (bf16[48,4736]{1,0:T(8,128)(2,1)S(1)}, bf16[48,4736]{1,0:T(8,128)(2,1)S(1)}, u32[]{:S(2)}, u32[]{:S(2)}) collective-permute-start(bf16[48,4736]{1,0:T(8,128)(2,1)S(1)} %get-tuple-element.114.refs_7_), channel_id=1, source_target_pairs={{0,1},{1,0},{2,3},{3,2},{4,5},{5,4},{6,7},{7,6},{8,9},{9,8},{10,11... | collective-permute-start | bytes 1363976 | tf_op jit(solution)/shard_map/ppermute | solution.py:98
  56.2 4.6 %collective-permute-start.12 = (bf16[4,48,3456]{2,1,0:T(8,128)(2,1)S(1)}, bf16[4,48,3456]{2,1,0:T(8,128)(2,1)S(1)}, u32[]{:S(2)}, u32[]{:S(2)}) collective-permute-start(bf16[4,48,3456]{2,1,0:T(8,128)(2,1)S(1)} %get-tuple-element.121), channel_id=1, source_target_pairs={{0,1},{1,0},{2,3},{3,2},{4,5},{5,4},{6,7},{7,6},{8,9},{9,8},{10,11... | collective-permute-start | bytes 3981320 | tf_op jit(solution)/shard_map/ppermute | solution.py:98
  63.1 17.4 %collective-permute-start.14 = (bf16[48,3456]{1,0:T(8,128)(2,1)}, bf16[48,3456]{1,0:T(8,128)(2,1)S(1)}, u32[]{:S(2)}, u32[]{:S(2)}) collective-permute-start(bf16[48,3456]{1,0:T(8,128)(2,1)} %get-tuple-element.127), channel_id=1, source_target_pairs={{0,4},{1,5},{2,6},{3,7},{4,0},{5,1},{6,2},{7,3},{8,12},{9,13},{10,... | collective-permute-start | bytes 995336 | tf_op jit(solution)/shard_map/ppermute | solution.py:98
  64.6 15.9 %collective-permute-start.15 = (bf16[48,3456]{1,0:T(8,128)(2,1)S(1)}, bf16[48,3456]{1,0:T(8,128)(2,1)S(1)}, u32[]{:S(2)}, u32[]{:S(2)}) collective-permute-start(bf16[48,3456]{1,0:T(8,128)(2,1)S(1)} %get-tuple-element.128), channel_id=1, source_target_pairs={{0,6},{1,7},{2,4},{3,5},{4,2},{5,3},{6,0},{7,1},{8,14},{9,15},{10,... | collective-permute-start | bytes 995336 | tf_op jit(solution)/shard_map/ppermute | solution.py:98
  65.9 15.6 %collective-permute-start.13 = (bf16[48,3456]{1,0:T(8,128)(2,1)S(1)}, bf16[48,3456]{1,0:T(8,128)(2,1)S(1)}, u32[]{:S(2)}, u32[]{:S(2)}) collective-permute-start(bf16[48,3456]{1,0:T(8,128)(2,1)S(1)} %get-tuple-element.126.refs_12_), channel_id=1, source_target_pairs={{0,2},{1,3},{2,0},{3,1},{4,6},{5,7},{6,4},{7,5},{8,10},{9,11},{10,... | collective-permute-start | bytes 995336 | tf_op jit(solution)/shard_map/ppermute | solution.py:98
  70.6 16.2 %collective-permute-start.22 = (bf16[4,48,1280]{2,1,0:T(8,128)(2,1)S(1)}, bf16[4,48,1280]{2,1,0:T(8,128)(2,1)S(1)}, u32[]{:S(2)}, u32[]{:S(2)}) collective-permute-start(bf16[4,48,1280]{2,1,0:T(8,128)(2,1)S(1)} %get-tuple-element.142), channel_id=1, source_target_pairs={{0,1},{1,0},{2,3},{3,2},{4,5},{5,4},{6,7},{7,6},{8,9},{9,8},{10,11... | collective-permute-start | bytes 1474568 | tf_op jit(solution)/shard_map/ppermute | solution.py:98
  70.6 16.2 %all-to-all-start.1 = ((bf16[4,16,512]{2,1,0:T(8,128)(2,1)}), bf16[4,16,512]{2,1,0:T(8,128)(2,1)S(1)}, u32[]{:S(2)}, u32[]{:S(2)}) async-start(bf16[4,16,512]{2,1,0:T(8,128)(2,1)} %get-tuple-element.143), calls=%async_computation.1 | async-start | bytes 131072 | tf_op jit(solution)/shard_map/all_to_all | solution.py:931
  84.2 9.4 %collective-permute-start.17 = (bf16[48,896]{1,0:T(8,128)(2,1)S(1)}, bf16[48,896]{1,0:T(8,128)(2,1)S(1)}, u32[]{:S(2)}, u32[]{:S(2)}) collective-permute-start(bf16[48,896]{1,0:T(8,128)(2,1)S(1)} %get-tuple-element.131), channel_id=1, source_target_pairs={{0,16},{8,24},{16,0},{24,8},{1,17},{9,25},{17,1},{25,9},{2,18},{10... | collective-permute-start | bytes 258056 | tf_op jit(solution)/shard_map/ppermute | solution.py:98
  88.6 12.2 %collective-permute-start.23 = (bf16[64,1792]{1,0:T(8,128)(2,1)S(1)}, bf16[64,1792]{1,0:T(8,128)(2,1)S(1)}, u32[]{:S(2)}, u32[]{:S(2)}) collective-permute-start(bf16[64,1792]{1,0:T(8,128)(2,1)S(1)} %get-tuple-element.145), channel_id=1, source_target_pairs={{0,2},{1,3},{2,0},{3,1},{4,6},{5,7},{6,4},{7,5},{8,10},{9,11},{10,... | collective-permute-start | bytes 688136 | tf_op jit(solution)/shard_map/ppermute | solution.py:98
  90.0 13.4 %collective-permute-start.24 = (bf16[64,1792]{1,0:T(8,128)(2,1)S(1)}, bf16[64,1792]{1,0:T(8,128)(2,1)S(1)}, u32[]{:S(2)}, u32[]{:S(2)}) collective-permute-start(bf16[64,1792]{1,0:T(8,128)(2,1)S(1)} %get-tuple-element.146), channel_id=1, source_target_pairs={{0,4},{1,5},{2,6},{3,7},{4,0},{5,1},{6,2},{7,3},{8,12},{9,13},{10,... | collective-permute-start | bytes 688136 | tf_op jit(solution)/shard_map/ppermute | solution.py:98
  90.9 12.6 %collective-permute-start.25 = (bf16[64,1792]{1,0:T(8,128)(2,1)S(1)}, bf16[64,1792]{1,0:T(8,128)(2,1)S(1)}, u32[]{:S(2)}, u32[]{:S(2)}) collective-permute-start(bf16[64,1792]{1,0:T(8,128)(2,1)S(1)} %get-tuple-element.147), channel_id=1, source_target_pairs={{0,6},{1,7},{2,4},{3,5},{4,2},{5,3},{6,0},{7,1},{8,14},{9,15},{10,... | collective-permute-start | bytes 688136 | tf_op jit(solution)/shard_map/ppermute | solution.py:98
  92.2 6.4 %collective-permute-start.18 = (bf16[48,896]{1,0:T(8,128)(2,1)S(1)}, bf16[48,896]{1,0:T(8,128)(2,1)S(1)}, u32[]{:S(2)}, u32[]{:S(2)}) collective-permute-start(bf16[48,896]{1,0:T(8,128)(2,1)S(1)} %get-tuple-element.132), channel_id=1, source_target_pairs={{0,24},{8,16},{16,8},{24,0},{1,25},{9,17},{17,9},{25,1},{2,26},{10... | collective-permute-start | bytes 258056 | tf_op jit(solution)/shard_map/ppermute | solution.py:98
  93.5 5.4 %collective-permute-start.16 = (bf16[48,896]{1,0:T(8,128)(2,1)S(1)}, bf16[48,896]{1,0:T(8,128)(2,1)S(1)}, u32[]{:S(2)}, u32[]{:S(2)}) collective-permute-start(bf16[48,896]{1,0:T(8,128)(2,1)S(1)} %get-tuple-element.130.refs_4_), channel_id=1, source_target_pairs={{0,8},{8,0},{16,24},{24,16},{1,9},{9,1},{17,25},{25,17},{2,10},{10... | collective-permute-start | bytes 258056 | tf_op jit(solution)/shard_map/ppermute | solution.py:98
  99.0 6.4 %collective-permute-start.21 = (bf16[48,896]{1,0:T(8,128)(2,1)S(1)}, bf16[48,896]{1,0:T(8,128)(2,1)S(1)}, u32[]{:S(2)}, u32[]{:S(2)}) collective-permute-start(bf16[48,896]{1,0:T(8,128)(2,1)S(1)} %shard_map.401.refs_1_), channel_id=1, source_target_pairs={{0,24},{8,16},{16,8},{24,0},{1,25},{9,17},{17,9},{25,1},{2,26},{10... | collective-permute-start | bytes 258056 | tf_op jit(solution)/shard_map/ppermute | solution.py:98
  100.8 6.3 %collective-permute-start.20 = (bf16[48,896]{1,0:T(8,128)(2,1)S(1)}, bf16[48,896]{1,0:T(8,128)(2,1)S(1)}, u32[]{:S(2)}, u32[]{:S(2)}) collective-permute-start(bf16[48,896]{1,0:T(8,128)(2,1)S(1)} %shard_map.401.refs_1_), channel_id=1, source_target_pairs={{0,16},{8,24},{16,0},{24,8},{1,17},{9,25},{17,1},{25,9},{2,18},{10... | collective-permute-start | bytes 258056 | tf_op jit(solution)/shard_map/ppermute | solution.py:98
  100.8 6.3 %collective-permute-start.19 = (bf16[48,896]{1,0:T(8,128)(2,1)S(1)}, bf16[48,896]{1,0:T(8,128)(2,1)S(1)}, u32[]{:S(2)}, u32[]{:S(2)}) collective-permute-start(bf16[48,896]{1,0:T(8,128)(2,1)S(1)} %shard_map.401.refs_1_), channel_id=1, source_target_pairs={{0,8},{8,0},{16,24},{24,16},{1,9},{9,1},{17,25},{25,17},{2,10},{10... | collective-permute-start | bytes 258056 | tf_op jit(solution)/shard_map/ppermute | solution.py:98
  104.1 4.4 %collective-permute-start.26 = (bf16[4,64,512]{2,1,0:T(8,128)(2,1)S(1)}, bf16[4,64,512]{2,1,0:T(8,128)(2,1)S(1)}, u32[]{:S(2)}, u32[]{:S(2)}) collective-permute-start(bf16[4,64,512]{2,1,0:T(8,128)(2,1)S(1)} %get-tuple-element.149.refs_1_), channel_id=1, source_target_pairs={{0,1},{1,0},{2,3},{3,2},{4,5},{5,4},{6,7},{7,6},{8,9},{9,8},{10,11... | collective-permute-start | bytes 786440 | tf_op jit(solution)/shard_map/ppermute | solution.py:98
  111.5 13.7 %collective-permute-start.29 = (bf16[48,1280]{1,0:T(8,128)(2,1)S(1)}, bf16[48,1280]{1,0:T(8,128)(2,1)S(1)}, u32[]{:S(2)}, u32[]{:S(2)}) collective-permute-start(bf16[48,1280]{1,0:T(8,128)(2,1)S(1)} %get-tuple-element.157.refs_1_), channel_id=1, source_target_pairs={{0,24},{8,16},{16,8},{24,0},{1,25},{9,17},{17,9},{25,1},{2,26},{10... | collective-permute-start | bytes 368648 | tf_op jit(solution)/shard_map/ppermute | solution.py:98
  113.3 11.9 %collective-permute-start.28 = (bf16[48,1280]{1,0:T(8,128)(2,1)S(1)}, bf16[48,1280]{1,0:T(8,128)(2,1)S(1)}, u32[]{:S(2)}, u32[]{:S(2)}) collective-permute-start(bf16[48,1280]{1,0:T(8,128)(2,1)S(1)} %get-tuple-element.157.refs_1_), channel_id=1, source_target_pairs={{0,16},{8,24},{16,0},{24,8},{1,17},{9,25},{17,1},{25,9},{2,18},{10... | collective-permute-start | bytes 368648 | tf_op jit(solution)/shard_map/ppermute | solution.py:98
  113.7 11.5 %collective-permute-start.27 = (bf16[48,1280]{1,0:T(8,128)(2,1)S(1)}, bf16[48,1280]{1,0:T(8,128)(2,1)S(1)}, u32[]{:S(2)}, u32[]{:S(2)}) collective-permute-start(bf16[48,1280]{1,0:T(8,128)(2,1)S(1)} %get-tuple-element.157.refs_1_), channel_id=1, source_target_pairs={{0,8},{8,0},{16,24},{24,16},{1,9},{9,1},{17,25},{25,17},{2,10},{10... | collective-permute-start | bytes 368648 | tf_op jit(solution)/shard_map/ppermute | solution.py:98
  115.9 8.8 %all-to-all-start.2 = ((bf16[8,64,128]{2,1,0:T(8,128)(2,1)}), bf16[8,64,128]{2,1,0:T(8,128)(2,1)S(1)}, u32[]{:S(2)}, u32[]{:S(2)}) async-start(bf16[8,64,128]{2,1,0:T(8,128)(2,1)} %get-tuple-element.158), calls=%async_computation.2 | async-start | bytes 262144 | tf_op jit(solution)/shard_map/all_to_all | solution.py:941
  (47 other events, 321.4 us)

commit v4 on v3

--- a/solution.py
+++ b/solution.py
@@ -162,16 +162,17 @@
 
 
 def shards_of(refs):
-    return list(refs[:5]) + [refs[5].at[n] for n in range(3)]
+    own, near, core, far = refs[:4]
+    return [own] + [near.at[n] for n in range(3)] + [core] + [far.at[n] for n in range(3)]
 
 
 def attention_forward(tsteps, lat, noi, plan, grid, weights, shares, place, after=()):
     images = lat.shape[0]
-    fast = len(weights) == 6
+    fast = len(weights) == 4
 
     def body(ts, at, lat_r, noi_r, plan_r, grid_r, share_r, *refs):
         if fast:
-            wq_r, head_r, head_s = refs[6], refs[7], refs[-1]
+            wq_r, head_r, head_s = refs[4], refs[5], refs[-1]
             shards = shards_of(refs)
             for n in range(8):
                 owner = piece_owner(at, n)
@@ -180,7 +181,7 @@
                 head_s[owner] = shards[n][:, 3 * D : 3 * D + 48]
             for p in range(8):
                 head_r[:, p * 48 : (p + 1) * 48] = head_s[p]
-            refs = refs[8:-1]
+            refs = refs[6:-1]
         else:
             wq_r, head_r = refs[:2]
             refs = refs[2:]
@@ -256,7 +257,7 @@
     bend_scale = math.sqrt(2.0 / math.pi)
     share = 1.0 / (TOK_IMG * PIN)
 
-    fast = len(weights) == 6
+    fast = len(weights) == 4
 
     def body(at, noi_r, con_r, mod_r, h0_r, mix_r, head_r, *refs):
         if fast:
@@ -269,7 +270,7 @@
                 w1_r[rows, :] = shards[n][:, TAIL + D : TAIL + D + FF]
                 for b in range(4):
                     w2_r[pl.ds(pl.multiple_of(owner * 192 + b * 48, 48), 48), :] = shards[n][:, TAIL + D + FF + b * D : TAIL + D + FF + (b + 1) * D]
-            refs = refs[6:-3]
+            refs = refs[4:-3]
         else:
             wp_r, w1_r, w2_r = refs[:3]
             refs = refs[3:]
@@ -524,15 +525,19 @@
     return kernel_call(body, [((BUNDLE, D), bf16)], ops, 1.5, places="hhhh", scratch=scratch)[0]
 
 
+def lay_shard(w_r, pa, ou, qk, pr, f1, f2):
+    w_r[:, 0 : 3 * D] = qk[...].astype(bf16)
+    head = jnp.concatenate([pa[0], ou[0]], axis=0)
+    w_r[:, 3 * D : TAIL] = jnp.concatenate([head, jnp.zeros((HEAD, 128 - 48), f32)], axis=1).astype(bf16)
+    w_r[:, TAIL : TAIL + D] = pr[...].astype(bf16)
+    w_r[:, TAIL + D : TAIL + D + FF] = f1[...].astype(bf16)
+    for b in range(4):
+        w_r[:, TAIL + D + FF + b * D : TAIL + D + FF + (b + 1) * D] = f2[b * 48 : (b + 1) * 48, :].astype(bf16)
+
+
 def cast_weights(patch_state, out_t, time1_w, time2_w, table_t, mod_w, qkv_w, proj_w, fc1_w, fc2_w, after=()):
     def body(pa, ou, t1, t2, ta, mo, qk, pr, f1, f2, w_r, mod16, tab16, sums):
-        w_r[:, 0 : 3 * D] = qk[...].astype(bf16)
-        head = jnp.concatenate([pa[0], ou[0]], axis=0)
-        w_r[:, 3 * D : TAIL] = jnp.concatenate([head, jnp.zeros((HEAD, 128 - 48), f32)], axis=1).astype(bf16)
-        w_r[:, TAIL : TAIL + D] = pr[...].astype(bf16)
-        w_r[:, TAIL + D : TAIL + D + FF] = f1[...].astype(bf16)
-        for b in range(4):
-            w_r[:, TAIL + D + FF + b * D : TAIL + D + FF + (b + 1) * D] = f2[b * 48 : (b + 1) * 48, :].astype(bf16)
+        lay_shard(w_r, pa, ou, qk, pr, f1, f2)
         mod16[...] = mo[...].astype(bf16)
         tab16[...] = ta[...].astype(bf16)
         lane = lax.broadcasted_iota(jnp.int32, (8, D), 1)
@@ -815,13 +820,36 @@
     return near + [flip(a, 1) for a in near]
 
 
-def stacked_pieces(pieces, after=()):
-    def body(*refs):
-        for n, ref in enumerate(refs[:-1]):
-            refs[-1][n] = ref[...]
-
-    shape = (len(pieces),) + pieces[0].shape
-    return kernel_call(body, [(shape, pieces[0].dtype)], pieces, 1, after=after)[0]
+HALF = 2432
+
+
+def half_shard(place, patch_state, out_t, qkv_w, proj_w, fc1_w, fc2_w, after=()):
+    def body(at, pa, ou, qk, pr, f1, f2, out, all_s):
+        lay_shard(all_s, pa, ou, qk, pr, f1, f2)
+        for j in range(2):
+
+            @pl.when(at[2] % 2 == j)
+            def _():
+                out[...] = all_s[:, j * HALF : (j + 1) * HALF]
+
+    ops = (place, patch_state, out_t, qkv_w, proj_w, fc1_w, fc2_w)
+    scratch = [pltpu.VMEM((48, 2 * HALF), bf16)]
+    return kernel_call(body, [((48, HALF), bf16)], ops, 1, scratch=scratch, places="s" + "v" * 6, after=after)[0]
+
+
+def stacked_pieces(place, two, halves, after=()):
+    def body(at, x, y, a, b, out, cuts):
+        out[0] = x[...]
+        out[1] = y[...]
+        for n, ref in enumerate((a, b)):
+            cuts[jnp.bitwise_xor(at[2] % 2, n)] = ref[...]
+        for j in range(2):
+            size = min(HALF, SENT - j * HALF)
+            out[2, :, j * HALF : j * HALF + size] = cuts[j][:, 0:size]
+
+    ops = (place, *two, *halves)
+    scratch = [pltpu.VMEM((2, 48, HALF), bf16)]
+    return kernel_call(body, [((3, 48, SENT), bf16)], ops, 1, scratch=scratch, places="s" + "v" * 4, after=after)[0]
 
 
 def chip_blocks(place, keep, sent, micros, after=()):
@@ -907,11 +935,15 @@
     w_own, mod16, tab16, sums = cast_weights(
         patch_state, out_t, time1_w, time2_w, table_t, mod_w, qkv_w, proj_w, fc1_w, fc2_w, after=pieces[1:4]
     )
-    w_near = [flip(w_own, k) for k in (2, 4, 6)]
+    half = half_shard(place, patch_state, out_t, qkv_w, proj_w, fc1_w, fc2_w, after=(bundle,))
+    half = flip(half, 6)
+    halves = [half, flip(half, 1, "rep")]
+    w_two = [flip(w_own, k) for k in (2, 4)]
     w_core = flip(w_own, 1)
     shares, w1, w2 = modulation_shares(place, pieces, times, tab16, mod16, images)
     shares = lax.all_to_all(shares, "fsdp", 0, 0)
-    w_pieces = [w_own, *w_near, w_core, flip(stacked_pieces(w_near, after=(shares,)), 1)]
+    w_near = stacked_pieces(place, w_two, halves, after=(shares,))
+    w_pieces = [w_own, w_near, w_core, flip(w_near, 1)]
 
     w_qkv, head, mod, con, noisy, hidden0, attn16, qkv16, totals, mixture16 = attention_forward(
         tsteps, latents, noise, plan, grid, w_pieces, shares, place

time: 146 us -> 139 us (0.952)
  blocking collectives: 35 us -> 25.3 us
  starting transfers between devices: 37.5 us -> 39.9 us
    all_to_all x1, blocking collectives: 19 us -> 9.25 us  [eight_by_four(): shares = lax.all_to_all(shares, 'fsdp', 0, 0)]
    ppermute x30 -> x31, starting transfers between devices: 29.2 us -> 32.6 us  [flip(): return lax.ppermute(x, axis, [(i, i ^ bit) for i in range(size)])]
    pallas_call x20 -> x21, Pallas kernels: 38.7 us -> 39.8 us  [kernel_call(): pl.pallas_call(run, out_shape=[jax.ShapeDtypeStruct(s, t) for s, t in out...]
    ppermute x30 -> x31, waiting for transfers between devices: 21.7 us -> 22.2 us  [flip(): return lax.ppermute(x, axis, [(i, i ^ bit) for i in range(size)])]
  transfers between devices with their start and end apart: 32 -> 33, of which waited for: 11 -> 9; matrix products, arithmetic and copies ran while one was open for 0% -> 0% of each run, Pallas kernels for 10% -> 10%
where the time goes in v4:
time: 139 us; the launch traced here: 138 us
  starting transfers between devices  39.9 us (29%)
  Pallas kernels  39.8 us (29%)
  waiting for transfers between devices  26.9 us (19%)
  blocking collectives  25.3 us (18%)
  local copies, waits for them, and re-layouts  5.06 us (4%)
  between operations  1.4 us (1%)
    pallas_call x21, Pallas kernels, kernel_call(): pl.pallas_call(run, out_shape=[jax.ShapeDtypeStruct(s, t) for s, t in out...  39.8 us
    ppermute x31, starting transfers between devices, flip(): return lax.ppermute(x, axis, [(i, i ^ bit) for i in range(size)])  32.6 us
    ppermute x31, waiting for transfers between devices, flip(): return lax.ppermute(x, axis, [(i, i ^ bit) for i in range(size)])  22.2 us
    all_to_all x1, blocking collectives, eight_by_four(): shares = lax.all_to_all(shares, 'fsdp', 0, 0)  9.25 us
    all_gather x1, blocking collectives, gather_rows(): return lax.all_gather(x, 'fsdp', axis=0, tiled=True)  8.62 us
    all_to_all x1, blocking collectives, eight_by_four(): usq = lax.all_to_all(usq, 'fsdp', 0, 0)  7.39 us
    unnamed x94, local copies, waits for them, and re-layouts  5.06 us
    all_to_all x1, waiting for transfers between devices, eight_by_four(): d_time = lax.all_to_all(d_time, 'fsdp', 0, 0)  4.72 us
  transfers between devices with their start and end apart: 33, of which 9 were waited for; matrix products, arithmetic and copies ran while one was open for 0% of the time, Pallas kernels for 10%

profile of v4, /device:TPU:0, one launch (start us, length us, event | category | flops | bytes accessed | tf_op | source)
XLA Modules:
  0.0 138.4 jit_solution(14174334219265245503)
XLA Ops:
  2.3 3.5 %collective-permute-start.2 = (bf16[96,384]{1,0:T(8,128)(2,1)S(1)}, bf16[96,384]{1,0:T(8,128)(2,1)S(1)}, u32[]{:S(2)}, u32[]{:S(2)}) collective-permute-start(bf16[96,384]{1,0:T(8,128)(2,1)S(1)} %shard_map.392.refs_1_.refs_7_.refs_11_), channel_id=1, source_target_pairs={{0,6},{1,7},{2,4},{3,5},{4,2},{5,3},{6,0},{7,1},{8,14},{9,15},{10,... | collective-permute-start | bytes 221192 | tf_op jit(solution)/shard_map/ppermute | solution.py:98
  7.2 2.9 %collective-permute-start.9 = (bf16[48,2432]{1,0:T(8,128)(2,1)S(1)}, bf16[48,2432]{1,0:T(8,128)(2,1)S(1)}, u32[]{:S(2)}, u32[]{:S(2)}) collective-permute-start(bf16[48,2432]{1,0:T(8,128)(2,1)S(1)} %shard_map.395), channel_id=1, source_target_pairs={{0,6},{1,7},{2,4},{3,5},{4,2},{5,3},{6,0},{7,1},{8,14},{9,15},{10,... | collective-permute-start | bytes 700424 | tf_op jit(solution)/shard_map/ppermute | solution.py:98
  11.1 2.3 %collective-permute-start.8 = (bf16[48,4736]{1,0:T(8,128)(2,1)S(1)}, bf16[48,4736]{1,0:T(8,128)(2,1)S(1)}, u32[]{:S(2)}, u32[]{:S(2)}) collective-permute-start(bf16[48,4736]{1,0:T(8,128)(2,1)S(1)} %get-tuple-element.114.refs_7_), channel_id=1, source_target_pairs={{0,4},{1,5},{2,6},{3,7},{4,0},{5,1},{6,2},{7,3},{8,12},{9,13},{10,... | collective-permute-start | bytes 1363976 | tf_op jit(solution)/shard_map/ppermute | solution.py:98
  13.5 3.2 %collective-permute-done.9.refs_3_ = bf16[48,2432]{1,0:T(8,128)(2,1)S(1)} collective-permute-done((bf16[48,2432]{1,0:T(8,128)(2,1)S(1)}, bf16[48,2432]{1,0:T(8,128)(2,1)S(1)}, u32[]{:S(2)}, u32[]{:S(2)}) %collective-permute-start.9) | collective-permute-done | bytes 233504 | tf_op jit(solution)/shard_map/ppermute | solution.py:98
  16.7 2.0 %collective-permute-start.10 = (bf16[48,2432]{1,0:T(8,128)(2,1)S(1)}, bf16[48,2432]{1,0:T(8,128)(2,1)S(1)}, u32[]{:S(2)}, u32[]{:S(2)}) collective-permute-start(bf16[48,2432]{1,0:T(8,128)(2,1)S(1)} %collective-permute-done.9.refs_3_), channel_id=1, source_target_pairs={{0,8},{8,0},{16,24},{24,16},{1,9},{9,1},{17,25},{25,17},{2,10},{10... | collective-permute-start | bytes 700424 | tf_op jit(solution)/shard_map/ppermute | solution.py:98
  18.7 1.6 %shard_map.394 = (f32[8,8,768]{2,1,0:T(8,128)S(1)}, bf16[256,384]{1,0:T(8,128)(2,1)S(1)}, bf16[384,384]{1,0:T(8,128)(2,1)S(1)}) custom-call(s32[3]{0:T(128)S(1)} %pad_add_fusion.refs_0_.refs_1_, bf16[96,384]{1,0:T(8,128)(2,1)S(1)} %shard_map.392.refs_1_.refs_7_.refs_11_, bf16[96,384]{1,0:T(8,128)(2,1)S(1)} %collective-permute-done.refs_10_.refs_2_, ...), custom_call_target="tpu_custom_call" | custom-call | flops 3449999872 | bytes 1000000 | tf_op jit(solution)/shard_map/pallas_call | solution.py:141
  20.4 9.3 %all_to_all.20.refs_5_.refs_6_ = f32[8,8,768]{2,1,0:T(8,128)S(1)} all-to-all(f32[8,8,768]{2,1,0:T(8,128)S(1)} %get-tuple-element.113), channel_id=1, replica_groups=mesh['rep'=4,'fsdp'=8] {'fsdp'}, dimensions={0} | all-to-all | bytes 393216 | tf_op jit(solution)/shard_map/all_to_all | solution.py:944
  31.0 3.3 %collective-permute-done.11.refs_9_ = bf16[48,4736]{1,0:T(8,128)(2,1)S(1)} collective-permute-done((bf16[48,4736]{1,0:T(8,128)(2,1)S(1)}, bf16[48,4736]{1,0:T(8,128)(2,1)S(1)}, u32[]{:S(2)}, u32[]{:S(2)}) %collective-permute-start.11) | collective-permute-done | bytes 454688 | tf_op jit(solution)/shard_map/ppermute | solution.py:98
  34.3 5.0 %shard_map.397 = (bf16[384,1152]{1,0:T(8,128)(2,1)S(1)}, bf16[48,384]{1,0:T(8,128)(2,1)S(1)}, f32[2,3072]{1,0:T(2,128)S(1)}, f32[2,8]{1,0:T(2,128)S(1)}, bf16[2,...) custom-call(s32[2]{0:T(128)S(1)} %bitcast.29, ...), custom_call_target="tpu_custom_call" | custom-call | flops 9200000000 | bytes 1000000 | tf_op jit(solution)/shard_map/pallas_call | solution.py:141
  39.3 10.2 %shard_map.398 = (f32[4,48,3456]{2,1,0:T(8,128)S(1)}, bf16[4,48,3456]{2,1,0:T(8,128)(2,1)S(1)}, f32[32,384]{1,0:T(8,128)S(1)}, bf16[2,256,384]{2,1,0:T(8,128)(2,...) custom-call(s32[3]{0:T(128)S(1)} %pad_add_fusion.refs_0_.refs_1_, ...), custom_call_target="tpu_custom_call" | custom-call | flops 14949999616 | bytes 1000000 | tf_op jit(solution)/shard_map/pallas_call | solution.py:141
  49.7 4.3 %shard_map.399.refs_3_.refs_4_ = bf16[512,1152]{1,0:T(8,128)(2,1)S(1)} custom-call(bf16[2,256,1152]{2,1,0:T(8,128)(2,1)S(1)} %get-tuple-element.122.refs_0_, f32[2,256,128]{2,1,0:T(8,128)S(1)} %get-tuple-element.123.refs_1_, bf16[2,256,384]{2,1,0:T(8,128)(2,1)S(1)} %get-tuple-element.124.refs_2_, f32[4,48,3456]{2,1,0:T(8,128)S(1)} %get-tuple-element.120.refs_3_.refs_1_), custom_call_target="tpu_custom_call" | custom-call | flops 4600000000 | bytes 1000000 | tf_op jit(solution)/shard_map/pallas_call | solution.py:141
  54.0 1.5 %shard_map.400 = (f32[48,3456]{1,0:T(8,128)S(1)}, bf16[48,3456]{1,0:T(8,128)(2,1)S(1)}, bf16[48,3456]{1,0:T(8,128)(2,1)}, bf16[48,3456]{1,0:T(8,128)(2,1)S(1)}) custom-call(s32[3]{0:T(128)S(1)} %pad_add_fusion.refs_0_.refs_1_, f32[4,48,3456]{2,1,0:T(8,128)S(1)} %get-tuple-element.120.refs_3_.refs_1_, ...), custom_call_target="tpu_custom_call" | custom-call | flops 2300000000 | bytes 1000000 | tf_op jit(solution)/shard_map/pallas_call | solution.py:141
  57.0 1.4 %collective-permute-start.16 = (bf16[48,3456]{1,0:T(8,128)(2,1)S(1)}, bf16[48,3456]{1,0:T(8,128)(2,1)S(1)}, u32[]{:S(2)}, u32[]{:S(2)}) collective-permute-start(bf16[48,3456]{1,0:T(8,128)(2,1)S(1)} %get-tuple-element.128), channel_id=1, source_target_pairs={{0,6},{1,7},{2,4},{3,5},{4,2},{5,3},{6,0},{7,1},{8,14},{9,15},{10,... | collective-permute-start | bytes 995336 | tf_op jit(solution)/shard_map/ppermute | solution.py:98
  58.4 1.5 %collective-permute-start.14 = (bf16[48,3456]{1,0:T(8,128)(2,1)S(1)}, bf16[48,3456]{1,0:T(8,128)(2,1)S(1)}, u32[]{:S(2)}, u32[]{:S(2)}) collective-permute-start(bf16[48,3456]{1,0:T(8,128)(2,1)S(1)} %get-tuple-element.126.refs_12_), channel_id=1, source_target_pairs={{0,2},{1,3},{2,0},{3,1},{4,6},{5,7},{6,4},{7,5},{8,10},{9,11},{10,... | collective-permute-start | bytes 995336 | tf_op jit(solution)/shard_map/ppermute | solution.py:98
  59.9 3.0 %shard_map.404 = (f32[4,48,1280]{2,1,0:T(8,128)S(1)}, bf16[4,48,1280]{2,1,0:T(8,128)(2,1)S(1)}, bf16[4,16,512]{2,1,0:T(8,128)(2,1)}) custom-call(s32[3]{0:T(128)S(1)} %pad_add_fusion.refs_0_.refs_1_, f32[2,3072]{1,0:T(2,128)S(1)} %get-tuple-element.116.refs_3_.refs_1_, f32[2,256,384]{2,1,0:T(8,128)S(1)} %get-tuple-element.117.refs_4_.refs_2_, ...), custom_call_target="tpu_custom_call" | custom-call | flops 4600000000 | bytes 1000000 | tf_op jit(solution)/shard_map/pallas_call | solution.py:141
  63.8 3.9 %all-to-all-start.1 = ((bf16[4,16,512]{2,1,0:T(8,128)(2,1)}), bf16[4,16,512]{2,1,0:T(8,128)(2,1)S(1)}, u32[]{:S(2)}, u32[]{:S(2)}) async-start(bf16[4,16,512]{2,1,0:T(8,128)(2,1)} %get-tuple-element.143), calls=%async_computation.1 | async-start | bytes 131072 | tf_op jit(solution)/shard_map/all_to_all | solution.py:963
  67.7 6.2 %collective-permute-done.15.refs_3_ = bf16[48,3456]{1,0:T(8,128)(2,1)S(1)} collective-permute-done((bf16[48,3456]{1,0:T(8,128)(2,1)}, bf16[48,3456]{1,0:T(8,128)(2,1)S(1)}, u32[]{:S(2)}, u32[]{:S(2)}) %collective-permute-start.15) | collective-permute-done | bytes 331808 | tf_op jit(solution)/shard_map/ppermute | solution.py:98
  77.5 2.6 %collective-permute-start.18 = (bf16[48,896]{1,0:T(8,128)(2,1)S(1)}, bf16[48,896]{1,0:T(8,128)(2,1)S(1)}, u32[]{:S(2)}, u32[]{:S(2)}) collective-permute-start(bf16[48,896]{1,0:T(8,128)(2,1)S(1)} %get-tuple-element.131), channel_id=1, source_target_pairs={{0,16},{8,24},{16,0},{24,8},{1,17},{9,25},{17,1},{25,9},{2,18},{10... | collective-permute-start | bytes 258056 | tf_op jit(solution)/shard_map/ppermute | solution.py:98
  83.2 2.4 %collective-permute-start.26 = (bf16[64,1792]{1,0:T(8,128)(2,1)S(1)}, bf16[64,1792]{1,0:T(8,128)(2,1)S(1)}, u32[]{:S(2)}, u32[]{:S(2)}) collective-permute-start(bf16[64,1792]{1,0:T(8,128)(2,1)S(1)} %get-tuple-element.147), channel_id=1, source_target_pairs={{0,6},{1,7},{2,4},{3,5},{4,2},{5,3},{6,0},{7,1},{8,14},{9,15},{10,... | collective-permute-start | bytes 688136 | tf_op jit(solution)/shard_map/ppermute | solution.py:98
  86.4 5.4 %collective-permute-done.19.refs_3_ = bf16[48,896]{1,0:T(8,128)(2,1)S(1)} collective-permute-done((bf16[48,896]{1,0:T(8,128)(2,1)S(1)}, bf16[48,896]{1,0:T(8,128)(2,1)S(1)}, u32[]{:S(2)}, u32[]{:S(2)}) %collective-permute-start.19) | collective-permute-done | bytes 86048 | tf_op jit(solution)/shard_map/ppermute | solution.py:98
  91.9 2.1 %collective-permute-start.22 = (bf16[48,896]{1,0:T(8,128)(2,1)S(1)}, bf16[48,896]{1,0:T(8,128)(2,1)S(1)}, u32[]{:S(2)}, u32[]{:S(2)}) collective-permute-start(bf16[48,896]{1,0:T(8,128)(2,1)S(1)} %shard_map.402.refs_1_), channel_id=1, source_target_pairs={{0,24},{8,16},{16,8},{24,0},{1,25},{9,17},{17,9},{25,1},{2,26},{10... | collective-permute-start | bytes 258056 | tf_op jit(solution)/shard_map/ppermute | solution.py:98
  94.0 2.4 %collective-permute-start.20 = (bf16[48,896]{1,0:T(8,128)(2,1)S(1)}, bf16[48,896]{1,0:T(8,128)(2,1)S(1)}, u32[]{:S(2)}, u32[]{:S(2)}) collective-permute-start(bf16[48,896]{1,0:T(8,128)(2,1)S(1)} %shard_map.402.refs_1_), channel_id=1, source_target_pairs={{0,8},{8,0},{16,24},{24,16},{1,9},{9,1},{17,25},{25,17},{2,10},{10... | collective-permute-start | bytes 258056 | tf_op jit(solution)/shard_map/ppermute | solution.py:98
  98.3 1.8 %collective-permute-done.21.refs_3_ = bf16[48,896]{1,0:T(8,128)(2,1)S(1)} collective-permute-done((bf16[48,896]{1,0:T(8,128)(2,1)S(1)}, bf16[48,896]{1,0:T(8,128)(2,1)S(1)}, u32[]{:S(2)}, u32[]{:S(2)}) %collective-permute-start.21) | collective-permute-done | bytes 86048 | tf_op jit(solution)/shard_map/ppermute | solution.py:98
  101.5 2.9 %shard_map.407 = (f32[48,3072]{1,0:T(8,128)S(1)}, f32[48,1001]{1,0:T(8,128)S(1)}, bf16[8,64,128]{2,1,0:T(8,128)(2,1)}, f32[8,128]{1,0:T(8,128)S(1)}, bf16[64,32]...) custom-call(s32[3]{0:T(128)S(1)} %pad_add_fusion.refs_0_.refs_1_, ...), custom_call_target="tpu_custom_call" | custom-call | flops 4600000000 | bytes 1000000 | tf_op jit(solution)/shard_map/pallas_call | solution.py:141
  104.4 2.0 %collective-permute-start.30 = (bf16[48,1280]{1,0:T(8,128)(2,1)S(1)}, bf16[48,1280]{1,0:T(8,128)(2,1)S(1)}, u32[]{:S(2)}, u32[]{:S(2)}) collective-permute-start(bf16[48,1280]{1,0:T(8,128)(2,1)S(1)} %get-tuple-element.157.refs_1_), channel_id=1, source_target_pairs={{0,24},{8,16},{16,8},{24,0},{1,25},{9,17},{17,9},{25,1},{2,26},{10... | collective-permute-start | bytes 368648 | tf_op jit(solution)/shard_map/ppermute | solution.py:98
  106.6 2.2 %collective-permute-start.28 = (bf16[48,1280]{1,0:T(8,128)(2,1)S(1)}, bf16[48,1280]{1,0:T(8,128)(2,1)S(1)}, u32[]{:S(2)}, u32[]{:S(2)}) collective-permute-start(bf16[48,1280]{1,0:T(8,128)(2,1)S(1)} %get-tuple-element.157.refs_1_), channel_id=1, source_target_pairs={{0,8},{8,0},{16,24},{24,16},{1,9},{9,1},{17,25},{25,17},{2,10},{10... | collective-permute-start | bytes 368648 | tf_op jit(solution)/shard_map/ppermute | solution.py:98
  108.8 3.4 %all-to-all-start.2 = ((bf16[8,64,128]{2,1,0:T(8,128)(2,1)}), bf16[8,64,128]{2,1,0:T(8,128)(2,1)S(1)}, u32[]{:S(2)}, u32[]{:S(2)}) async-start(bf16[8,64,128]{2,1,0:T(8,128)(2,1)} %get-tuple-element.158), calls=%async_computation.2 | async-start | bytes 262144 | tf_op jit(solution)/shard_map/all_to_all | solution.py:973
  112.9 4.7 %all-to-all-done.2.refs_0_ = bf16[8,64,128]{2,1,0:T(8,128)(2,1)S(1)} async-done(((bf16[8,64,128]{2,1,0:T(8,128)(2,1)}), bf16[8,64,128]{2,1,0:T(8,128)(2,1)S(1)}, u32[]{:S(2)}, u32[]{:S(2)}) %all-to-all-start.2) | async-done | bytes 131104 | tf_op jit(solution)/shard_map/all_to_all | solution.py:973
  118.7 8.6 %all_gather.3 = f32[256,384]{1,0:T(8,128)S(1)} all-gather(f32[32,384]{1,0:T(8,128)S(1)} %get-tuple-element.164), channel_id=1, replica_groups=mesh['rep'=4,'fsdp'=8] {'fsdp'}, dimensions={0}, use_global_device_ids=true | all-gather | bytes 442368 | tf_op jit(solution)/shard_map/all_gather | solution.py:121
  127.4 2.0 %shard_map.411 = (f32[640]{0:T(1024)}, f32[768]{0:T(1024)}, f32[1385]{0:T(1024)}, f32[3456]{0:T(1024)}, f32[1536]{0:T(1024)}, /*index=5*/f32[768]{0:T(1024)}, f3...) custom-call(s32[3]{0:T(128)S(1)} %pad_add_fusion.refs_0_.refs_1_, ...), custom_call_target="tpu_custom_call" | custom-call | flops 4024999936 | bytes 1000000 | tf_op jit(solution)/shard_map/pallas_call | solution.py:141
  129.4 7.4 %all_to_all.21.refs_0_ = f32[8,8,128]{2,1,0:T(8,128)S(1)} all-to-all(f32[8,8,128]{2,1,0:T(8,128)S(1)} %get-tuple-element.168), channel_id=1, replica_groups=mesh['rep'=4,'fsdp'=8] {'fsdp'}, dimensions={0} | all-to-all | bytes 65536 | tf_op jit(solution)/shard_map/all_to_all | solution.py:981
  136.9 1.5 %shard_map.412 = (f32[32,384]{1,0:T(8,128)}, f32[48,384]{1,0:T(8,128)}, f32[48,1001]{1,0:T(8,128)}, f32[48,3072]{1,0:T(8,128)}, f32[48,1152]{1,0:T(8,128)}, /*in...) custom-call(f32[8,8,128]{2,1,0:T(8,128)S(1)} %all_to_all.21.refs_0_,, ...), custom_call_target="tpu_custom_call" | custom-call | flops 4024999936 | bytes 1000000 | tf_op jit(solution)/shard_map/pallas_call | solution.py:141
  (153 shorter events, 20.7 us)
Async XLA Ops:
  1.8 9.3 %collective-permute-start.3 = (bf16[96,384]{1,0:T(8,128)(2,1)S(1)}, bf16[96,384]{1,0:T(8,128)(2,1)S(1)}, u32[]{:S(2)}, u32[]{:S(2)}) collective-permute-start(bf16[96,384]{1,0:T(8,128)(2,1)S(1)} %shard_map.392.refs_1_.refs_7_.refs_11_), channel_id=1, source_target_pairs={{0,1},{1,0},{2,3},{3,2},{4,5},{5,4},{6,7},{7,6},{8,9},{9,8},{10,11... | collective-permute-start | bytes 221192 | tf_op jit(solution)/shard_map/ppermute | solution.py:98
  2.3 7.9 %collective-permute-start.2 = (bf16[96,384]{1,0:T(8,128)(2,1)S(1)}, bf16[96,384]{1,0:T(8,128)(2,1)S(1)}, u32[]{:S(2)}, u32[]{:S(2)}) collective-permute-start(bf16[96,384]{1,0:T(8,128)(2,1)S(1)} %shard_map.392.refs_1_.refs_7_.refs_11_), channel_id=1, source_target_pairs={{0,6},{1,7},{2,4},{3,5},{4,2},{5,3},{6,0},{7,1},{8,14},{9,15},{10,... | collective-permute-start | bytes 221192 | tf_op jit(solution)/shard_map/ppermute | solution.py:98
  5.8 4.4 %collective-permute-start.1 = (bf16[96,384]{1,0:T(8,128)(2,1)S(1)}, bf16[96,384]{1,0:T(8,128)(2,1)S(1)}, u32[]{:S(2)}, u32[]{:S(2)}) collective-permute-start(bf16[96,384]{1,0:T(8,128)(2,1)S(1)} %shard_map.392.refs_1_.refs_7_.refs_11_), channel_id=1, source_target_pairs={{0,4},{1,5},{2,6},{3,7},{4,0},{5,1},{6,2},{7,3},{8,12},{9,13},{10,... | collective-permute-start | bytes 221192 | tf_op jit(solution)/shard_map/ppermute | solution.py:98
  6.3 4.4 %collective-permute-start = (bf16[96,384]{1,0:T(8,128)(2,1)S(1)}, bf16[96,384]{1,0:T(8,128)(2,1)S(1)}, u32[]{:S(2)}, u32[]{:S(2)}) collective-permute-start(bf16[96,384]{1,0:T(8,128)(2,1)S(1)} %shard_map.392.refs_1_.refs_7_.refs_11_), channel_id=1, source_target_pairs={{0,2},{1,3},{2,0},{3,1},{4,6},{5,7},{6,4},{7,5},{8,10},{9,11},{10,... | collective-permute-start | bytes 221192 | tf_op jit(solution)/shard_map/ppermute | solution.py:98
  7.2 9.5 %collective-permute-start.9 = (bf16[48,2432]{1,0:T(8,128)(2,1)S(1)}, bf16[48,2432]{1,0:T(8,128)(2,1)S(1)}, u32[]{:S(2)}, u32[]{:S(2)}) collective-permute-start(bf16[48,2432]{1,0:T(8,128)(2,1)S(1)} %shard_map.395), channel_id=1, source_target_pairs={{0,6},{1,7},{2,4},{3,5},{4,2},{5,3},{6,0},{7,1},{8,14},{9,15},{10,... | collective-permute-start | bytes 700424 | tf_op jit(solution)/shard_map/ppermute | solution.py:98
  10.3 8.4 %collective-permute-start.5 = (bf16[96,384]{1,0:T(8,128)(2,1)S(1)}, bf16[96,384]{1,0:T(8,128)(2,1)S(1)}, u32[]{:S(2)}, u32[]{:S(2)}) collective-permute-start(bf16[96,384]{1,0:T(8,128)(2,1)S(1)} %collective-permute-done.1.refs_11_.refs_3_), channel_id=1, source_target_pairs={{0,1},{1,0},{2,3},{3,2},{4,5},{5,4},{6,7},{7,6},{8,9},{9,8},{10,11... | collective-permute-start | bytes 221192 | tf_op jit(solution)/shard_map/ppermute | solution.py:98
  10.7 8.0 %collective-permute-start.4 = (bf16[96,384]{1,0:T(8,128)(2,1)S(1)}, bf16[96,384]{1,0:T(8,128)(2,1)S(1)}, u32[]{:S(2)}, u32[]{:S(2)}) collective-permute-start(bf16[96,384]{1,0:T(8,128)(2,1)S(1)} %collective-permute-done.refs_10_.refs_2_), channel_id=1, source_target_pairs={{0,1},{1,0},{2,3},{3,2},{4,5},{5,4},{6,7},{7,6},{8,9},{9,8},{10,11... | collective-permute-start | bytes 221192 | tf_op jit(solution)/shard_map/ppermute | solution.py:98
  11.1 18.5 %collective-permute-start.8 = (bf16[48,4736]{1,0:T(8,128)(2,1)S(1)}, bf16[48,4736]{1,0:T(8,128)(2,1)S(1)}, u32[]{:S(2)}, u32[]{:S(2)}) collective-permute-start(bf16[48,4736]{1,0:T(8,128)(2,1)S(1)} %get-tuple-element.114.refs_7_), channel_id=1, source_target_pairs={{0,4},{1,5},{2,6},{3,7},{4,0},{5,1},{6,2},{7,3},{8,12},{9,13},{10,... | collective-permute-start | bytes 1363976 | tf_op jit(solution)/shard_map/ppermute | solution.py:98
  13.4 16.3 %collective-permute-start.7 = (bf16[48,4736]{1,0:T(8,128)(2,1)S(1)}, bf16[48,4736]{1,0:T(8,128)(2,1)S(1)}, u32[]{:S(2)}, u32[]{:S(2)}) collective-permute-start(bf16[48,4736]{1,0:T(8,128)(2,1)S(1)} %get-tuple-element.114.refs_7_), channel_id=1, source_target_pairs={{0,2},{1,3},{2,0},{3,1},{4,6},{5,7},{6,4},{7,5},{8,10},{9,11},{10,... | collective-permute-start | bytes 1363976 | tf_op jit(solution)/shard_map/ppermute | solution.py:98
  16.7 12.9 %collective-permute-start.10 = (bf16[48,2432]{1,0:T(8,128)(2,1)S(1)}, bf16[48,2432]{1,0:T(8,128)(2,1)S(1)}, u32[]{:S(2)}, u32[]{:S(2)}) collective-permute-start(bf16[48,2432]{1,0:T(8,128)(2,1)S(1)} %collective-permute-done.9.refs_3_), channel_id=1, source_target_pairs={{0,8},{8,0},{16,24},{24,16},{1,9},{9,1},{17,25},{25,17},{2,10},{10... | collective-permute-start | bytes 700424 | tf_op jit(solution)/shard_map/ppermute | solution.py:98
  30.4 3.8 %collective-permute-start.12 = (bf16[3,48,4736]{2,1,0:T(8,128)(2,1)S(1)}, bf16[3,48,4736]{2,1,0:T(8,128)(2,1)S(1)}, u32[]{:S(2)}, u32[]{:S(2)}) collective-permute-start(bf16[3,48,4736]{2,1,0:T(8,128)(2,1)S(1)} %shard_map.396.refs_8_), channel_id=1, source_target_pairs={{0,1},{1,0},{2,3},{3,2},{4,5},{5,4},{6,7},{7,6},{8,9},{9,8},{10,11... | collective-permute-start | bytes 4091912 | tf_op jit(solution)/shard_map/ppermute | solution.py:98
  30.5 3.7 %collective-permute-start.11 = (bf16[48,4736]{1,0:T(8,128)(2,1)S(1)}, bf16[48,4736]{1,0:T(8,128)(2,1)S(1)}, u32[]{:S(2)}, u32[]{:S(2)}) collective-permute-start(bf16[48,4736]{1,0:T(8,128)(2,1)S(1)} %get-tuple-element.114.refs_7_), channel_id=1, source_target_pairs={{0,1},{1,0},{2,3},{3,2},{4,5},{5,4},{6,7},{7,6},{8,9},{9,8},{10,11... | collective-permute-start | bytes 1363976 | tf_op jit(solution)/shard_map/ppermute | solution.py:98
  49.5 4.5 %collective-permute-start.13 = (bf16[4,48,3456]{2,1,0:T(8,128)(2,1)S(1)}, bf16[4,48,3456]{2,1,0:T(8,128)(2,1)S(1)}, u32[]{:S(2)}, u32[]{:S(2)}) collective-permute-start(bf16[4,48,3456]{2,1,0:T(8,128)(2,1)S(1)} %get-tuple-element.121), channel_id=1, source_target_pairs={{0,1},{1,0},{2,3},{3,2},{4,5},{5,4},{6,7},{7,6},{8,9},{9,8},{10,11... | collective-permute-start | bytes 3981320 | tf_op jit(solution)/shard_map/ppermute | solution.py:98
  56.4 17.5 %collective-permute-start.15 = (bf16[48,3456]{1,0:T(8,128)(2,1)}, bf16[48,3456]{1,0:T(8,128)(2,1)S(1)}, u32[]{:S(2)}, u32[]{:S(2)}) collective-permute-start(bf16[48,3456]{1,0:T(8,128)(2,1)} %get-tuple-element.127), channel_id=1, source_target_pairs={{0,4},{1,5},{2,6},{3,7},{4,0},{5,1},{6,2},{7,3},{8,12},{9,13},{10,... | collective-permute-start | bytes 995336 | tf_op jit(solution)/shard_map/ppermute | solution.py:98
  57.0 16.9 %collective-permute-start.16 = (bf16[48,3456]{1,0:T(8,128)(2,1)S(1)}, bf16[48,3456]{1,0:T(8,128)(2,1)S(1)}, u32[]{:S(2)}, u32[]{:S(2)}) collective-permute-start(bf16[48,3456]{1,0:T(8,128)(2,1)S(1)} %get-tuple-element.128), channel_id=1, source_target_pairs={{0,6},{1,7},{2,4},{3,5},{4,2},{5,3},{6,0},{7,1},{8,14},{9,15},{10,... | collective-permute-start | bytes 995336 | tf_op jit(solution)/shard_map/ppermute | solution.py:98
  58.4 16.5 %collective-permute-start.14 = (bf16[48,3456]{1,0:T(8,128)(2,1)S(1)}, bf16[48,3456]{1,0:T(8,128)(2,1)S(1)}, u32[]{:S(2)}, u32[]{:S(2)}) collective-permute-start(bf16[48,3456]{1,0:T(8,128)(2,1)S(1)} %get-tuple-element.126.refs_12_), channel_id=1, source_target_pairs={{0,2},{1,3},{2,0},{3,1},{4,6},{5,7},{6,4},{7,5},{8,10},{9,11},{10,... | collective-permute-start | bytes 995336 | tf_op jit(solution)/shard_map/ppermute | solution.py:98
  63.8 16.3 %collective-permute-start.23 = (bf16[4,48,1280]{2,1,0:T(8,128)(2,1)S(1)}, bf16[4,48,1280]{2,1,0:T(8,128)(2,1)S(1)}, u32[]{:S(2)}, u32[]{:S(2)}) collective-permute-start(bf16[4,48,1280]{2,1,0:T(8,128)(2,1)S(1)} %get-tuple-element.142), channel_id=1, source_target_pairs={{0,1},{1,0},{2,3},{3,2},{4,5},{5,4},{6,7},{7,6},{8,9},{9,8},{10,11... | collective-permute-start | bytes 1474568 | tf_op jit(solution)/shard_map/ppermute | solution.py:98
  63.8 16.2 %all-to-all-start.1 = ((bf16[4,16,512]{2,1,0:T(8,128)(2,1)}), bf16[4,16,512]{2,1,0:T(8,128)(2,1)S(1)}, u32[]{:S(2)}, u32[]{:S(2)}) async-start(bf16[4,16,512]{2,1,0:T(8,128)(2,1)} %get-tuple-element.143), calls=%async_computation.1 | async-start | bytes 131072 | tf_op jit(solution)/shard_map/all_to_all | solution.py:963
  77.5 8.3 %collective-permute-start.18 = (bf16[48,896]{1,0:T(8,128)(2,1)S(1)}, bf16[48,896]{1,0:T(8,128)(2,1)S(1)}, u32[]{:S(2)}, u32[]{:S(2)}) collective-permute-start(bf16[48,896]{1,0:T(8,128)(2,1)S(1)} %get-tuple-element.131), channel_id=1, source_target_pairs={{0,16},{8,24},{16,0},{24,8},{1,17},{9,25},{17,1},{25,9},{2,18},{10... | collective-permute-start | bytes 258056 | tf_op jit(solution)/shard_map/ppermute | solution.py:98
  82.0 12.0 %collective-permute-start.24 = (bf16[64,1792]{1,0:T(8,128)(2,1)S(1)}, bf16[64,1792]{1,0:T(8,128)(2,1)S(1)}, u32[]{:S(2)}, u32[]{:S(2)}) collective-permute-start(bf16[64,1792]{1,0:T(8,128)(2,1)S(1)} %get-tuple-element.145), channel_id=1, source_target_pairs={{0,2},{1,3},{2,0},{3,1},{4,6},{5,7},{6,4},{7,5},{8,10},{9,11},{10,... | collective-permute-start | bytes 688136 | tf_op jit(solution)/shard_map/ppermute | solution.py:98
  82.6 13.7 %collective-permute-start.25 = (bf16[64,1792]{1,0:T(8,128)(2,1)S(1)}, bf16[64,1792]{1,0:T(8,128)(2,1)S(1)}, u32[]{:S(2)}, u32[]{:S(2)}) collective-permute-start(bf16[64,1792]{1,0:T(8,128)(2,1)S(1)} %get-tuple-element.146), channel_id=1, source_target_pairs={{0,4},{1,5},{2,6},{3,7},{4,0},{5,1},{6,2},{7,3},{8,12},{9,13},{10,... | collective-permute-start | bytes 688136 | tf_op jit(solution)/shard_map/ppermute | solution.py:98
  83.2 13.2 %collective-permute-start.26 = (bf16[64,1792]{1,0:T(8,128)(2,1)S(1)}, bf16[64,1792]{1,0:T(8,128)(2,1)S(1)}, u32[]{:S(2)}, u32[]{:S(2)}) collective-permute-start(bf16[64,1792]{1,0:T(8,128)(2,1)S(1)} %get-tuple-element.147), channel_id=1, source_target_pairs={{0,6},{1,7},{2,4},{3,5},{4,2},{5,3},{6,0},{7,1},{8,14},{9,15},{10,... | collective-permute-start | bytes 688136 | tf_op jit(solution)/shard_map/ppermute | solution.py:98
  85.5 6.3 %collective-permute-start.19 = (bf16[48,896]{1,0:T(8,128)(2,1)S(1)}, bf16[48,896]{1,0:T(8,128)(2,1)S(1)}, u32[]{:S(2)}, u32[]{:S(2)}) collective-permute-start(bf16[48,896]{1,0:T(8,128)(2,1)S(1)} %get-tuple-element.132), channel_id=1, source_target_pairs={{0,24},{8,16},{16,8},{24,0},{1,25},{9,17},{17,9},{25,1},{2,26},{10... | collective-permute-start | bytes 258056 | tf_op jit(solution)/shard_map/ppermute | solution.py:98
  85.8 6.1 %collective-permute-start.17 = (bf16[48,896]{1,0:T(8,128)(2,1)S(1)}, bf16[48,896]{1,0:T(8,128)(2,1)S(1)}, u32[]{:S(2)}, u32[]{:S(2)}) collective-permute-start(bf16[48,896]{1,0:T(8,128)(2,1)S(1)} %get-tuple-element.130.refs_4_), channel_id=1, source_target_pairs={{0,8},{8,0},{16,24},{24,16},{1,9},{9,1},{17,25},{25,17},{2,10},{10... | collective-permute-start | bytes 258056 | tf_op jit(solution)/shard_map/ppermute | solution.py:98
  91.9 6.4 %collective-permute-start.22 = (bf16[48,896]{1,0:T(8,128)(2,1)S(1)}, bf16[48,896]{1,0:T(8,128)(2,1)S(1)}, u32[]{:S(2)}, u32[]{:S(2)}) collective-permute-start(bf16[48,896]{1,0:T(8,128)(2,1)S(1)} %shard_map.402.refs_1_), channel_id=1, source_target_pairs={{0,24},{8,16},{16,8},{24,0},{1,25},{9,17},{17,9},{25,1},{2,26},{10... | collective-permute-start | bytes 258056 | tf_op jit(solution)/shard_map/ppermute | solution.py:98
  94.0 6.1 %collective-permute-start.21 = (bf16[48,896]{1,0:T(8,128)(2,1)S(1)}, bf16[48,896]{1,0:T(8,128)(2,1)S(1)}, u32[]{:S(2)}, u32[]{:S(2)}) collective-permute-start(bf16[48,896]{1,0:T(8,128)(2,1)S(1)} %shard_map.402.refs_1_), channel_id=1, source_target_pairs={{0,16},{8,24},{16,0},{24,8},{1,17},{9,25},{17,1},{25,9},{2,18},{10... | collective-permute-start | bytes 258056 | tf_op jit(solution)/shard_map/ppermute | solution.py:98
  94.0 6.1 %collective-permute-start.20 = (bf16[48,896]{1,0:T(8,128)(2,1)S(1)}, bf16[48,896]{1,0:T(8,128)(2,1)S(1)}, u32[]{:S(2)}, u32[]{:S(2)}) collective-permute-start(bf16[48,896]{1,0:T(8,128)(2,1)S(1)} %shard_map.402.refs_1_), channel_id=1, source_target_pairs={{0,8},{8,0},{16,24},{24,16},{1,9},{9,1},{17,25},{25,17},{2,10},{10... | collective-permute-start | bytes 258056 | tf_op jit(solution)/shard_map/ppermute | solution.py:98
  97.0 4.4 %collective-permute-start.27 = (bf16[4,64,512]{2,1,0:T(8,128)(2,1)S(1)}, bf16[4,64,512]{2,1,0:T(8,128)(2,1)S(1)}, u32[]{:S(2)}, u32[]{:S(2)}) collective-permute-start(bf16[4,64,512]{2,1,0:T(8,128)(2,1)S(1)} %get-tuple-element.149.refs_1_), channel_id=1, source_target_pairs={{0,1},{1,0},{2,3},{3,2},{4,5},{5,4},{6,7},{7,6},{8,9},{9,8},{10,11... | collective-permute-start | bytes 786440 | tf_op jit(solution)/shard_map/ppermute | solution.py:98
  104.4 13.7 %collective-permute-start.30 = (bf16[48,1280]{1,0:T(8,128)(2,1)S(1)}, bf16[48,1280]{1,0:T(8,128)(2,1)S(1)}, u32[]{:S(2)}, u32[]{:S(2)}) collective-permute-start(bf16[48,1280]{1,0:T(8,128)(2,1)S(1)} %get-tuple-element.157.refs_1_), channel_id=1, source_target_pairs={{0,24},{8,16},{16,8},{24,0},{1,25},{9,17},{17,9},{25,1},{2,26},{10... | collective-permute-start | bytes 368648 | tf_op jit(solution)/shard_map/ppermute | solution.py:98
  106.4 11.7 %collective-permute-start.29 = (bf16[48,1280]{1,0:T(8,128)(2,1)S(1)}, bf16[48,1280]{1,0:T(8,128)(2,1)S(1)}, u32[]{:S(2)}, u32[]{:S(2)}) collective-permute-start(bf16[48,1280]{1,0:T(8,128)(2,1)S(1)} %get-tuple-element.157.refs_1_), channel_id=1, source_target_pairs={{0,16},{8,24},{16,0},{24,8},{1,17},{9,25},{17,1},{25,9},{2,18},{10... | collective-permute-start | bytes 368648 | tf_op jit(solution)/shard_map/ppermute | solution.py:98
  106.6 11.5 %collective-permute-start.28 = (bf16[48,1280]{1,0:T(8,128)(2,1)S(1)}, bf16[48,1280]{1,0:T(8,128)(2,1)S(1)}, u32[]{:S(2)}, u32[]{:S(2)}) collective-permute-start(bf16[48,1280]{1,0:T(8,128)(2,1)S(1)} %get-tuple-element.157.refs_1_), channel_id=1, source_target_pairs={{0,8},{8,0},{16,24},{24,16},{1,9},{9,1},{17,25},{25,17},{2,10},{10... | collective-permute-start | bytes 368648 | tf_op jit(solution)/shard_map/ppermute | solution.py:98
  108.8 8.8 %all-to-all-start.2 = ((bf16[8,64,128]{2,1,0:T(8,128)(2,1)}), bf16[8,64,128]{2,1,0:T(8,128)(2,1)S(1)}, u32[]{:S(2)}, u32[]{:S(2)}) async-start(bf16[8,64,128]{2,1,0:T(8,128)(2,1)} %get-tuple-element.158), calls=%async_computation.2 | async-start | bytes 262144 | tf_op jit(solution)/shard_map/all_to_all | solution.py:973
  (48 other events, 312.0 us)

commit v5 on v4

--- a/solution.py
+++ b/solution.py
@@ -126,7 +126,7 @@
     return (lane < HEAD_DIM) if which == 0 else (lane >= HEAD_DIM)
 
 
-FLOPS_US = 1_150_000_000
+FLOPS_US = 5000_000_000
 
 
 def kernel_call(body, outs, operands, micros, scratch=(), places=None, after=(), room=16):
@@ -162,17 +162,17 @@
 
 
 def shards_of(refs):
-    own, near, core, far = refs[:4]
-    return [own] + [near.at[n] for n in range(3)] + [core] + [far.at[n] for n in range(3)]
+    near, far = refs[:2]
+    return [near.at[n] for n in range(4)] + [far.at[n] for n in range(4)]
 
 
 def attention_forward(tsteps, lat, noi, plan, grid, weights, shares, place, after=()):
     images = lat.shape[0]
-    fast = len(weights) == 4
+    fast = len(weights[0].shape) == 3
 
     def body(ts, at, lat_r, noi_r, plan_r, grid_r, share_r, *refs):
         if fast:
-            wq_r, head_r, head_s = refs[4], refs[5], refs[-1]
+            wq_r, head_r, head_s = refs[2], refs[3], refs[-1]
             shards = shards_of(refs)
             for n in range(8):
                 owner = piece_owner(at, n)
@@ -181,7 +181,7 @@
                 head_s[owner] = shards[n][:, 3 * D : 3 * D + 48]
             for p in range(8):
                 head_r[:, p * 48 : (p + 1) * 48] = head_s[p]
-            refs = refs[6:-1]
+            refs = refs[4:-1]
         else:
             wq_r, head_r = refs[:2]
             refs = refs[2:]
@@ -257,7 +257,7 @@
     bend_scale = math.sqrt(2.0 / math.pi)
     share = 1.0 / (TOK_IMG * PIN)
 
-    fast = len(weights) == 4
+    fast = len(weights[0].shape) == 3
 
     def body(at, noi_r, con_r, mod_r, h0_r, mix_r, head_r, *refs):
         if fast:
@@ -266,11 +266,11 @@
             for n in range(8):
                 owner = piece_owner(at, n)
                 rows = pl.ds(pl.multiple_of(owner * 48, 48), 48)
-                wp_r[rows, :] = shards[n][:, TAIL : TAIL + D]
-                w1_r[rows, :] = shards[n][:, TAIL + D : TAIL + D + FF]
+                wp_r[rows, :] = shards[n][:, 0:D]
+                w1_r[rows, :] = shards[n][:, D : D + FF]
                 for b in range(4):
-                    w2_r[pl.ds(pl.multiple_of(owner * 192 + b * 48, 48), 48), :] = shards[n][:, TAIL + D + FF + b * D : TAIL + D + FF + (b + 1) * D]
-            refs = refs[4:-3]
+                    w2_r[pl.ds(pl.multiple_of(owner * 192 + b * 48, 48), 48), :] = shards[n][:, D + FF + b * D : D + FF + (b + 1) * D]
+            refs = refs[2:-3]
         else:
             wp_r, w1_r, w2_r = refs[:3]
             refs = refs[3:]
@@ -837,19 +837,21 @@
     return kernel_call(body, [((48, HALF), bf16)], ops, 1, scratch=scratch, places="s" + "v" * 6, after=after)[0]
 
 
-def stacked_pieces(place, two, halves, after=()):
-    def body(at, x, y, a, b, out, cuts):
-        out[0] = x[...]
-        out[1] = y[...]
+def stacked_pieces(place, three, halves, after=()):
+    def body(at, own, x, y, a, b, first, second, cuts):
+        for n, ref in enumerate((own, x, y)):
+            first[n] = ref[:, 0:TAIL]
+            second[n] = ref[:, TAIL:]
         for n, ref in enumerate((a, b)):
             cuts[jnp.bitwise_xor(at[2] % 2, n)] = ref[...]
-        for j in range(2):
-            size = min(HALF, SENT - j * HALF)
-            out[2, :, j * HALF : j * HALF + size] = cuts[j][:, 0:size]
-
-    ops = (place, *two, *halves)
+        first[3] = cuts[0][:, 0:TAIL]
+        second[3, :, 0 : HALF - TAIL] = cuts[0][:, TAIL:]
+        second[3, :, HALF - TAIL :] = cuts[1][:, 0 : SENT - HALF]
+
+    ops = (place, *three, *halves)
     scratch = [pltpu.VMEM((2, 48, HALF), bf16)]
-    return kernel_call(body, [((3, 48, SENT), bf16)], ops, 1, scratch=scratch, places="s" + "v" * 4, after=after)[0]
+    outs = [((4, 48, TAIL), bf16), ((4, 48, SENT - TAIL), bf16)]
+    return kernel_call(body, outs, ops, 1, scratch=scratch, places="s" + "v" * 5, after=after)
 
 
 def chip_blocks(place, keep, sent, micros, after=()):
@@ -938,15 +940,14 @@
     half = half_shard(place, patch_state, out_t, qkv_w, proj_w, fc1_w, fc2_w, after=(bundle,))
     half = flip(half, 6)
     halves = [half, flip(half, 1, "rep")]
-    w_two = [flip(w_own, k) for k in (2, 4)]
-    w_core = flip(w_own, 1)
+    w_three = [w_own, flip(w_own, 2), flip(w_own, 4)]
     shares, w1, w2 = modulation_shares(place, pieces, times, tab16, mod16, images)
     shares = lax.all_to_all(shares, "fsdp", 0, 0)
-    w_near = stacked_pieces(place, w_two, halves, after=(shares,))
-    w_pieces = [w_own, w_near, w_core, flip(w_near, 1)]
+    w_near = stacked_pieces(place, w_three, halves, after=(shares,))
+    q_pieces, w_pieces = ([near, flip(near, 1)] for near in w_near)
 
     w_qkv, head, mod, con, noisy, hidden0, attn16, qkv16, totals, mixture16 = attention_forward(
-        tsteps, latents, noise, plan, grid, w_pieces, shares, place
+        tsteps, latents, noise, plan, grid, q_pieces, shares, place
     )
     keep, send, g_last, d_mix16, d_h1, d_mod, loss_tile = mlp_pass(
         noise, con, mod, hidden0, mixture16, head, w_pieces, place

time: 139 us -> 134 us (0.964)
  waiting for transfers between devices: 26.9 us -> 23.6 us
  starting transfers between devices: 39.9 us -> 37.9 us
    ppermute x31, waiting for transfers between devices: 22.2 us -> 18.9 us  [flip(): return lax.ppermute(x, axis, [(i, i ^ bit) for i in range(size)])]
    ppermute x31, starting transfers between devices: 32.6 us -> 30.7 us  [flip(): return lax.ppermute(x, axis, [(i, i ^ bit) for i in range(size)])]
    unnamed x94 -> x90, local copies, waits for them, and re-layouts: 5.06 us -> 5.04 us
  transfers between devices with their start and end apart: 33 -> 33, of which waited for: 9 -> 11; matrix products, arithmetic and copies ran while one was open for 0% -> 0% of each run, Pallas kernels for 10% -> 15%
where the time goes in v5:
time: 134 us; the launch traced here: 133 us
  Pallas kernels  39.2 us (29%)
  starting transfers between devices  37.9 us (28%)
  blocking collectives  25.9 us (19%)
  waiting for transfers between devices  23.6 us (18%)
  local copies, waits for them, and re-layouts  5.04 us (4%)
  between operations  1.4 us (1%)
    pallas_call x21, Pallas kernels, kernel_call(): pl.pallas_call(run, out_shape=[jax.ShapeDtypeStruct(s, t) for s, t in out...  39.2 us
    ppermute x31, starting transfers between devices, flip(): return lax.ppermute(x, axis, [(i, i ^ bit) for i in range(size)])  30.7 us
    ppermute x31, waiting for transfers between devices, flip(): return lax.ppermute(x, axis, [(i, i ^ bit) for i in range(size)])  18.9 us
    all_gather x1, blocking collectives, gather_rows(): return lax.all_gather(x, 'fsdp', axis=0, tiled=True)  9.28 us
    all_to_all x1, blocking collectives, eight_by_four(): shares = lax.all_to_all(shares, 'fsdp', 0, 0)  9.24 us
    all_to_all x1, blocking collectives, eight_by_four(): usq = lax.all_to_all(usq, 'fsdp', 0, 0)  7.38 us
    unnamed x90, local copies, waits for them, and re-layouts  5.04 us
    all_to_all x1, waiting for transfers between devices, eight_by_four(): d_time = lax.all_to_all(d_time, 'fsdp', 0, 0)  4.73 us
  transfers between devices with their start and end apart: 33, of which 11 were waited for; matrix products, arithmetic and copies ran while one was open for 0% of the time, Pallas kernels for 15%

profile of v5, /device:TPU:0, one launch (start us, length us, event | category | flops | bytes accessed | tf_op | source)
XLA Modules:
  0.0 133.2 jit_solution(3419579754063924060)
XLA Ops:
  2.3 3.5 %collective-permute-start.2 = (bf16[96,384]{1,0:T(8,128)(2,1)S(1)}, bf16[96,384]{1,0:T(8,128)(2,1)S(1)}, u32[]{:S(2)}, u32[]{:S(2)}) collective-permute-start(bf16[96,384]{1,0:T(8,128)(2,1)S(1)} %shard_map.392.refs_1_.refs_7_.refs_11_), channel_id=1, source_target_pairs={{0,6},{1,7},{2,4},{3,5},{4,2},{5,3},{6,0},{7,1},{8,14},{9,15},{10,... | collective-permute-start | bytes 221192 | tf_op jit(solution)/shard_map/ppermute | solution.py:98
  7.2 2.9 %collective-permute-start.9 = (bf16[48,2432]{1,0:T(8,128)(2,1)S(1)}, bf16[48,2432]{1,0:T(8,128)(2,1)S(1)}, u32[]{:S(2)}, u32[]{:S(2)}) collective-permute-start(bf16[48,2432]{1,0:T(8,128)(2,1)S(1)} %shard_map.395), channel_id=1, source_target_pairs={{0,6},{1,7},{2,4},{3,5},{4,2},{5,3},{6,0},{7,1},{8,14},{9,15},{10,... | collective-permute-start | bytes 700424 | tf_op jit(solution)/shard_map/ppermute | solution.py:98
  11.1 2.3 %collective-permute-start.8 = (bf16[48,4736]{1,0:T(8,128)(2,1)S(1)}, bf16[48,4736]{1,0:T(8,128)(2,1)S(1)}, u32[]{:S(2)}, u32[]{:S(2)}) collective-permute-start(bf16[48,4736]{1,0:T(8,128)(2,1)S(1)} %get-tuple-element.116.refs_1_), channel_id=1, source_target_pairs={{0,4},{1,5},{2,6},{3,7},{4,0},{5,1},{6,2},{7,3},{8,12},{9,13},{10,... | collective-permute-start | bytes 1363976 | tf_op jit(solution)/shard_map/ppermute | solution.py:98
  13.5 3.2 %collective-permute-done.9.refs_4_ = bf16[48,2432]{1,0:T(8,128)(2,1)S(1)} collective-permute-done((bf16[48,2432]{1,0:T(8,128)(2,1)S(1)}, bf16[48,2432]{1,0:T(8,128)(2,1)S(1)}, u32[]{:S(2)}, u32[]{:S(2)}) %collective-permute-start.9) | collective-permute-done | bytes 233504 | tf_op jit(solution)/shard_map/ppermute | solution.py:98
  16.7 2.0 %collective-permute-start.10 = (bf16[48,2432]{1,0:T(8,128)(2,1)S(1)}, bf16[48,2432]{1,0:T(8,128)(2,1)S(1)}, u32[]{:S(2)}, u32[]{:S(2)}) collective-permute-start(bf16[48,2432]{1,0:T(8,128)(2,1)S(1)} %collective-permute-done.9.refs_4_), channel_id=1, source_target_pairs={{0,8},{8,0},{16,24},{24,16},{1,9},{9,1},{17,25},{25,17},{2,10},{10... | collective-permute-start | bytes 700424 | tf_op jit(solution)/shard_map/ppermute | solution.py:98
  18.7 1.6 %shard_map.394 = (f32[8,8,768]{2,1,0:T(8,128)S(1)}, bf16[256,384]{1,0:T(8,128)(2,1)S(1)}, bf16[384,384]{1,0:T(8,128)(2,1)S(1)}) custom-call(s32[3]{0:T(128)S(1)} %pad_add_fusion.refs_0_.refs_1_, bf16[96,384]{1,0:T(8,128)(2,1)S(1)} %shard_map.392.refs_1_.refs_7_.refs_11_, bf16[96,384]{1,0:T(8,128)(2,1)S(1)} %collective-permute-done.refs_10_.refs_2_, ...), custom_call_target="tpu_custom_call" | custom-call | flops 15000000512 | bytes 1000000 | tf_op jit(solution)/shard_map/pallas_call | solution.py:141
  21.0 9.2 %all_to_all.20.refs_6_ = f32[8,8,768]{2,1,0:T(8,128)S(1)} all-to-all(f32[8,8,768]{2,1,0:T(8,128)S(1)} %get-tuple-element.115), channel_id=1, replica_groups=mesh['rep'=4,'fsdp'=8] {'fsdp'}, dimensions={0} | all-to-all | bytes 393216 | tf_op jit(solution)/shard_map/all_to_all | solution.py:945
  31.6 1.4 %collective-permute-done.11.refs_8_ = bf16[4,48,1280]{2,1,0:T(8,128)(2,1)S(1)} collective-permute-done((bf16[4,48,1280]{2,1,0:T(8,128)(2,1)S(1)}, bf16[4,48,1280]{2,1,0:T(8,128)(2,1)S(1)}, u32[]{:S(2)}, u32[]{:S(2)}) %collective-permute-start.11) | collective-permute-done | bytes 491552 | tf_op jit(solution)/shard_map/ppermute | solution.py:98
  33.0 5.0 %shard_map.397 = (bf16[384,1152]{1,0:T(8,128)(2,1)S(1)}, bf16[48,384]{1,0:T(8,128)(2,1)S(1)}, f32[2,3072]{1,0:T(2,128)S(1)}, f32[2,8]{1,0:T(2,128)S(1)}, bf16[2,...) custom-call(s32[2]{0:T(128)S(1)} %bitcast.29, ...), custom_call_target="tpu_custom_call" | custom-call | flops 40000000000 | bytes 1000000 | tf_op jit(solution)/shard_map/pallas_call | solution.py:141
  38.0 10.2 %shard_map.398 = (f32[4,48,3456]{2,1,0:T(8,128)S(1)}, bf16[4,48,3456]{2,1,0:T(8,128)(2,1)S(1)}, f32[32,384]{1,0:T(8,128)S(1)}, bf16[2,256,384]{2,1,0:T(8,128)(2,...) custom-call(s32[3]{0:T(128)S(1)} %pad_add_fusion.refs_0_.refs_1_, ...), custom_call_target="tpu_custom_call" | custom-call | flops 65000001536 | bytes 1000000 | tf_op jit(solution)/shard_map/pallas_call | solution.py:141
  48.5 4.3 %shard_map.399.refs_3_.refs_4_ = bf16[512,1152]{1,0:T(8,128)(2,1)S(1)} custom-call(bf16[2,256,1152]{2,1,0:T(8,128)(2,1)S(1)} %get-tuple-element.126.refs_0_, f32[2,256,128]{2,1,0:T(8,128)S(1)} %get-tuple-element.127.refs_1_, bf16[2,256,384]{2,1,0:T(8,128)(2,1)S(1)} %get-tuple-element.128.refs_2_, f32[4,48,3456]{2,1,0:T(8,128)S(1)} %get-tuple-element.124.refs_3_.refs_1_), custom_call_target="tpu_custom_call" | custom-call | flops 20000000000 | bytes 1000000 | tf_op jit(solution)/shard_map/pallas_call | solution.py:141
  55.1 1.5 %collective-permute-start.16 = (bf16[48,3456]{1,0:T(8,128)(2,1)S(1)}, bf16[48,3456]{1,0:T(8,128)(2,1)S(1)}, u32[]{:S(2)}, u32[]{:S(2)}) collective-permute-start(bf16[48,3456]{1,0:T(8,128)(2,1)S(1)} %get-tuple-element.132), channel_id=1, source_target_pairs={{0,6},{1,7},{2,4},{3,5},{4,2},{5,3},{6,0},{7,1},{8,14},{9,15},{10,... | collective-permute-start | bytes 995336 | tf_op jit(solution)/shard_map/ppermute | solution.py:98
  56.5 1.5 %collective-permute-start.14 = (bf16[48,3456]{1,0:T(8,128)(2,1)S(1)}, bf16[48,3456]{1,0:T(8,128)(2,1)S(1)}, u32[]{:S(2)}, u32[]{:S(2)}) collective-permute-start(bf16[48,3456]{1,0:T(8,128)(2,1)S(1)} %get-tuple-element.130.refs_12_), channel_id=1, source_target_pairs={{0,2},{1,3},{2,0},{3,1},{4,6},{5,7},{6,4},{7,5},{8,10},{9,11},{10,... | collective-permute-start | bytes 995336 | tf_op jit(solution)/shard_map/ppermute | solution.py:98
  58.0 3.0 %shard_map.404 = (f32[4,48,1280]{2,1,0:T(8,128)S(1)}, bf16[4,48,1280]{2,1,0:T(8,128)(2,1)S(1)}, bf16[4,16,512]{2,1,0:T(8,128)(2,1)}) custom-call(s32[3]{0:T(128)S(1)} %pad_add_fusion.refs_0_.refs_1_, f32[2,3072]{1,0:T(2,128)S(1)} %get-tuple-element.119.refs_3_.refs_1_, f32[2,256,384]{2,1,0:T(8,128)S(1)} %get-tuple-element.120.refs_4_.refs_2_, ...), custom_call_target="tpu_custom_call" | custom-call | flops 20000000000 | bytes 1000000 | tf_op jit(solution)/shard_map/pallas_call | solution.py:141
  62.0 3.9 %all-to-all-start.1 = ((bf16[4,16,512]{2,1,0:T(8,128)(2,1)}), bf16[4,16,512]{2,1,0:T(8,128)(2,1)S(1)}, u32[]{:S(2)}, u32[]{:S(2)}) async-start(bf16[4,16,512]{2,1,0:T(8,128)(2,1)} %get-tuple-element.147), calls=%async_computation.1 | async-start | bytes 131072 | tf_op jit(solution)/shard_map/all_to_all | solution.py:964
  65.8 5.9 %collective-permute-done.15.refs_3_ = bf16[48,3456]{1,0:T(8,128)(2,1)S(1)} collective-permute-done((bf16[48,3456]{1,0:T(8,128)(2,1)S(1)}, bf16[48,3456]{1,0:T(8,128)(2,1)S(1)}, u32[]{:S(2)}, u32[]{:S(2)}) %collective-permute-start.15) | collective-permute-done | bytes 331808 | tf_op jit(solution)/shard_map/ppermute | solution.py:98
  74.9 2.6 %collective-permute-start.18 = (bf16[48,896]{1,0:T(8,128)(2,1)S(1)}, bf16[48,896]{1,0:T(8,128)(2,1)S(1)}, u32[]{:S(2)}, u32[]{:S(2)}) collective-permute-start(bf16[48,896]{1,0:T(8,128)(2,1)S(1)} %get-tuple-element.135), channel_id=1, source_target_pairs={{0,16},{8,24},{16,0},{24,8},{1,17},{9,25},{17,1},{25,9},{2,18},{10... | collective-permute-start | bytes 258056 | tf_op jit(solution)/shard_map/ppermute | solution.py:98
  81.5 2.6 %collective-permute-done.18.refs_2_ = bf16[48,896]{1,0:T(8,128)(2,1)S(1)} collective-permute-done((bf16[48,896]{1,0:T(8,128)(2,1)S(1)}, bf16[48,896]{1,0:T(8,128)(2,1)S(1)}, u32[]{:S(2)}, u32[]{:S(2)}) %collective-permute-start.18) | collective-permute-done | bytes 86048 | tf_op jit(solution)/shard_map/ppermute | solution.py:98
  84.7 2.8 %collective-permute-start.22 = (bf16[48,896]{1,0:T(8,128)(2,1)S(1)}, bf16[48,896]{1,0:T(8,128)(2,1)S(1)}, u32[]{:S(2)}, u32[]{:S(2)}) collective-permute-start(bf16[48,896]{1,0:T(8,128)(2,1)S(1)} %shard_map.402.refs_1_), channel_id=1, source_target_pairs={{0,24},{8,16},{16,8},{24,0},{1,25},{9,17},{17,9},{25,1},{2,26},{10... | collective-permute-start | bytes 258056 | tf_op jit(solution)/shard_map/ppermute | solution.py:98
  88.8 1.4 %collective-permute-start.20 = (bf16[48,896]{1,0:T(8,128)(2,1)S(1)}, bf16[48,896]{1,0:T(8,128)(2,1)S(1)}, u32[]{:S(2)}, u32[]{:S(2)}) collective-permute-start(bf16[48,896]{1,0:T(8,128)(2,1)S(1)} %shard_map.402.refs_1_), channel_id=1, source_target_pairs={{0,8},{8,0},{16,24},{24,16},{1,9},{9,1},{17,25},{25,17},{2,10},{10... | collective-permute-start | bytes 258056 | tf_op jit(solution)/shard_map/ppermute | solution.py:98
  90.1 1.3 %collective-permute-done.25.refs_3_ = bf16[64,1792]{1,0:T(8,128)(2,1)S(1)} collective-permute-done((bf16[64,1792]{1,0:T(8,128)(2,1)S(1)}, bf16[64,1792]{1,0:T(8,128)(2,1)S(1)}, u32[]{:S(2)}, u32[]{:S(2)}) %collective-permute-start.25) | collective-permute-done | bytes 229408 | tf_op jit(solution)/shard_map/ppermute | solution.py:98
  92.3 1.6 %collective-permute-done.21.refs_3_ = bf16[48,896]{1,0:T(8,128)(2,1)S(1)} collective-permute-done((bf16[48,896]{1,0:T(8,128)(2,1)S(1)}, bf16[48,896]{1,0:T(8,128)(2,1)S(1)}, u32[]{:S(2)}, u32[]{:S(2)}) %collective-permute-start.21) | collective-permute-done | bytes 86048 | tf_op jit(solution)/shard_map/ppermute | solution.py:98
  94.2 1.3 shard_map.403
  95.6 2.9 %shard_map.407 = (f32[48,3072]{1,0:T(8,128)S(1)}, f32[48,1001]{1,0:T(8,128)S(1)}, bf16[8,64,128]{2,1,0:T(8,128)(2,1)}, f32[8,128]{1,0:T(8,128)S(1)}, bf16[64,32]...) custom-call(s32[3]{0:T(128)S(1)} %pad_add_fusion.refs_0_.refs_1_, ...), custom_call_target="tpu_custom_call" | custom-call | flops 20000000000 | bytes 1000000 | tf_op jit(solution)/shard_map/pallas_call | solution.py:141
  98.5 3.1 %collective-permute-start.30 = (bf16[48,1280]{1,0:T(8,128)(2,1)S(1)}, bf16[48,1280]{1,0:T(8,128)(2,1)S(1)}, u32[]{:S(2)}, u32[]{:S(2)}) collective-permute-start(bf16[48,1280]{1,0:T(8,128)(2,1)S(1)} %get-tuple-element.161.refs_1_), channel_id=1, source_target_pairs={{0,24},{8,16},{16,8},{24,0},{1,25},{9,17},{17,9},{25,1},{2,26},{10... | collective-permute-start | bytes 368648 | tf_op jit(solution)/shard_map/ppermute | solution.py:98
  101.6 1.3 collective-permute-start.28
  102.9 3.4 %all-to-all-start.2 = ((bf16[8,64,128]{2,1,0:T(8,128)(2,1)}), bf16[8,64,128]{2,1,0:T(8,128)(2,1)S(1)}, u32[]{:S(2)}, u32[]{:S(2)}) async-start(bf16[8,64,128]{2,1,0:T(8,128)(2,1)} %get-tuple-element.162), calls=%async_computation.2 | async-start | bytes 262144 | tf_op jit(solution)/shard_map/all_to_all | solution.py:974
  107.0 4.7 %all-to-all-done.2.refs_0_ = bf16[8,64,128]{2,1,0:T(8,128)(2,1)S(1)} async-done(((bf16[8,64,128]{2,1,0:T(8,128)(2,1)}), bf16[8,64,128]{2,1,0:T(8,128)(2,1)S(1)}, u32[]{:S(2)}, u32[]{:S(2)}) %all-to-all-start.2) | async-done | bytes 131104 | tf_op jit(solution)/shard_map/all_to_all | solution.py:974
  112.7 9.3 %all_gather.3 = f32[256,384]{1,0:T(8,128)S(1)} all-gather(f32[32,384]{1,0:T(8,128)S(1)} %get-tuple-element.168), channel_id=1, replica_groups=mesh['rep'=4,'fsdp'=8] {'fsdp'}, dimensions={0}, use_global_device_ids=true | all-gather | bytes 442368 | tf_op jit(solution)/shard_map/all_gather | solution.py:121
  122.2 2.0 %shard_map.411 = (f32[640]{0:T(1024)}, f32[768]{0:T(1024)}, f32[1385]{0:T(1024)}, f32[3456]{0:T(1024)}, f32[1536]{0:T(1024)}, /*index=5*/f32[768]{0:T(1024)}, f3...) custom-call(s32[3]{0:T(128)S(1)} %pad_add_fusion.refs_0_.refs_1_, ...), custom_call_target="tpu_custom_call" | custom-call | flops 17500000256 | bytes 1000000 | tf_op jit(solution)/shard_map/pallas_call | solution.py:141
  124.2 7.4 %all_to_all.21.refs_0_ = f32[8,8,128]{2,1,0:T(8,128)S(1)} all-to-all(f32[8,8,128]{2,1,0:T(8,128)S(1)} %get-tuple-element.172), channel_id=1, replica_groups=mesh['rep'=4,'fsdp'=8] {'fsdp'}, dimensions={0} | all-to-all | bytes 65536 | tf_op jit(solution)/shard_map/all_to_all | solution.py:982
  131.7 1.5 %shard_map.412 = (f32[32,384]{1,0:T(8,128)}, f32[48,384]{1,0:T(8,128)}, f32[48,1001]{1,0:T(8,128)}, f32[48,3072]{1,0:T(8,128)}, f32[48,1152]{1,0:T(8,128)}, /*in...) custom-call(f32[8,8,128]{2,1,0:T(8,128)S(1)} %all_to_all.21.refs_0_,, ...), custom_call_target="tpu_custom_call" | custom-call | flops 17500000256 | bytes 1000000 | tf_op jit(solution)/shard_map/pallas_call | solution.py:141
  (149 shorter events, 21.1 us)
Async XLA Ops:
  1.8 9.3 %collective-permute-start.3 = (bf16[96,384]{1,0:T(8,128)(2,1)S(1)}, bf16[96,384]{1,0:T(8,128)(2,1)S(1)}, u32[]{:S(2)}, u32[]{:S(2)}) collective-permute-start(bf16[96,384]{1,0:T(8,128)(2,1)S(1)} %shard_map.392.refs_1_.refs_7_.refs_11_), channel_id=1, source_target_pairs={{0,1},{1,0},{2,3},{3,2},{4,5},{5,4},{6,7},{7,6},{8,9},{9,8},{10,11... | collective-permute-start | bytes 221192 | tf_op jit(solution)/shard_map/ppermute | solution.py:98
  2.3 7.9 %collective-permute-start.2 = (bf16[96,384]{1,0:T(8,128)(2,1)S(1)}, bf16[96,384]{1,0:T(8,128)(2,1)S(1)}, u32[]{:S(2)}, u32[]{:S(2)}) collective-permute-start(bf16[96,384]{1,0:T(8,128)(2,1)S(1)} %shard_map.392.refs_1_.refs_7_.refs_11_), channel_id=1, source_target_pairs={{0,6},{1,7},{2,4},{3,5},{4,2},{5,3},{6,0},{7,1},{8,14},{9,15},{10,... | collective-permute-start | bytes 221192 | tf_op jit(solution)/shard_map/ppermute | solution.py:98
  5.8 4.4 %collective-permute-start.1 = (bf16[96,384]{1,0:T(8,128)(2,1)S(1)}, bf16[96,384]{1,0:T(8,128)(2,1)S(1)}, u32[]{:S(2)}, u32[]{:S(2)}) collective-permute-start(bf16[96,384]{1,0:T(8,128)(2,1)S(1)} %shard_map.392.refs_1_.refs_7_.refs_11_), channel_id=1, source_target_pairs={{0,4},{1,5},{2,6},{3,7},{4,0},{5,1},{6,2},{7,3},{8,12},{9,13},{10,... | collective-permute-start | bytes 221192 | tf_op jit(solution)/shard_map/ppermute | solution.py:98
  6.3 4.4 %collective-permute-start = (bf16[96,384]{1,0:T(8,128)(2,1)S(1)}, bf16[96,384]{1,0:T(8,128)(2,1)S(1)}, u32[]{:S(2)}, u32[]{:S(2)}) collective-permute-start(bf16[96,384]{1,0:T(8,128)(2,1)S(1)} %shard_map.392.refs_1_.refs_7_.refs_11_), channel_id=1, source_target_pairs={{0,2},{1,3},{2,0},{3,1},{4,6},{5,7},{6,4},{7,5},{8,10},{9,11},{10,... | collective-permute-start | bytes 221192 | tf_op jit(solution)/shard_map/ppermute | solution.py:98
  7.2 9.5 %collective-permute-start.9 = (bf16[48,2432]{1,0:T(8,128)(2,1)S(1)}, bf16[48,2432]{1,0:T(8,128)(2,1)S(1)}, u32[]{:S(2)}, u32[]{:S(2)}) collective-permute-start(bf16[48,2432]{1,0:T(8,128)(2,1)S(1)} %shard_map.395), channel_id=1, source_target_pairs={{0,6},{1,7},{2,4},{3,5},{4,2},{5,3},{6,0},{7,1},{8,14},{9,15},{10,... | collective-permute-start | bytes 700424 | tf_op jit(solution)/shard_map/ppermute | solution.py:98
  10.2 3.2 %collective-permute-start.6 = (bf16[96,384]{1,0:T(8,128)(2,1)S(1)}, bf16[96,384]{1,0:T(8,128)(2,1)S(1)}, u32[]{:S(2)}, u32[]{:S(2)}) collective-permute-start(bf16[96,384]{1,0:T(8,128)(2,1)S(1)} %collective-permute-done.2.refs_12_.refs_4_), channel_id=1, source_target_pairs={{0,1},{1,0},{2,3},{3,2},{4,5},{5,4},{6,7},{7,6},{8,9},{9,8},{10,11... | collective-permute-start | bytes 221192 | tf_op jit(solution)/shard_map/ppermute | solution.py:98
  10.3 8.4 %collective-permute-start.5 = (bf16[96,384]{1,0:T(8,128)(2,1)S(1)}, bf16[96,384]{1,0:T(8,128)(2,1)S(1)}, u32[]{:S(2)}, u32[]{:S(2)}) collective-permute-start(bf16[96,384]{1,0:T(8,128)(2,1)S(1)} %collective-permute-done.1.refs_11_.refs_3_), channel_id=1, source_target_pairs={{0,1},{1,0},{2,3},{3,2},{4,5},{5,4},{6,7},{7,6},{8,9},{9,8},{10,11... | collective-permute-start | bytes 221192 | tf_op jit(solution)/shard_map/ppermute | solution.py:98
  10.7 8.0 %collective-permute-start.4 = (bf16[96,384]{1,0:T(8,128)(2,1)S(1)}, bf16[96,384]{1,0:T(8,128)(2,1)S(1)}, u32[]{:S(2)}, u32[]{:S(2)}) collective-permute-start(bf16[96,384]{1,0:T(8,128)(2,1)S(1)} %collective-permute-done.refs_10_.refs_2_), channel_id=1, source_target_pairs={{0,1},{1,0},{2,3},{3,2},{4,5},{5,4},{6,7},{7,6},{8,9},{9,8},{10,11... | collective-permute-start | bytes 221192 | tf_op jit(solution)/shard_map/ppermute | solution.py:98
  11.1 19.2 %collective-permute-start.8 = (bf16[48,4736]{1,0:T(8,128)(2,1)S(1)}, bf16[48,4736]{1,0:T(8,128)(2,1)S(1)}, u32[]{:S(2)}, u32[]{:S(2)}) collective-permute-start(bf16[48,4736]{1,0:T(8,128)(2,1)S(1)} %get-tuple-element.116.refs_1_), channel_id=1, source_target_pairs={{0,4},{1,5},{2,6},{3,7},{4,0},{5,1},{6,2},{7,3},{8,12},{9,13},{10,... | collective-permute-start | bytes 1363976 | tf_op jit(solution)/shard_map/ppermute | solution.py:98
  13.4 16.9 %collective-permute-start.7 = (bf16[48,4736]{1,0:T(8,128)(2,1)S(1)}, bf16[48,4736]{1,0:T(8,128)(2,1)S(1)}, u32[]{:S(2)}, u32[]{:S(2)}) collective-permute-start(bf16[48,4736]{1,0:T(8,128)(2,1)S(1)} %get-tuple-element.116.refs_1_), channel_id=1, source_target_pairs={{0,2},{1,3},{2,0},{3,1},{4,6},{5,7},{6,4},{7,5},{8,10},{9,11},{10,... | collective-permute-start | bytes 1363976 | tf_op jit(solution)/shard_map/ppermute | solution.py:98
  16.7 13.6 %collective-permute-start.10 = (bf16[48,2432]{1,0:T(8,128)(2,1)S(1)}, bf16[48,2432]{1,0:T(8,128)(2,1)S(1)}, u32[]{:S(2)}, u32[]{:S(2)}) collective-permute-start(bf16[48,2432]{1,0:T(8,128)(2,1)S(1)} %collective-permute-done.9.refs_4_), channel_id=1, source_target_pairs={{0,8},{8,0},{16,24},{24,16},{1,9},{9,1},{17,25},{25,17},{2,10},{10... | collective-permute-start | bytes 700424 | tf_op jit(solution)/shard_map/ppermute | solution.py:98
  31.1 6.9 %collective-permute-start.12 = (bf16[4,48,3456]{2,1,0:T(8,128)(2,1)S(1)}, bf16[4,48,3456]{2,1,0:T(8,128)(2,1)S(1)}, u32[]{:S(2)}, u32[]{:S(2)}) collective-permute-start(bf16[4,48,3456]{2,1,0:T(8,128)(2,1)S(1)} %get-tuple-element.123.refs_7_), channel_id=1, source_target_pairs={{0,1},{1,0},{2,3},{3,2},{4,5},{5,4},{6,7},{7,6},{8,9},{9,8},{10,11... | collective-permute-start | bytes 3981320 | tf_op jit(solution)/shard_map/ppermute | solution.py:98
  48.3 4.5 %collective-permute-start.13 = (bf16[4,48,3456]{2,1,0:T(8,128)(2,1)S(1)}, bf16[4,48,3456]{2,1,0:T(8,128)(2,1)S(1)}, u32[]{:S(2)}, u32[]{:S(2)}) collective-permute-start(bf16[4,48,3456]{2,1,0:T(8,128)(2,1)S(1)} %get-tuple-element.125), channel_id=1, source_target_pairs={{0,1},{1,0},{2,3},{3,2},{4,5},{5,4},{6,7},{7,6},{8,9},{9,8},{10,11... | collective-permute-start | bytes 3981320 | tf_op jit(solution)/shard_map/ppermute | solution.py:98
  54.5 17.2 %collective-permute-start.15 = (bf16[48,3456]{1,0:T(8,128)(2,1)S(1)}, bf16[48,3456]{1,0:T(8,128)(2,1)S(1)}, u32[]{:S(2)}, u32[]{:S(2)}) collective-permute-start(bf16[48,3456]{1,0:T(8,128)(2,1)S(1)} %get-tuple-element.131), channel_id=1, source_target_pairs={{0,4},{1,5},{2,6},{3,7},{4,0},{5,1},{6,2},{7,3},{8,12},{9,13},{10,... | collective-permute-start | bytes 995336 | tf_op jit(solution)/shard_map/ppermute | solution.py:98
  55.1 16.6 %collective-permute-start.16 = (bf16[48,3456]{1,0:T(8,128)(2,1)S(1)}, bf16[48,3456]{1,0:T(8,128)(2,1)S(1)}, u32[]{:S(2)}, u32[]{:S(2)}) collective-permute-start(bf16[48,3456]{1,0:T(8,128)(2,1)S(1)} %get-tuple-element.132), channel_id=1, source_target_pairs={{0,6},{1,7},{2,4},{3,5},{4,2},{5,3},{6,0},{7,1},{8,14},{9,15},{10,... | collective-permute-start | bytes 995336 | tf_op jit(solution)/shard_map/ppermute | solution.py:98
  56.5 16.4 %collective-permute-start.14 = (bf16[48,3456]{1,0:T(8,128)(2,1)S(1)}, bf16[48,3456]{1,0:T(8,128)(2,1)S(1)}, u32[]{:S(2)}, u32[]{:S(2)}) collective-permute-start(bf16[48,3456]{1,0:T(8,128)(2,1)S(1)} %get-tuple-element.130.refs_12_), channel_id=1, source_target_pairs={{0,2},{1,3},{2,0},{3,1},{4,6},{5,7},{6,4},{7,5},{8,10},{9,11},{10,... | collective-permute-start | bytes 995336 | tf_op jit(solution)/shard_map/ppermute | solution.py:98
  62.0 16.5 %all-to-all-start.1 = ((bf16[4,16,512]{2,1,0:T(8,128)(2,1)}), bf16[4,16,512]{2,1,0:T(8,128)(2,1)S(1)}, u32[]{:S(2)}, u32[]{:S(2)}) async-start(bf16[4,16,512]{2,1,0:T(8,128)(2,1)} %get-tuple-element.147), calls=%async_computation.1 | async-start | bytes 131072 | tf_op jit(solution)/shard_map/all_to_all | solution.py:964
  65.8 12.6 %collective-permute-start.23 = (bf16[4,48,1280]{2,1,0:T(8,128)(2,1)S(1)}, bf16[4,48,1280]{2,1,0:T(8,128)(2,1)S(1)}, u32[]{:S(2)}, u32[]{:S(2)}) collective-permute-start(bf16[4,48,1280]{2,1,0:T(8,128)(2,1)S(1)} %get-tuple-element.146), channel_id=1, source_target_pairs={{0,1},{1,0},{2,3},{3,2},{4,5},{5,4},{6,7},{7,6},{8,9},{9,8},{10,11... | collective-permute-start | bytes 1474568 | tf_op jit(solution)/shard_map/ppermute | solution.py:98
  74.9 9.2 %collective-permute-start.18 = (bf16[48,896]{1,0:T(8,128)(2,1)S(1)}, bf16[48,896]{1,0:T(8,128)(2,1)S(1)}, u32[]{:S(2)}, u32[]{:S(2)}) collective-permute-start(bf16[48,896]{1,0:T(8,128)(2,1)S(1)} %get-tuple-element.135), channel_id=1, source_target_pairs={{0,16},{8,24},{16,0},{24,8},{1,17},{9,25},{17,1},{25,9},{2,18},{10... | collective-permute-start | bytes 258056 | tf_op jit(solution)/shard_map/ppermute | solution.py:98
  77.5 7.1 %collective-permute-start.19 = (bf16[48,896]{1,0:T(8,128)(2,1)S(1)}, bf16[48,896]{1,0:T(8,128)(2,1)S(1)}, u32[]{:S(2)}, u32[]{:S(2)}) collective-permute-start(bf16[48,896]{1,0:T(8,128)(2,1)S(1)} %get-tuple-element.136), channel_id=1, source_target_pairs={{0,24},{8,16},{16,8},{24,0},{1,25},{9,17},{17,9},{25,1},{2,26},{10... | collective-permute-start | bytes 258056 | tf_op jit(solution)/shard_map/ppermute | solution.py:98
  77.8 6.9 %collective-permute-start.17 = (bf16[48,896]{1,0:T(8,128)(2,1)S(1)}, bf16[48,896]{1,0:T(8,128)(2,1)S(1)}, u32[]{:S(2)}, u32[]{:S(2)}) collective-permute-start(bf16[48,896]{1,0:T(8,128)(2,1)S(1)} %get-tuple-element.134.refs_4_), channel_id=1, source_target_pairs={{0,8},{8,0},{16,24},{24,16},{1,9},{9,1},{17,25},{25,17},{2,10},{10... | collective-permute-start | bytes 258056 | tf_op jit(solution)/shard_map/ppermute | solution.py:98
  80.3 8.4 %collective-permute-start.24 = (bf16[64,1792]{1,0:T(8,128)(2,1)S(1)}, bf16[64,1792]{1,0:T(8,128)(2,1)S(1)}, u32[]{:S(2)}, u32[]{:S(2)}) collective-permute-start(bf16[64,1792]{1,0:T(8,128)(2,1)S(1)} %get-tuple-element.149), channel_id=1, source_target_pairs={{0,2},{1,3},{2,0},{3,1},{4,6},{5,7},{6,4},{7,5},{8,10},{9,11},{10,... | collective-permute-start | bytes 688136 | tf_op jit(solution)/shard_map/ppermute | solution.py:98
  80.9 10.6 %collective-permute-start.25 = (bf16[64,1792]{1,0:T(8,128)(2,1)S(1)}, bf16[64,1792]{1,0:T(8,128)(2,1)S(1)}, u32[]{:S(2)}, u32[]{:S(2)}) collective-permute-start(bf16[64,1792]{1,0:T(8,128)(2,1)S(1)} %get-tuple-element.150), channel_id=1, source_target_pairs={{0,4},{1,5},{2,6},{3,7},{4,0},{5,1},{6,2},{7,3},{8,12},{9,13},{10,... | collective-permute-start | bytes 688136 | tf_op jit(solution)/shard_map/ppermute | solution.py:98
  84.1 7.4 %collective-permute-start.26 = (bf16[64,1792]{1,0:T(8,128)(2,1)S(1)}, bf16[64,1792]{1,0:T(8,128)(2,1)S(1)}, u32[]{:S(2)}, u32[]{:S(2)}) collective-permute-start(bf16[64,1792]{1,0:T(8,128)(2,1)S(1)} %get-tuple-element.151), channel_id=1, source_target_pairs={{0,6},{1,7},{2,4},{3,5},{4,2},{5,3},{6,0},{7,1},{8,14},{9,15},{10,... | collective-permute-start | bytes 688136 | tf_op jit(solution)/shard_map/ppermute | solution.py:98
  84.7 7.6 %collective-permute-start.22 = (bf16[48,896]{1,0:T(8,128)(2,1)S(1)}, bf16[48,896]{1,0:T(8,128)(2,1)S(1)}, u32[]{:S(2)}, u32[]{:S(2)}) collective-permute-start(bf16[48,896]{1,0:T(8,128)(2,1)S(1)} %shard_map.402.refs_1_), channel_id=1, source_target_pairs={{0,24},{8,16},{16,8},{24,0},{1,25},{9,17},{17,9},{25,1},{2,26},{10... | collective-permute-start | bytes 258056 | tf_op jit(solution)/shard_map/ppermute | solution.py:98
  87.5 6.4 %collective-permute-start.21 = (bf16[48,896]{1,0:T(8,128)(2,1)S(1)}, bf16[48,896]{1,0:T(8,128)(2,1)S(1)}, u32[]{:S(2)}, u32[]{:S(2)}) collective-permute-start(bf16[48,896]{1,0:T(8,128)(2,1)S(1)} %shard_map.402.refs_1_), channel_id=1, source_target_pairs={{0,16},{8,24},{16,0},{24,8},{1,17},{9,25},{17,1},{25,9},{2,18},{10... | collective-permute-start | bytes 258056 | tf_op jit(solution)/shard_map/ppermute | solution.py:98
  88.8 5.4 %collective-permute-start.20 = (bf16[48,896]{1,0:T(8,128)(2,1)S(1)}, bf16[48,896]{1,0:T(8,128)(2,1)S(1)}, u32[]{:S(2)}, u32[]{:S(2)}) collective-permute-start(bf16[48,896]{1,0:T(8,128)(2,1)S(1)} %shard_map.402.refs_1_), channel_id=1, source_target_pairs={{0,8},{8,0},{16,24},{24,16},{1,9},{9,1},{17,25},{25,17},{2,10},{10... | collective-permute-start | bytes 258056 | tf_op jit(solution)/shard_map/ppermute | solution.py:98
  92.2 3.3 %collective-permute-start.27 = (bf16[4,64,512]{2,1,0:T(8,128)(2,1)S(1)}, bf16[4,64,512]{2,1,0:T(8,128)(2,1)S(1)}, u32[]{:S(2)}, u32[]{:S(2)}) collective-permute-start(bf16[4,64,512]{2,1,0:T(8,128)(2,1)S(1)} %get-tuple-element.153.refs_1_), channel_id=1, source_target_pairs={{0,1},{1,0},{2,3},{3,2},{4,5},{5,4},{6,7},{7,6},{8,9},{9,8},{10,11... | collective-permute-start | bytes 786440 | tf_op jit(solution)/shard_map/ppermute | solution.py:98
  98.5 13.7 %collective-permute-start.30 = (bf16[48,1280]{1,0:T(8,128)(2,1)S(1)}, bf16[48,1280]{1,0:T(8,128)(2,1)S(1)}, u32[]{:S(2)}, u32[]{:S(2)}) collective-permute-start(bf16[48,1280]{1,0:T(8,128)(2,1)S(1)} %get-tuple-element.161.refs_1_), channel_id=1, source_target_pairs={{0,24},{8,16},{16,8},{24,0},{1,25},{9,17},{17,9},{25,1},{2,26},{10... | collective-permute-start | bytes 368648 | tf_op jit(solution)/shard_map/ppermute | solution.py:98
  101.6 10.6 %collective-permute-start.29 = (bf16[48,1280]{1,0:T(8,128)(2,1)S(1)}, bf16[48,1280]{1,0:T(8,128)(2,1)S(1)}, u32[]{:S(2)}, u32[]{:S(2)}) collective-permute-start(bf16[48,1280]{1,0:T(8,128)(2,1)S(1)} %get-tuple-element.161.refs_1_), channel_id=1, source_target_pairs={{0,16},{8,24},{16,0},{24,8},{1,17},{9,25},{17,1},{25,9},{2,18},{10... | collective-permute-start | bytes 368648 | tf_op jit(solution)/shard_map/ppermute | solution.py:98
  101.6 10.6 %collective-permute-start.28 = (bf16[48,1280]{1,0:T(8,128)(2,1)S(1)}, bf16[48,1280]{1,0:T(8,128)(2,1)S(1)}, u32[]{:S(2)}, u32[]{:S(2)}) collective-permute-start(bf16[48,1280]{1,0:T(8,128)(2,1)S(1)} %get-tuple-element.161.refs_1_), channel_id=1, source_target_pairs={{0,8},{8,0},{16,24},{24,16},{1,9},{9,1},{17,25},{25,17},{2,10},{10... | collective-permute-start | bytes 368648 | tf_op jit(solution)/shard_map/ppermute | solution.py:98
  102.9 8.8 %all-to-all-start.2 = ((bf16[8,64,128]{2,1,0:T(8,128)(2,1)}), bf16[8,64,128]{2,1,0:T(8,128)(2,1)S(1)}, u32[]{:S(2)}, u32[]{:S(2)}) async-start(bf16[8,64,128]{2,1,0:T(8,128)(2,1)} %get-tuple-element.162), calls=%async_computation.2 | async-start | bytes 262144 | tf_op jit(solution)/shard_map/all_to_all | solution.py:974
  (46 other events, 286.4 us)
